TPU v7x, 32 devices: a whole 2x2x4 slice. The times are simulated.
32 devices in a mesh: dp: 4 (over z), ctx: 8 (over y, x, core).
Axes of the slice: x: 2, y: 2, z: 4, core: 2. Of those that a mesh axis runs over, the one named last changes fastest.
Arguments:
- hidden: bfloat16 [4, 2048, 2048], P('dp', 'ctx'), may hold values from -6 to 6
- x_weight: bfloat16 [2048, 2048], replicated, may hold values from -0.125 to 0.125
- state_weight: bfloat16 [2048, 160], replicated, may hold values from -0.125 to 0.125
- log_rates: float32 [32], replicated, as said below
- step_bias: float32 [32], replicated, may hold values from -1 to 1
- out_gain: float32 [2048], replicated, may hold values from 0.5 to 1.5
- cotangent: bfloat16 [4, 2048, 2048], P('dp', 'ctx'), may hold values from -6 to 6
Outputs:
- mixed: bfloat16 [4, 2048, 2048], P('dp', 'ctx')
- grad_x: float32 [2048, 2048], P('ctx')
- grad_small: float32 [2048, 160], P('ctx')
Inputs may be any that keep to these rules, and one draw needn't show every extreme that they name: Each head's rate exp(log_rates) lies between 0.05 / 2048 and 1 / 30.
All inputs are finite; a program needn't handle non-finite values.
Results may differ from a plain program's by a relative error of at most 0.0049.
Values may be sent and summed in bfloat16 or wider, within the bound.
No kernel may reach another device: no remote copies, remote signals or barrier semaphores. Data moves between devices by JAX's collectives and lax.ppermute only.
A program may use at most 192 MiB of HBM per device.

v0:
```python
import jax
import jax.numpy as jnp
from jax import lax
from jax.sharding import PartitionSpec as P

HEAD = 64
STATE = 64


precise = lax.Precision.HIGHEST


def swapped(array, axis, apart):
    return lax.ppermute(array, axis, [(i, i ^ 1 << apart) for i in range(lax.axis_size(axis))])


def carried_in(array, axis, combine, identity, reverse):
    peers, place = (lax.axis_size(axis), lax.axis_index(axis))
    everything = jax.tree.map(lambda part: lax.all_gather(part, axis), array)
    start = jax.tree.map(
        lambda part, zero: jnp.broadcast_to(jnp.asarray(zero, part.dtype), part.shape),
        array,
        identity,
    )

    def step(k, before):
        at = peers - 1 - k if reverse else k
        reached = at > place if reverse else at < place
        new = combine(before, jax.tree.map(lambda part: part[at], everything))
        return jax.tree.map(lambda a, b: jnp.where(reached, a, b), new, before)

    return lax.fori_loop(0, peers, step, start)


def split_small(projected, log_rates, step_bias):
    inputs_b = projected[:, :STATE]
    inputs_c = projected[:, STATE : 2 * STATE]
    step_size = jax.nn.softplus(projected[:, 2 * STATE :] + step_bias[None, :])
    cumlog = jnp.cumsum(-jnp.exp(log_rates)[None, :] * step_size, axis=0)
    return (inputs_b, inputs_c, step_size, cumlog)


def block_state(values_in, projected, log_rates, step_bias):
    inputs_b, inputs_c, step_size, cumlog = split_small(projected, log_rates, step_bias)
    block_rows, channels = values_in.shape
    head_count = channels // HEAD
    per_head = values_in.reshape(block_rows, head_count, HEAD)
    weighting = jnp.exp(cumlog[-1][None, :] - cumlog) * step_size
    local_end = jnp.einsum("sh,shp,sn->hpn", weighting, per_head, inputs_b, precision=precise)
    return (jnp.exp(cumlog[-1]), local_end)


def forward_y(values_in, projected, state_in, log_rates, step_bias, out_gain):
    inputs_b, inputs_c, step_size, cumlog = split_small(projected, log_rates, step_bias)
    block_rows, channels = values_in.shape
    head_count = channels // HEAD
    per_head = values_in.reshape(block_rows, head_count, HEAD)
    log_heads = cumlog.T
    log_gap = log_heads[:, :, None] - log_heads[:, None, :]
    position = jnp.arange(block_rows)
    causal = position[:, None] >= position[None, :]
    decay_mat = jnp.exp(jnp.where(causal[None, :, :], log_gap, -jnp.inf)) * step_size.T[:, None, :]
    scores = jnp.dot(inputs_c, inputs_b.T, precision=precise)
    mixing = decay_mat * scores[None, :, :]
    inner = jnp.einsum("hts,shp->thp", mixing, per_head, precision=precise)
    readout = (
        jnp.einsum("tn,hpn->thp", inputs_c, state_in, precision=precise)
        * jnp.exp(cumlog)[:, :, None]
    )
    unnormed = (inner + readout).reshape(block_rows, channels)
    rescale = lax.rsqrt(jnp.mean(unnormed * unnormed, axis=1, keepdims=True) + 1e-05)
    return unnormed * rescale * out_gain[None, :]


def chain(earlier, later):
    return (earlier[0] * later[0], later[0][:, None, None] * earlier[1] + later[1])


def chain_pair(earlier, later):
    return chain(earlier[:2], later[:2]) + chain(earlier[2:], later[2:])


def contract(left_rows, right_rows):
    return lax.dot_general(
        left_rows, right_rows, (((0,), (0,)), ((), ())), preferred_element_type=jnp.float32
    )


def shards(hidden, x_weight, state_weight, log_rates, step_bias, out_gain, cotangent):
    own_rows = hidden[0]
    own_cot = cotangent[0]
    channels = x_weight.shape[0]
    head_count = channels // HEAD
    unit = (jnp.ones((head_count,), jnp.float32), jnp.zeros((head_count, HEAD, STATE), jnp.float32))
    mirror_steps = lax.axis_size("ctx").bit_length() - 1

    def project(rows_in):
        values = jnp.dot(rows_in, x_weight, preferred_element_type=jnp.float32).astype(jnp.bfloat16)
        projected = jnp.dot(rows_in, state_weight, preferred_element_type=jnp.float32)
        return (values.astype(jnp.float32), projected)

    def local_state(values_in, projected):
        return block_state(values_in, projected, log_rates, step_bias)

    def local_output(values_in, projected, state_in):
        return forward_y(values_in, projected, state_in, log_rates, step_bias, out_gain)

    own_rc_rows = own_rows[::-1, ::-1]
    parcel = jnp.stack([own_rc_rows, own_cot])
    for bit_index in range(mirror_steps):
        parcel = swapped(parcel, "ctx", bit_index)
    rows_rc = parcel[0]
    cot_rc = parcel[1][::-1, ::-1].astype(jnp.float32)
    cot_fwd = own_cot.astype(jnp.float32)
    values_fwd, proj_fwd = project(own_rows)
    values_rc, proj_rc = project(rows_rc)
    (total_fwd, end_fwd), state_back_fwd = jax.vjp(local_state, values_fwd, proj_fwd)
    (total_rc, end_rc), state_back_rc = jax.vjp(local_state, values_rc, proj_rc)
    carried = carried_in(
        (total_fwd, end_fwd, total_rc, end_rc), "ctx", chain_pair, unit + unit, False
    )
    start_fwd = carried[1]
    start_rc = carried[3]
    y_fwd, out_back_fwd = jax.vjp(local_output, values_fwd, proj_fwd, start_fwd)
    y_rc, out_back_rc = jax.vjp(local_output, values_rc, proj_rc, start_rc)
    returned = y_rc.astype(jnp.bfloat16)
    for bit_index in range(mirror_steps):
        returned = swapped(returned, "ctx", bit_index)
    mixed = (y_fwd + returned[::-1, ::-1].astype(jnp.float32)).astype(jnp.bfloat16)
    dval_fwd, dproj_fwd, local_fwd = out_back_fwd(cot_fwd)
    dval_rc, dproj_rc, local_rc = out_back_rc(cot_rc)
    adjoints = carried_in(
        (total_fwd, local_fwd, total_rc, local_rc), "ctx", chain_pair, unit + unit, True
    )
    after_fwd = adjoints[1]
    after_rc = adjoints[3]

    def finish(state_back, dval_first, dproj_first, state_in, after_end):
        dtotal = jnp.sum(after_end * state_in, axis=(1, 2))
        dval_second, dproj_second = state_back((dtotal, after_end))
        return (
            (dval_first + dval_second).astype(jnp.bfloat16),
            (dproj_first + dproj_second).astype(jnp.bfloat16),
        )

    grad_vf, grad_pf = finish(state_back_fwd, dval_fwd, dproj_fwd, start_fwd, after_fwd)
    grad_vr, grad_pr = finish(state_back_rc, dval_rc, dproj_rc, start_rc, after_rc)
    term_x = contract(own_rows, grad_vf) + contract(rows_rc, grad_vr)
    term_small = contract(own_rows, grad_pf) + contract(rows_rc, grad_pr)
    shard_x, shard_small = (
        lax.psum_scatter(term_x, "ctx", scatter_dimension=0, tiled=True),
        lax.psum_scatter(term_small, "ctx", scatter_dimension=0, tiled=True),
    )
    grad_x, grad_small = lax.psum((shard_x, shard_small), "dp")
    return (mixed[None], grad_x, grad_small)


def solution(mesh):
    return jax.shard_map(
        shards,
        mesh=mesh,
        in_specs=(P("dp", "ctx", None), P(), P(), P(), P(), P(), P("dp", "ctx", None)),
        out_specs=(P("dp", "ctx", None), P("ctx", None), P("ctx", None)),
        check_vma=False,
    )
```

profile of v0, /device:TPU:0, one launch (start us, length us, event | category | flops | bytes accessed | tf_op | source)
XLA Modules:
  0.0 742.7 jit_solution(6565808909158796053)
XLA Ops:
  7.2 16.5 %rev.9 = bf16[256,2048]{1,0:T(8,128)(2,1)} reverse(bf16[256,2048]{1,0:T(8,128)(2,1)} %bitcast.344), dimensions={0,1} | reverse | bytes 2097152 | tf_op jit(solution)/shard_map/rev | solution.py:108
  25.7 3.8 collective-permute-done
  29.5 2.9 collective-permute-start.1
  32.4 46.0 %collective-permute-done.1 = bf16[2,256,2048]{2,1,0:T(8,128)(2,1)} collective-permute-done((bf16[2,256,2048]{2,1,0:T(8,128)(2,1)S(1)}, bf16[2,256,2048]{2,1,0:T(8,128)(2,1)}, u32[]{:S(2)}, u32[]{:S(2)}) %collective-permute-start.1) | collective-permute-done | bytes 2097184 | tf_op jit(solution)/shard_map/ppermute | solution.py:14
  80.2 6.7 convolution_convert_fusion.1
  88.9 37.0 %collective-permute-done.2 = bf16[2,256,2048]{2,1,0:T(8,128)(2,1)} collective-permute-done((bf16[2,256,2048]{2,1,0:T(8,128)(2,1)}, bf16[2,256,2048]{2,1,0:T(8,128)(2,1)}, u32[]{:S(2)}, u32[]{:S(2)}) %collective-permute-start.2) | collective-permute-done | bytes 2097184 | tf_op jit(solution)/shard_map/ppermute | solution.py:14
  131.3 2.8 fusion.49
  134.9 6.1 convolution_convert_fusion
  144.4 2.8 fusion.51
  147.9 2.3 slice_bitcast_fusion
  150.2 16.4 %rev.11 = bf16[256,2048]{1,0:T(8,128)(2,1)} reverse(bf16[256,2048]{1,0:T(8,128)(2,1)} %slice_bitcast_fusion), dimensions={0,1} | reverse | bytes 2097152 | tf_op jit(solution)/shard_map/rev | solution.py:113
  166.6 9.3 %all-gather.4 = f32[8,1,32]{2,1,0:T(1,128)} all-gather(f32[1,1,32]{2,1,0:T(1,128)S(1)} %bitcast.366), channel_id=1, replica_groups=mesh['dp'=4,'ctx'=8] {'ctx'}, dimensions={0}, use_global_device_ids=true | all-gather | bytes 1152 | tf_op jit(solution)/shard_map/all_gather | solution.py:19
  176.0 9.9 %all-gather.5 = f32[8,1,32]{2,1,0:T(1,128)} all-gather(f32[1,1,32]{2,1,0:T(1,128)} %bitcast.367), channel_id=1, replica_groups=mesh['dp'=4,'ctx'=8] {'ctx'}, dimensions={0}, use_global_device_ids=true | all-gather | bytes 1152 | tf_op jit(solution)/shard_map/all_gather | solution.py:19
  186.9 2.9 all-gather.11.cloned.1.call-done
  189.9 56.9 %all-gather.13.cloned.1.call-done = f32[256,64,64]{2,1,0:T(8,128)} async-done(((f32[32,64,64]{2,1,0:T(8,128)}), f32[256,64,64]{2,1,0:T(8,128)}) %all-gather.13.cloned.1.call-update) | async-done | bytes 4194320 | tf_op jit(solution)/shard_map/all_gather | solution.py:19
  246.8 26.4 %while.34 = (s32[]{:T(128)}, f32[32,64,64]{2,1,0:T(8,128)S(1)}, f32[32,64,64]{2,1,0:T(8,128)S(1)}, s32[]{:T(128)}, f32[8,32]{1,0:T(8,128)}, /*index=5*/f32[8,32,...) while((s32[]{:T(128)}, f32[32,64,64]{2,1,0:T(8,128)S(1)}, ...), condition=%wide.region_5.7_spmd.clone, body=%wide.region_4.6_spmd.clone.sunk | while | flops 1048580 | bytes 3146637 | solution.py:32
  248.1 1.9 fusion.207
  251.5 1.9 fusion.207
  254.8 1.9 fusion.207
  258.1 1.9 fusion.207
  275.1 8.3 %multiply_reduce_fusion.8 = (f32[256]{0:T(256)}, f32[256,32,64]{0,2,1:T(8,128)}) fusion(f32[256,32,64]{0,2,1:T(8,128)S(1)} %fusion.96, f32[256,32]{0,1:T(8,128)S(1)} %copy-done.35, bf16[256,32,64]{0,2,1:T(8,128)(2,1)S(1)} %bitcast.346, f32[256,256]{1,0:T(8,128)S(1)} %copy-done.39, f32[32,256]{1,0:T(8,128)S(1)} %copy-done.69, f32[32,256]{1,0:T(8,128)S(1)} %copy-done.59, ...), kind=kOutput, calls=%fused_computation.94 | convolution fusion | flops 1621098240 | bytes 5669888 | tf_op jit(solution)/shard_map/jvp(hts,shp->thp)/dot_general | solution.py:65
  283.4 2.9 copy.73
  286.4 2.4 multiply_reduce_fusion.6
  289.2 2.7 add_add_fusion
  291.9 2.9 copy.77
  294.8 4.4 fusion.61
  300.1 2.6 copy.74
  305.0 6.3 multiply_reduce_fusion.7
  313.9 2.8 fusion.65
  317.4 5.5 fusion.56
  323.0 14.0 %fusion.23 = (f32[32,256]{1,0:T(8,128)}, f32[32,256]{1,0:T(8,128)}, f32[32,256]{1,0:T(8,128)}, f32[256,256]{1,0:T(8,128)}, f32[256,256]{1,0:T(8,128)}, /*index=5...) fusion(f32[256,256]{1,0:T(8,128)S(1)} %copy-done.40, f32[32,256]{1,0:T(8,128)S(1)} %copy-done.70, ...), kind=kOutput, calls=%fused_computation.36 | convolution fusion | flops 1664958464 | bytes 12976128 | tf_op jit(solution)/shard_map/transpose(jvp(hts,shp->thp))/dot_general | solution.py:65
  337.7 3.8 reduce-window.46
  341.5 2.7 multiply_reduce_fusion.4
  344.9 3.8 reduce-window.54
  356.5 3.5 fusion.80
  360.0 2.0 fusion.77
  365.8 44.1 %all-gather.15.cloned.1.call-done = f32[256,64,64]{2,1,0:T(8,128)} async-done(((f32[32,64,64]{2,1,0:T(8,128)}), f32[256,64,64]{2,1,0:T(8,128)}) %all-gather.15.cloned.1.call-update) | async-done | bytes 4194320 | tf_op jit(solution)/shard_map/all_gather | solution.py:19
  409.9 35.7 %while.35 = (s32[]{:T(128)}, f32[32,64,64]{2,1,0:T(8,128)}, f32[32,64,64]{2,1,0:T(8,128)S(1)}, s32[]{:T(128)}, f32[8,32]{1,0:T(8,128)}, /*index=5*/f32[8,32,64,6...) while((s32[]{:T(128)}, f32[32,64,64]{2,1,0:T(8,128)}, ...), condition=%wide.region_11.13_spmd.clone, body=%wide.region_10.12_spmd.clone.sunk | while | flops 1048584 | bytes 3146699 | solution.py:32
  411.3 2.8 fusion.210
  415.4 3.1 fusion.210
  419.9 3.1 fusion.210
  424.4 3.1 fusion.210
  428.9 3.1 fusion.210
  433.4 3.1 fusion.210
  437.9 3.1 fusion.210
  442.4 3.1 fusion.210
  446.9 2.6 fusion.83
  449.8 2.0 fusion.84
  451.8 3.2 fusion.52
  455.0 3.2 fusion.53
  458.8 9.7 %fusion.55 = bf16[256,32,64]{0,2,1:T(8,128)(2,1)} fusion(f32[256,32,64]{0,2,1:T(8,128)} %get-tuple-element.513, f32[256,256]{1,0:T(8,128)S(1)} %copy-done.44, f32[32,256]{1,0:T(8,128)S(1)} %copy-done.73, f32[32,256]{1,0:T(8,128)S(1)} %copy-done.64, pred[256,256]{1,0:T(8,128)(4,1)S(1)} %copy-done.57, f32[256,32,64]{0,2,1:T(8,128)} %copy-done.5, ...), kind=kOutput, calls=%fused_computation.81 | convolution fusion | flops 1620574208 | bytes 5668864 | tf_op jit(solution)/shard_map/transpose(jvp(hts,shp->thp))/dot_general | solution.py:65
  468.9 2.7 reduce-window.56
  471.9 2.5 reduce-window.50
  475.2 2.9 convolution_add_fusion
  478.2 9.6 %fusion.54 = bf16[256,32,64]{0,2,1:T(8,128)(2,1)} fusion(f32[256,32,64]{0,2,1:T(8,128)} %get-tuple-element.511, f32[32,64,256]{2,1,0:T(8,128)S(1)} %bitcast.339, f32[256,256]{1,0:T(8,128)S(1)} %copy-done.41, f32[32,256]{1,0:T(8,128)} %get-tuple-element.487, f32[32,256]{1,0:T(8,128)S(1)} %copy-done.61, pred[256,256]{1,0:T(8,128)(4,1)S(1)} %copy-done.58, ...), kind=kOutput, calls=%fused_computation.79 | convolution fusion | flops 1620574208 | bytes 5668864 | tf_op jit(solution)/shard_map/transpose(jvp(hts,shp->thp))/dot_general | solution.py:65
  487.8 2.3 fusion.156
  490.2 9.4 %bitcast_add_fusion.4 = f32[2048,2048]{0,1:T(8,128)} fusion(f32[2048,2048]{1,0:T(8,128)S(1)} %fusion.156, bf16[256,2048]{0,1:T(8,128)(2,1)S(1)} %bitcast.357, bf16[2,256,2048]{2,1,0:T(8,128)(2,1)} %collective-permute-done.2), kind=kOutput, calls=%fused_computation.16 | convolution fusion | flops 2151677952 | bytes 35651584 | tf_op jit(solution)/shard_map/dot_general | solution.py:84
  501.0 2.6 collective-permute-done.3
  505.0 12.3 %reduce-scatter.5.cloned.1.call-done = f32[256,160]{0,1:T(8,128)} async-done(((f32[2048,160]{0,1:T(8,128)}), f32[256,160]{0,1:T(8,128)}) %reduce-scatter.5.cloned.1.call-update) | async-done | bytes 163856 | tf_op jit(solution)/shard_map/reduce_scatter | solution.py:152
  517.3 119.4 %reduce-scatter.3.cloned.1.call-done = f32[256,2048]{0,1:T(8,128)} async-done(((f32[2048,2048]{0,1:T(8,128)}), f32[256,2048]{0,1:T(8,128)}) %reduce-scatter.3.cloned.1.call-update) | async-done | bytes 2097168 | tf_op jit(solution)/shard_map/reduce_scatter | solution.py:151
  640.0 21.8 %collective-permute-done.5 = bf16[256,2048]{1,0:T(8,128)(2,1)} collective-permute-done((bf16[256,2048]{1,0:T(8,128)(2,1)S(1)}, bf16[256,2048]{1,0:T(8,128)(2,1)}, u32[]{:S(2)}, u32[]{:S(2)}) %collective-permute-start.5) | collective-permute-done | bytes 1048608 | tf_op jit(solution)/shard_map/ppermute | solution.py:14
  661.8 13.9 %rev.10 = bf16[256,2048]{1,0:T(8,128)(2,1)S(1)} reverse(bf16[256,2048]{1,0:T(8,128)(2,1)} %collective-permute-done.5), dimensions={0,1} | reverse | bytes 2097152 | tf_op jit(solution)/shard_map/rev | solution.py:129
  677.0 54.9 %all-reduce.17.cloned.1.call-done = (f32[256,2048]{0,1:T(8,128)}, f32[256,160]{0,1:T(8,128)}) async-done(((f32[256,2048]{0,1:T(8,128)}, f32[256,160]{0,1:T(8,128)}), (f32[256,2048]{0,1:T(8,128)}, f32[256,160]{0,1:T(8,128)})) %all-reduce.17.cloned.1.call-update) | async-done | bytes 2261008 | tf_op jit(solution)/shard_map/psum | solution.py:154
  732.0 3.0 copy.95
  (306 shorter events, 80.0 us)
Async XLA Ops:
  7.2 81.2 %copy-start = (bf16[2048,160]{0,1:T(8,128)(2,1)S(1)}, bf16[2048,160]{0,1:T(8,128)(2,1)}, u32[]{:S(2)}) copy-start(bf16[2048,160]{0,1:T(8,128)(2,1)} %param.14) | copy-start | bytes 1966084
  7.2 16.5 %copy-start.22 = (bf16[1,256,2048]{2,1,0:T(8,128)(2,1)S(1)}, bf16[1,256,2048]{2,1,0:T(8,128)(2,1)}, u32[]{:S(2)}) copy-start(bf16[1,256,2048]{2,1,0:T(8,128)(2,1)} %param.18) | copy-start | bytes 3145732
  7.2 182.7 %all-gather.11.cloned.1.call-start = ((), (), s32[]{:S(2)}) async-start(), calls=%async_computation.4 | async-start | bytes 9437184 | tf_op jit(solution)/shard_map/all_gather | solution.py:19
  23.7 56.5 %copy-start.10 = (bf16[1,256,2048]{2,1,0:T(8,128)(2,1)S(1)}, bf16[1,256,2048]{2,1,0:T(8,128)(2,1)}, u32[]{:S(2)}) copy-start(bf16[1,256,2048]{2,1,0:T(8,128)(2,1)} %param.12) | copy-start | bytes 3145732
  25.2 4.3 collective-permute-start
  29.5 48.9 %collective-permute-start.1 = (bf16[2,256,2048]{2,1,0:T(8,128)(2,1)S(1)}, bf16[2,256,2048]{2,1,0:T(8,128)(2,1)}, u32[]{:S(2)}, u32[]{:S(2)}) collective-permute-start(bf16[2,256,2048]{2,1,0:T(8,128)(2,1)S(1)} %collective-permute-done), channel_id=1, source_target_pairs={{0,2},{1,3},{2,0},{3,1},{4,6},{5,7},{6,4},{7,5},{8,10},{9,11},{10,... | collective-permute-start | bytes 6291464 | tf_op jit(solution)/shard_map/ppermute | solution.py:14
  78.4 47.5 %collective-permute-start.2 = (bf16[2,256,2048]{2,1,0:T(8,128)(2,1)}, bf16[2,256,2048]{2,1,0:T(8,128)(2,1)}, u32[]{:S(2)}, u32[]{:S(2)}) collective-permute-start(bf16[2,256,2048]{2,1,0:T(8,128)(2,1)} %collective-permute-done.1), channel_id=1, source_target_pairs={{0,4},{1,5},{2,6},{3,7},{4,0},{5,1},{6,2},{7,3},{8,12},{9,13},{10,... | collective-permute-start | bytes 6291464 | tf_op jit(solution)/shard_map/ppermute | solution.py:14
  88.4 216.6 %copy-start.7 = (bf16[256,2048]{0,1:T(8,128)(2,1)}, bf16[256,2048]{0,1:T(8,128)(2,1)S(1)}, u32[]{:S(2)}) copy-start(bf16[256,2048]{0,1:T(8,128)(2,1)S(1)} %copy.66) | copy-start | bytes 3145732
  88.4 39.2 %copy-start.74 = (f32[32]{0:T(128)S(1)}, f32[32]{0:T(128)}, u32[]{:S(2)}) copy-start(f32[32]{0:T(128)} %param.16) | copy-start | bytes 388
  88.4 39.9 %copy-start.86 = (f32[32]{0:T(128)}, f32[32]{0:T(128)S(1)}, u32[]{:S(2)}) copy-start(f32[32]{0:T(128)S(1)} %exponential_negate_fusion) | copy-start | bytes 388
  130.6 10.4 %copy-start.78 = (f32[32]{0:T(128)}, f32[32]{0:T(128)S(1)}, u32[]{:S(2)}) copy-start(f32[32]{0:T(128)S(1)} %get-tuple-element.433) | copy-start | bytes 388
  131.3 3.6 copy-start.31
  134.1 112.7 %all-gather.13.cloned.1.call-start = ((), (), s32[]{:S(2)}) async-start(), calls=%async_computation.5 | async-start | bytes 9437184 | tf_op jit(solution)/shard_map/all_gather | solution.py:19
  141.5 5.7 copy-start.12
  143.1 103.7 %copy-start.80 = (f32[32]{0:T(128)}, f32[32]{0:T(128)S(1)}, u32[]{:S(2)}) copy-start(f32[32]{0:T(128)S(1)} %get-tuple-element.431) | copy-start | bytes 388
  147.2 218.6 %all-gather.17.cloned.1.call-start = ((), (), s32[]{:S(2)}) async-start(), calls=%async_computation.7 | async-start | bytes 9437184 | tf_op jit(solution)/shard_map/all_gather | solution.py:19
  147.9 18.7 %copy-start.85 = (f32[32]{0:T(128)S(1)}, f32[32]{0:T(128)}, u32[]{:S(2)}) copy-start(f32[32]{0:T(128)} %get-tuple-element.434) | copy-start | bytes 388
  275.1 8.4 %copy-start.21 = (f32[256,32,64]{0,2,1:T(8,128)}, f32[256,32,64]{0,2,1:T(8,128)S(1)}, u32[]{:S(2)}) copy-start(f32[256,32,64]{0,2,1:T(8,128)S(1)} %fusion.96) | copy-start | bytes 6291460
  299.2 110.7 %all-gather.15.cloned.1.call-start = ((), (), s32[]{:S(2)}) async-start(), calls=%async_computation.6 | async-start | bytes 9437184 | tf_op jit(solution)/shard_map/all_gather | solution.py:19
  303.1 8.1 %copy-start.42 = (f32[256,256]{1,0:T(8,128)}, f32[256,256]{1,0:T(8,128)S(1)}, u32[]{:S(2)}) copy-start(f32[256,256]{1,0:T(8,128)S(1)} %fusion.120) | copy-start | bytes 786436
  316.8 200.5 %reduce-scatter.5.cloned.1.call-start = ((), (), s32[]{:S(2)}) async-start(), calls=%async_computation.3 | async-start | bytes 1474560 | tf_op jit(solution)/shard_map/reduce_scatter | solution.py:152
  317.3 5.6 copy-start.3
  317.3 5.6 copy-start.14
  317.3 5.6 copy-start.40
  317.3 5.6 copy-start.43
  317.3 5.6 copy-start.56
  317.4 5.6 copy-start.60
  317.4 5.6 copy-start.63
  317.4 5.6 copy-start.70
  317.4 5.6 copy-start.72
  323.0 14.1 %copy-start.48 = (f32[256,32]{0,1:T(8,128)S(1)}, f32[256,32]{0,1:T(8,128)}, u32[]{:S(2)}) copy-start(f32[256,32]{0,1:T(8,128)} %get-tuple-element.471) | copy-start | bytes 98308
  355.1 4.9 copy-start.6
  355.1 4.9 copy-start.34
  445.7 3.8 copy-start.2
  455.0 3.3 copy-start.84
  455.0 3.3 copy-start.52
  455.0 3.5 copy-start.50
  455.0 3.6 copy-start.44
  455.0 3.6 copy-start.57
  455.0 3.6 copy-start.64
  455.0 3.6 copy-start.73
  458.6 9.9 %copy-start.75 = (f32[32]{0:T(128)S(1)}, f32[32]{0:T(128)}, u32[]{:S(2)}) copy-start(f32[32]{0:T(128)} %param.16) | copy-start | bytes 388
  458.6 9.8 %copy-start.79 = (f32[32]{0:T(128)S(1)}, f32[32]{0:T(128)}, u32[]{:S(2)}) copy-start(f32[32]{0:T(128)} %copy-done.78) | copy-start | bytes 388
  458.6 9.8 %copy-start.81 = (f32[32]{0:T(128)S(1)}, f32[32]{0:T(128)}, u32[]{:S(2)}) copy-start(f32[32]{0:T(128)} %copy-done.80) | copy-start | bytes 388
  458.7 15.9 %copy-start.36 = (f32[32,2,128]{2,0,1:T(8,128)S(1)}, f32[32,2,128]{2,0,1:T(8,128)}, u32[]{:S(2)}) copy-start(f32[32,2,128]{2,0,1:T(8,128)} %reduce-window.46) | copy-start | bytes 98308
  458.7 15.9 %copy-start.37 = (f32[32,2,128]{2,0,1:T(8,128)S(1)}, f32[32,2,128]{2,0,1:T(8,128)}, u32[]{:S(2)}) copy-start(f32[32,2,128]{2,0,1:T(8,128)} %reduce-window.54) | copy-start | bytes 98308
  458.7 15.9 %copy-start.65 = (f32[32,256]{1,0:T(8,128)S(1)}, f32[32,256]{1,0:T(8,128)}, u32[]{:S(2)}) copy-start(f32[32,256]{1,0:T(8,128)} %get-tuple-element.421) | copy-start | bytes 98308
  458.7 15.9 %copy-start.66 = (f32[32,256]{1,0:T(8,128)S(1)}, f32[32,256]{1,0:T(8,128)}, u32[]{:S(2)}) copy-start(f32[32,256]{1,0:T(8,128)} %get-tuple-element.428) | copy-start | bytes 98308
  458.7 15.9 %copy-start.82 = (f32[32,2]{0,1:T(2,128)S(1)}, f32[32,2]{0,1:T(2,128)}, u32[]{:S(2)}) copy-start(f32[32,2]{0,1:T(2,128)} %slice.91) | copy-start | bytes 772
  458.7 15.9 %copy-start.83 = (f32[32,2]{0,1:T(2,128)S(1)}, f32[32,2]{0,1:T(2,128)}, u32[]{:S(2)}) copy-start(f32[32,2]{0,1:T(2,128)} %slice.87) | copy-start | bytes 772
  458.7 15.9 %copy-start.87 = (f32[32]{0:T(128)S(1)}, f32[32]{0:T(128)}, u32[]{:S(2)}) copy-start(f32[32]{0:T(128)} %copy-done.86) | copy-start | bytes 388
  458.7 16.0 %copy-start.11 = (bf16[1,256,2048]{2,1,0:T(8,128)(2,1)S(1)}, bf16[1,256,2048]{2,1,0:T(8,128)(2,1)}, u32[]{:S(2)}) copy-start(bf16[1,256,2048]{2,1,0:T(8,128)(2,1)} %param.12) | copy-start | bytes 3145732
  458.7 16.0 %copy-start.38 = (f32[256,64]{0,1:T(8,128)S(1)}, f32[256,64]{0,1:T(8,128)}, u32[]{:S(2)}) copy-start(f32[256,64]{0,1:T(8,128)} %convolution_add_fusion.2) | copy-start | bytes 196612
  458.7 16.0 %copy-start.45 = (f32[256,64]{0,1:T(8,128)S(1)}, f32[256,64]{0,1:T(8,128)}, u32[]{:S(2)}) copy-start(f32[256,64]{0,1:T(8,128)} %fusion.123) | copy-start | bytes 196612
  478.1 158.6 %reduce-scatter.3.cloned.1.call-start = ((), (), s32[]{:S(2)}) async-start(), calls=%async_computation.2 | async-start | bytes 18874368 | tf_op jit(solution)/shard_map/reduce_scatter | solution.py:151
  478.2 9.6 %copy-start.24 = (bf16[256,32,64]{0,2,1:T(8,128)(2,1)S(1)}, bf16[256,32,64]{0,2,1:T(8,128)(2,1)}, u32[]{:S(2)}) copy-start(bf16[256,32,64]{0,2,1:T(8,128)(2,1)} %fusion.55) | copy-start | bytes 3145732
  499.6 138.6 %copy-start.18 = (f32[256,32,64]{0,2,1:T(8,128)S(1)}, f32[256,32,64]{0,2,1:T(8,128)}, u32[]{:S(2)}) copy-start(f32[256,32,64]{0,2,1:T(8,128)} %copy-done.17) | copy-start | bytes 6291460
  499.6 232.4 %all-reduce.17.cloned.1.call-start = ((), (), s32[]{:S(2)}) async-start(), calls=%async_computation.8 | async-start | bytes 4521984 | tf_op jit(solution)/shard_map/psum | solution.py:154
  500.8 2.8 collective-permute-start.3
  503.6 133.2 %collective-permute-start.4 = (bf16[256,2048]{1,0:T(8,128)(2,1)}, bf16[256,2048]{1,0:T(8,128)(2,1)S(1)}, u32[]{:S(2)}, u32[]{:S(2)}) collective-permute-start(bf16[256,2048]{1,0:T(8,128)(2,1)} %collective-permute-done.3), channel_id=1, source_target_pairs={{0,2},{1,3},{2,0},{3,1},{4,6},{5,7},{6,4},{7,5},{8,10},{9,11},{10,... | collective-permute-start | bytes 3145736 | tf_op jit(solution)/shard_map/ppermute | solution.py:14
  636.8 25.0 %collective-permute-start.5 = (bf16[256,2048]{1,0:T(8,128)(2,1)S(1)}, bf16[256,2048]{1,0:T(8,128)(2,1)}, u32[]{:S(2)}, u32[]{:S(2)}) collective-permute-start(bf16[256,2048]{1,0:T(8,128)(2,1)S(1)} %collective-permute-done.4), channel_id=1, source_target_pairs={{0,4},{1,5},{2,6},{3,7},{4,0},{5,1},{6,2},{7,3},{8,12},{9,13},{10,... | collective-permute-start | bytes 3145736 | tf_op jit(solution)/shard_map/ppermute | solution.py:14
  638.2 37.5 %copy-start.77 = (f32[256]{0:T(256)S(1)}, f32[256]{0:T(256)}, u32[]{:S(2)}) copy-start(f32[256]{0:T(256)} %copy-done.76) | copy-start | bytes 3076
  640.0 35.7 %copy-start.20 = (f32[256,2048]{1,0:T(8,128)S(1)}, f32[256,2048]{1,0:T(8,128)}, u32[]{:S(2)}) copy-start(f32[256,2048]{1,0:T(8,128)} %copy.72) | copy-start | bytes 6291460
  732.0 3.6 copy-start.1
  (39 other events, 83.3 us)
Sparse Core Ops, SparseCore 0:
  134.2 55.6 all-gather.10
  192.3 54.4 all-gather.12
  299.3 54.3 all-gather.16
  355.5 54.3 all-gather.14
  478.2 39.0 reduce-scatter.4
  520.7 115.9 reduce-scatter.2
  639.2 92.7 all-reduce.16
where the time goes:
time: 757 us; the launch traced here: 743 us
  waiting for transfers between devices  402 us (53%)
  matrix products  121 us (16%)
  local copies, waits for them, and re-layouts  99.3 us (13%)
  other arithmetic  75.9 us (10%)
  blocking collectives  19.2 us (3%)
  between operations  15.5 us (2%)
  starting transfers between devices  9.26 us (1%)
    reduce_scatter x1, waiting for transfers between devices, shards(): lax.psum_scatter(term_x, 'ctx', scatter_dimension=0, tiled=True)  119 us
    ppermute x6, waiting for transfers between devices, swapped(): lax.ppermute(array, axis, [(i, i ^ 1 << apart) for i in range(lax.axis_si...  111 us
    all_gather x4, waiting for transfers between devices, carried_in(): everything = jax.tree.map(lambda part: lax.all_gather(part, axis), array)  104 us
    psum x1, waiting for transfers between devices, shards(): grad_x, grad_small = lax.psum((shard_x, shard_small), 'dp')  54.9 us
    dot_general x6, matrix products, forward_y(): inner = jnp.einsum('hts,shp->thp', mixing, per_head, precision=precise)  53.4 us
    select_n x16, other arithmetic, step(): return jax.tree.map(lambda a, b: jnp.where(reached, a, b), new, before)  39.9 us
    mul x32, local copies, waits for them, and re-layouts, chain(): later[0][:, None, None] * earlier[1] + later[1]  21.9 us
    another operation x18, other arithmetic  19.6 us
  transfers between devices with their start and end apart: 13, of which 11 were waited for; matrix products, arithmetic and copies ran while one was open for 19% of the time, Pallas kernels for 0%

commit v1 on v0

v1 whole, which is shorter than its diff:
```python
import functools

import jax
import jax.numpy as jnp
from jax import lax
from jax.experimental import pallas as pl
from jax.experimental.pallas import tpu as pltpu
from jax.sharding import PartitionSpec as P

STATE = 64
GROUP = 256
LANES = 128
BF = jnp.bfloat16
F32 = jnp.float32
precise = lax.Precision.HIGHEST
ORDER = pl.BlockSpec(memory_space=pl.ANY)
SCALARS = pl.BlockSpec(memory_space=pltpu.SMEM)
PARAMS = pltpu.CompilerParams(vmem_limit_bytes=48 * 2**20)


def send(array, axis, mask):
    return lax.ppermute(array, axis, [(i, i ^ mask) for i in range(lax.axis_size(axis))])


def mm(a, b, ca=1, cb=0):
    return lax.dot_general(a, b, (((ca,), (cb,)), ((), ())), preferred_element_type=F32)


def exact(a, b, ca=1, cb=0):
    dims = (((ca,), (cb,)), ((), ()))
    return lax.dot_general(a, b, dims, precision=precise, preferred_element_type=F32)


def split(a):
    high = a.astype(BF)
    return high, (a - high.astype(F32)).astype(BF)


def split_three(a, axis):
    high, rest = split(a)
    middle, low = split(a - high.astype(F32))
    return jnp.concatenate([high, middle, low], axis=axis)


def iota(shape, axis):
    return lax.broadcasted_iota(jnp.int32, shape, axis)


def ordered(rows, branch, strict_after=False):
    t, s = iota((rows, rows), 0), iota((rows, rows), 1)
    return (t >= s) if (branch == 0) != strict_after else (t <= s)


def mirror(width):
    return (iota((width, width), 0) + iota((width, width), 1) == width - 1).astype(BF)


def spread(heads, channels, start, copies):
    head = iota((heads, GROUP if start is not None else channels), 0)
    lane = iota((heads, GROUP if start is not None else channels), 1)
    size = channels // heads
    first = 0 if start is None else start
    one = (head == lane // size + first).astype(BF)
    return jnp.concatenate([one] * copies, axis=0)


def flip_lanes(a, eye):
    parts = [mm(a[:, k : k + GROUP], eye).astype(BF) for k in range(0, a.shape[1], GROUP)]
    return jnp.concatenate(parts[::-1], axis=1)


def softplus(a):
    return jnp.maximum(a, 0.0) + jnp.log1p(jnp.exp(-jnp.abs(a)))


def whole(a):
    return pl.BlockSpec(a.shape, lambda *_: (0,) * a.ndim)


def padded(a):
    return jnp.concatenate([a, jnp.zeros((a.shape[0], LANES - a.shape[1]), a.dtype)], axis=1)


CUM, STEP = LANES, 2 * LANES


def small_kernel(
    h_ref, ws_ref, rate_ref, bias_ref,
    both_ref, nat_ref, lines_ref, cg3_ref, bf3_ref, bt_ref, weight3_ref, tot3_ref,
):
    rows, channels = h_ref.shape
    heads = rate_ref.shape[1]
    eye = mirror(GROUP)
    both_ref[:rows] = h_ref[...]
    for k in range(0, channels, GROUP):
        both_ref[rows:, channels - k - GROUP : channels - k] = mm(
            h_ref[:, k : k + GROUP], eye
        ).astype(BF)
    projected = mm(both_ref[...], ws_ref[...])
    for branch in range(2):
        p = projected[branch * rows : (branch + 1) * rows]
        b, c = p[:, :STATE], p[:, STATE : 2 * STATE]
        pre = p[:, 2 * STATE :] + bias_ref[...]
        step = softplus(pre)
        la = -jnp.exp(rate_ref[...]) * step
        cum = exact(ordered(rows, branch).astype(F32), la)
        tot = cum[rows - 1 :] if branch == 0 else cum[:1]
        fade = jnp.exp(tot - cum)
        wide_step, wide_cum = padded(step), padded(cum)
        nat_ref[branch, :, :CUM] = p[:, : 2 * STATE]
        nat_ref[branch, :, CUM:STEP] = wide_cum
        nat_ref[branch, :, STEP:] = padded(jnp.concatenate([step, pre], axis=1))
        lines_ref[branch, :heads] = wide_cum.T[:heads]
        lines_ref[branch, heads:] = wide_step.T[:heads]
        b_high, b_low = split(b)
        c_high, c_low = split(c)
        grow3 = split_three(jnp.exp(cum), 1)
        cg3_ref[branch] = jnp.concatenate(
            [c_high, c_low, c_high, grow3, jnp.zeros_like(grow3)], axis=1
        )
        bf3_ref[branch] = jnp.concatenate(
            [b_high, b_low, b_high, split_three(fade, 1), split_three(step, 1)], axis=1
        )
        bt_ref[branch] = jnp.concatenate([b_high, b_low], axis=1).T
        weight3_ref[branch] = split_three(fade * step, 1)
        tot3_ref[branch] = split_three(jnp.broadcast_to(tot, (8, heads)), 1)


def project_small(h, ws, log_rates, step_bias):
    rows, channels = h.shape
    heads = log_rates.shape[0]
    f32 = lambda *shape: jax.ShapeDtypeStruct(shape, F32)
    bf16 = lambda *shape: jax.ShapeDtypeStruct(shape, BF)
    return pl.pallas_call(
        small_kernel,
        out_shape=[
            bf16(2 * rows, channels),
            f32(2, rows, 3 * LANES),
            f32(2, 2 * heads, rows),
            bf16(2, rows, 3 * STATE + 6 * heads),
            bf16(2, rows, 3 * STATE + 6 * heads),
            bf16(2, 2 * STATE, rows),
            bf16(2, rows, 3 * heads),
            bf16(2, 8, 3 * heads),
        ],
        compiler_params=PARAMS,
        name="small",
    )(h, ws, log_rates[None], step_bias[None])


def project_kernel(both_ref, w_ref, bt_ref, weight3_ref, tot3_ref, x_ref, end_ref):
    at = pl.program_id(0)
    rows = x_ref.shape[1]
    heads = weight3_ref.shape[2] // 3
    channels = both_ref.shape[1]
    copier = spread(heads, channels, at * (GROUP * heads // channels), 3)
    values = mm(both_ref[...], w_ref[...]).astype(BF)
    for branch in range(2):
        x = values[branch * rows : (branch + 1) * rows]
        x_ref[branch] = x
        weighted = mm(weight3_ref[branch], copier) * x.astype(F32)
        both = mm(bt_ref[branch], weighted.astype(BF))
        end_ref[branch, :STATE] = both[:STATE] + both[STATE:]
        end_ref[branch, STATE:] = mm(tot3_ref[branch], copier)


def project(both, w, bt, weight3, tot3):
    rows, channels = both.shape[0] // 2, both.shape[1]
    return pl.pallas_call(
        project_kernel,
        grid=(channels // GROUP,),
        in_specs=[
            whole(both),
            pl.BlockSpec((channels, GROUP), lambda j: (0, j)),
            whole(bt),
            whole(weight3),
            whole(tot3),
        ],
        out_specs=[
            pl.BlockSpec((2, rows, GROUP), lambda j: (0, 0, j)),
            pl.BlockSpec((2, STATE + 8, GROUP), lambda j: (0, 0, j)),
        ],
        out_shape=[
            jax.ShapeDtypeStruct((2, rows, channels), BF),
            jax.ShapeDtypeStruct((2, STATE + 8, channels), F32),
        ],
        compiler_params=PARAMS,
        name="project",
    )(both, w, bt, weight3, tot3)


def own_lanes(a, k, size):
    lane = iota(a.shape, 1) // size
    return jnp.where(lane == k, a.astype(F32), 0.0).astype(BF)


def inner_kernel(x_ref, nat_ref, lines_ref, sent, left, raw_ref, score):
    at = pl.program_id(0)
    rows = x_ref.shape[1]
    heads = lines_ref.shape[1] // 2
    size = x_ref.shape[2] * pl.num_programs(0) // heads
    half = rows // 2
    per = GROUP // size

    @pl.when(at == 0)
    def _():
        for branch in range(2):
            b, c = nat_ref[branch, :, :STATE], nat_ref[branch, :, STATE : 2 * STATE]
            full = exact(c, b, 1, 1)
            score[branch] = jnp.where(ordered(rows, branch), full, 0.0)

    for branch in range(2):
        alone, later = (0, half) if branch == 0 else (half, 0)
        columns = pltpu.roll(nat_ref[branch, :, CUM:STEP], -(at * per) % LANES, 1)
        tops, bottoms = 0.0, 0.0
        for k in range(per):
            line = lines_ref[branch, pl.ds(at * per + k, 1), :]
            step = lines_ref[branch, pl.ds(heads + at * per + k, 1), :]
            xk = own_lanes(x_ref[branch], k, size)
            own = pl.ds(alone, half)
            gap = jnp.minimum(columns[alone : alone + half, k : k + 1] - line[:, alone : alone + half], 0.0)
            m = jnp.exp(gap) * score[branch, own, own] * step[:, alone : alone + half]
            tops = tops + mm(m.astype(BF), xk[alone : alone + half])
            gap = jnp.minimum(columns[later : later + half, k : k + 1] - line, 0.0)
            m = jnp.exp(gap) * score[branch, pl.ds(later, half), :] * step
            bottoms = bottoms + mm(m.astype(BF), xk)
        raw_ref[branch, pl.ds(alone, half), :] = tops
        raw_ref[branch, pl.ds(later, half), :] = bottoms


def inner(x, nat, lines, sent, left):
    _, rows, channels = x.shape
    block = pl.BlockSpec((2, rows, GROUP), lambda j: (0, 0, j))
    return pl.pallas_call(
        inner_kernel,
        grid=(channels // GROUP,),
        in_specs=[block, whole(nat), whole(lines), ORDER, ORDER],
        out_specs=block,
        out_shape=jax.ShapeDtypeStruct(x.shape, F32),
        scratch_shapes=[pltpu.VMEM((2, rows, rows), F32)],
        compiler_params=PARAMS,
        name="inner",
    )(x, nat, lines, sent, left)


class Scalars:
    def __init__(self, chips, ref=None):
        self.chips, self.ref = chips, ref
        self.bits = bits_of(chips)

    def made(self):
        place = lax.axis_index("ctx")
        chip, core = place // 2, place % 2
        at = chip ^ jnp.arange(1, self.chips)
        up = (chip ^ jnp.array(self.bits)) > chip
        reach = jnp.concatenate([at < chip, at > chip])
        left = (at[None] > at[:, None]) & (at[None] < chip)
        right = (at[None] > chip) & (at[None] < at[:, None])
        parts = [jnp.stack([core == 0, core == 1]), up, reach, left.ravel(), right.ravel()]
        return jnp.concatenate(parts).astype(F32)

    def first(self, slot):
        return self.ref[slot]

    def up(self, n):
        return self.ref[2 + n]

    def reach(self, slot, m):
        return self.ref[2 + len(self.bits) + slot * (self.chips - 1) + m]

    def between(self, slot, m, k):
        most = self.chips - 1
        return self.ref[2 + len(self.bits) + 2 * most + (slot * most + m) * most + k]


def merge_kernel(chips, turned, scalars_ref, *refs):
    scalars = Scalars(chips, scalars_ref)
    if turned:
        tots_ref, own_ref, near_ref, *outs = refs
    else:
        own_ref, near_ref, *outs = refs
    sums, tots = [], []
    for slot in range(2):
        if turned:
            own, other = tots_ref[1 - slot : 2 - slot], tots_ref[3 - slot : 4 - slot]
        else:
            own, other = (ref[slot, STATE : STATE + 1] for ref in (own_ref, near_ref))
            tots.append(own + other)
        first = scalars.first(slot)
        a = first * jnp.exp(other) + (1.0 - first)
        p = first + (1.0 - first) * jnp.exp(own)
        sums.append(a * own_ref[slot, :STATE] + p * near_ref[slot, :STATE])
    for n, out in enumerate(outs):
        up = scalars.up(n)
        out[:STATE] = (up * sums[0] + (1.0 - up) * sums[1]).astype(BF)
        if not turned:
            extra = jnp.concatenate(tots + [jnp.zeros((6, tots[0].shape[1]), F32)], axis=0)
            high, rest = split(extra)
            middle, low = split(extra - high.astype(F32))
            for k, part in enumerate((high, middle, low)):
                out[STATE + 16 * k : STATE + 16 * (k + 1)] = jnp.concatenate(
                    [part, jnp.zeros_like(part)], axis=0
                )


def merge(chips, scalars, own, near, tots=None):
    channels = own.shape[2]
    rows = STATE if tots is not None else STATE + 48
    given = [own, near] if tots is None else [tots, own, near]
    bits = bits_of(chips)
    return pl.pallas_call(
        functools.partial(merge_kernel, chips, tots is not None),
        in_specs=[SCALARS] + [pl.BlockSpec(memory_space=pltpu.VMEM)] * len(given),
        out_shape=[jax.ShapeDtypeStruct((rows, channels), BF) for _ in bits],
        compiler_params=PARAMS,
        name="merge",
    )(scalars, *given)


def exchange(chips, sums):
    return [send(sums[m.bit_length() - 1], "ctx", 2 * m) for m in range(1, chips)]


def gather_states(scalars, tot, near_ref, arrived, out):
    for slot in range(2):
        last = 1.0 - scalars.first(slot)
        total = last * near_ref[slot, :STATE]
        for m, ref in enumerate(arrived):
            weight = last * tot(1, slot)
            for k in range(len(arrived)):
                weight = weight + scalars.between(slot, m, k) * tot(2 + k, slot)
            weight = scalars.reach(slot, m) * jnp.exp(weight)
            total = total + weight * ref[:STATE].astype(F32)
        out(slot, total)


TILE = 128


def normed_kernel(count, heads, raw_ref, cg3_ref, gain_ref, cot_ref, scalars_ref, own_ref, near_ref, *refs):
    arrived, refs = refs[:count], refs[count:]
    mixed_ref, draw_ref, ry_ref, adj_ref, dc_ref, s_ref, tots_ref, s3 = refs
    at = pl.program_id(0)
    channels = raw_ref.shape[2]
    copier = spread(heads, channels, None, 3)

    @pl.when(at == 0)
    def _():
        rows = [own_ref[0, :1], own_ref[1, :1]]
        rows += [near_ref[0, STATE : STATE + 1], near_ref[1, STATE : STATE + 1]]
        for ref in arrived:
            parts = [ref[STATE + 16 * k : STATE + 16 * (k + 1)].astype(F32) for k in range(3)]
            both = parts[0] + parts[1] + parts[2]
            rows += [both[:1], both[1:2]]
        fill = tots_ref.shape[0] - len(rows)
        tots_ref[...] = jnp.concatenate(rows + [jnp.zeros((fill, channels), F32)], axis=0)

        def out(slot, total):
            s_ref[slot] = total
            high, low = split(total)
            s3[slot, :STATE] = high
            s3[slot, STATE : 2 * STATE] = high
            s3[slot, 2 * STATE :] = low

        scalars = Scalars(count + 1, scalars_ref)
        gather_states(scalars, lambda n, slot: rows[2 * n + slot], near_ref, arrived, out)
        adj_ref[...] = jnp.zeros_like(adj_ref)

    eye = mirror(GROUP)
    one = spread(heads, channels, None, 1)
    ys = []
    for branch in range(2):
        c3 = cg3_ref[branch, :, : 3 * STATE]
        grow = mm(cg3_ref[branch, :, 3 * STATE : 3 * STATE + 3 * heads], copier)
        r = raw_ref[branch] + grow * mm(c3, s3[branch])
        scale = lax.rsqrt(jnp.sum(r * r, axis=1, keepdims=True) * (1.0 / channels) + 1e-05)
        n = r * scale
        ys.append(n * gain_ref[...])
        cot = cot_ref[...] if branch == 0 else flip_lanes(cot_ref[...], eye)
        dz = cot.astype(F32) * gain_ref[...]
        mean = jnp.sum(dz * n, axis=1, keepdims=True) * (1.0 / channels)
        draw = scale * (dz - n * mean)
        draw_ref[branch] = draw.astype(BF)
        high, low = split(draw * r)
        ry_ref[branch] = mm(high, one, 1, 1) + mm(low, one, 1, 1)
        grown = (grow * draw).astype(BF)
        both = mm(c3[:, : 2 * STATE].T, grown)
        adj_ref[1 - branch] += both[:STATE] + both[STATE:]
        both = mm(grown, s3[branch, STATE:], 1, 1)
        dc_ref[branch] = both[:, :STATE] + both[:, STATE:]
    back = flip_lanes(ys[1].astype(BF), eye)
    mixed_ref[...] = (ys[0] + back.astype(F32)).astype(BF)


def normed(raw, cg3, gain, cot, scalars, ends, near, arrived):
    _, rows, channels = raw.shape
    heads = (cg3.shape[2] - 3 * STATE) // 6
    band = lambda n: pl.BlockSpec((2, TILE, n), lambda j: (0, j, 0))
    flat = pl.BlockSpec((TILE, channels), lambda j: (j, 0))
    gain = gain[None]
    state = pl.BlockSpec((2, STATE, channels), lambda j: (0, 0, 0))
    tots = -(-2 * (len(arrived) + 2) // 8) * 8
    return pl.pallas_call(
        functools.partial(normed_kernel, len(arrived), heads),
        grid=(rows // TILE,),
        in_specs=[band(channels), band(cg3.shape[2]), whole(gain), flat, SCALARS]
        + [pl.BlockSpec((2, 8, channels), lambda j: (0, STATE // 8, 0))]
        + [whole(a) for a in (near, *arrived)],
        out_specs=[flat, band(channels), band(heads), state, band(STATE), state]
        + [pl.BlockSpec((tots, channels), lambda j: (0, 0))],
        out_shape=[
            jax.ShapeDtypeStruct((rows, channels), BF),
            jax.ShapeDtypeStruct((2, rows, channels), BF),
            jax.ShapeDtypeStruct((2, rows, heads), F32),
            jax.ShapeDtypeStruct((2, STATE, channels), F32),
            jax.ShapeDtypeStruct((2, rows, STATE), F32),
            jax.ShapeDtypeStruct((2, STATE, channels), F32),
            jax.ShapeDtypeStruct((tots, channels), F32),
        ],
        scratch_shapes=[pltpu.VMEM((2, 3 * STATE, channels), BF)],
        compiler_params=PARAMS,
        name="normed",
    )(raw, cg3, gain, cot, scalars, ends, near, *arrived)


def inner_back_kernel(
    x_ref, draw_ref, nat_ref, lines_ref, after, u_ref, db_ref, dc_ref, score, ds_all, ds_own,
):
    at = pl.program_id(0)
    rows = x_ref.shape[1]
    heads = lines_ref.shape[1] // 2
    size = x_ref.shape[2] * pl.num_programs(0) // heads
    half = rows // 2
    per = GROUP // size

    @pl.when(at == 0)
    def _():
        for branch in range(2):
            b, c = nat_ref[branch, :, :STATE], nat_ref[branch, :, STATE : 2 * STATE]
            full = exact(b, c, 1, 1)
            score[branch] = jnp.where(ordered(rows, 1 - branch), full, 0.0)
        ds_all[...] = jnp.zeros_like(ds_all)
        ds_own[...] = jnp.zeros_like(ds_own)

    for branch in range(2):
        alone, first = (half, 0) if branch == 0 else (0, half)
        columns = pltpu.roll(nat_ref[branch, :, CUM:STEP], -(at * per) % LANES, 1)
        steps = pltpu.roll(nat_ref[branch, :, STEP:], -(at * per) % LANES, 1)
        draw = draw_ref[branch]
        tops, bottoms = 0.0, 0.0
        for k in range(per):
            line = lines_ref[branch, pl.ds(at * per + k, 1), :]
            dk = own_lanes(draw, k, size)
            xk = own_lanes(x_ref[branch], k, size)
            gap = line[:, alone : alone + half] - columns[alone : alone + half, k : k + 1]
            d = jnp.exp(jnp.minimum(gap, 0.0))
            m = d * score[branch, pl.ds(alone, half), pl.ds(alone, half)]
            bottoms = bottoms + mm(m.astype(BF), dk[alone : alone + half])
            xd = mm(xk[alone : alone + half], draw[alone : alone + half], 1, 1)
            ds_own[branch] += d * xd * steps[alone : alone + half, k : k + 1]
            gap = line - columns[first : first + half, k : k + 1]
            d = jnp.exp(jnp.minimum(gap, 0.0))
            m = d * score[branch, pl.ds(first, half), :]
            tops = tops + mm(m.astype(BF), dk)
            xd = mm(xk[first : first + half], draw, 1, 1)
            ds_all[branch] += d * xd * steps[first : first + half, k : k + 1]
        u_ref[branch, pl.ds(alone, half), :] = bottoms
        u_ref[branch, pl.ds(first, half), :] = tops

    @pl.when(at == pl.num_programs(0) - 1)
    def _():
        for branch in range(2):
            alone, first = (half, 0) if branch == 0 else (0, half)
            place, column = iota((half, rows), 0) + first, iota((half, rows), 1)
            seen = (place <= column) if branch == 0 else (place >= column)
            all_part = jnp.where(seen, ds_all[branch], 0.0)
            own_part = jnp.where(ordered(half, 1 - branch), ds_own[branch], 0.0)
            b, c = nat_ref[branch, :, :STATE], nat_ref[branch, :, STATE : 2 * STATE]
            db_ref[branch, pl.ds(first, half), :] = exact(all_part, c)
            db_ref[branch, pl.ds(alone, half), :] = exact(own_part, c[alone : alone + half])
            dc = exact(all_part.T, b[first : first + half])
            dc_own = dc[alone : alone + half] + exact(own_part.T, b[alone : alone + half])
            dc_ref[branch, pl.ds(first, half), :] = dc[first : first + half]
            dc_ref[branch, pl.ds(alone, half), :] = dc_own


def inner_back(x, draw, nat, lines, after):
    _, rows, channels = x.shape
    block = pl.BlockSpec((2, rows, GROUP), lambda j: (0, 0, j))
    return pl.pallas_call(
        inner_back_kernel,
        grid=(channels // GROUP,),
        in_specs=[block, block, whole(nat), whole(lines), ORDER],
        out_specs=[block] + [pl.BlockSpec((2, rows, STATE), lambda j: (0, 0, 0))] * 2,
        out_shape=[
            jax.ShapeDtypeStruct(x.shape, F32),
            jax.ShapeDtypeStruct((2, rows, STATE), F32),
            jax.ShapeDtypeStruct((2, rows, STATE), F32),
        ],
        scratch_shapes=[
            pltpu.VMEM((2, rows, rows), F32),
            pltpu.VMEM((2, rows // 2, rows), F32),
            pltpu.VMEM((2, rows // 2, rows // 2), F32),
        ],
        compiler_params=PARAMS,
        name="inner_back",
    )(x, draw, nat, lines, after)


def finish_kernel(first, count, last, heads, channels, *refs):
    x_ref, u_ref, bf3_ref, s_ref, end_ref, tots_ref, scalars_ref, near_ref, *refs = refs
    arrived, refs = refs[:count], refs[count:]
    if last:
        nat_ref, db_ref, dc_ref, dc0_ref, ry_ref, rate_ref, *refs = refs
        before, refs = refs[: len(refs) - 4], refs[len(refs) - 4 :]
    out_ref, dbs_ref, direct_ref, dtot_ref = refs
    at = pl.program_id(0)
    start = (first + at) * (GROUP * heads // channels)
    one = spread(heads, channels, start, 1)
    copier = spread(heads, channels, start, 3)
    columns = pl.ds(pl.multiple_of(at * GROUP, GROUP), GROUP)

    def per_head(a):
        high, low = split(a)
        return mm(high, one, 1, 1) + mm(low, one, 1, 1)

    @pl.when(at == 0)
    def _():
        dbs_ref[...] = jnp.zeros_like(dbs_ref)
        direct_ref[...] = jnp.zeros_like(direct_ref)
        dtot_ref[...] = jnp.zeros_like(dtot_ref)

    def tot(n, slot):
        at = 2 * n + 1 - slot
        return tots_ref[at : at + 1]

    def out(slot, g):
        branch = 1 - slot
        g_high, g_low = split(g)
        us = mm(bf3_ref[branch, :, : 3 * STATE], jnp.concatenate([g_high, g_high, g_low], axis=0))
        fade = mm(bf3_ref[branch, :, 3 * STATE : 3 * STATE + 3 * heads], copier)
        step = mm(bf3_ref[branch, :, 3 * STATE + 3 * heads :], copier)
        both = u_ref[branch] + fade * us
        xf = x_ref[branch].astype(F32)
        dx = (step * both).astype(BF)
        if last:
            out_ref[branch, :, columns] = dx
        else:
            out_ref[branch] = dx
        direct_ref[branch] += per_head(xf * both)
        weighted = (fade * step * xf).astype(BF)
        sums = mm(weighted, jnp.concatenate([g_high, g_low], axis=0), 1, 1)
        dbs_ref[branch] += sums[:, :STATE] + sums[:, STATE:]
        ended = jnp.exp(tot(0, slot)) * s_ref[branch] + end_ref[branch]
        kept = jnp.sum(g * ended, axis=0, keepdims=True)
        kept = jnp.concatenate([kept, jnp.zeros((7, GROUP), F32)], axis=0)
        dtot_ref[branch] += per_head(kept)[:1]

    gather_states(Scalars(count + 1, scalars_ref), tot, near_ref, arrived, out)

    if last:

        @pl.when(at == pl.num_programs(0) - 1)
        def _():
            rows, width = direct_ref.shape[1], out_ref.shape[2] - 2 * STATE - heads
            for branch in range(2):
                dbs, direct, dtot = dbs_ref[branch], direct_ref[branch], dtot_ref[branch]
                for n in range(0, len(before), 3):
                    dbs = dbs + before[n][branch]
                    direct = direct + before[n + 1][branch]
                    dtot = dtot + before[n + 2][branch]
                step = nat_ref[branch, :, STEP : STEP + heads]
                pre = nat_ref[branch, :, STEP + heads : STEP + 2 * heads]
                dcum = ry_ref[branch] - step * direct
                dla = exact(ordered(rows, 1 - branch).astype(F32), dcum) + dtot
                dpre = (direct - jnp.exp(rate_ref[...]) * dla) * jax.nn.sigmoid(pre)
                small = [db_ref[branch] + dbs, dc_ref[branch] + dc0_ref[branch], dpre]
                out_ref[branch, :, width:] = jnp.concatenate(small, axis=1).astype(BF)


def finish(piece, pieces, x, u, bf3, s_in, ends, tots, scalars, near, arrived, more, before):
    _, rows, channels = x.shape
    heads = (bf3.shape[2] - 3 * STATE) // 6
    last = piece == pieces - 1
    groups = channels // GROUP // pieces
    first = piece * groups
    block = pl.BlockSpec((2, rows, GROUP), lambda j: (0, 0, first + j))
    state = pl.BlockSpec((2, STATE, GROUP), lambda j: (0, 0, first + j))
    flat = lambda n: pl.BlockSpec((n, GROUP), lambda j: (0, first + j))
    extra = [*more, *before] if last else []
    width = groups * GROUP + (2 * STATE + heads if last else 0)
    sums = [(2, rows, STATE), (2, rows, heads), (2, 1, heads)]
    return pl.pallas_call(
        functools.partial(finish_kernel, first, len(arrived), last, heads, channels),
        grid=(groups,),
        in_specs=[block, block, whole(bf3), state, state, flat(tots.shape[0]), SCALARS, state]
        + [flat(STATE)] * len(arrived)
        + [whole(a) for a in extra],
        out_specs=[
            pl.BlockSpec((2, rows, width), lambda j: (0, 0, 0))
            if last
            else pl.BlockSpec((2, rows, GROUP), lambda j: (0, 0, j))
        ]
        + [pl.BlockSpec(shape, lambda j: (0, 0, 0)) for shape in sums],
        out_shape=[jax.ShapeDtypeStruct((2, rows, width), BF)]
        + [jax.ShapeDtypeStruct(shape, F32) for shape in sums],
        compiler_params=PARAMS,
        name="finish",
    )(x, u, bf3, s_in, ends, tots, scalars, near, *arrived, *extra)


def turned_kernel(
    chips, where_ref, own_ref, own_mirror_ref, peer_ref, peer_mirror_ref, after, out_ref, held
):
    parts = where_ref.shape[0] - chips
    wide, rows = held.shape[1], held.shape[2]
    thin = wide // parts
    eye = (iota((wide, wide), 0) == iota((wide, wide), 1)).astype(BF)
    back = mirror(wide)
    sources = [(own_ref, eye), (own_mirror_ref, back), (peer_ref, eye), (peer_mirror_ref, back)]
    for n, (ref, turn) in enumerate(sources):
        held[n] = mm(turn, ref[...], 1, 1).astype(BF)
    for n in range(4):
        for k in range(parts):
            start = pl.multiple_of(where_ref[chips + k] * thin, thin)
            out_ref[k * thin : (k + 1) * thin, n * rows : (n + 1) * rows] = held[
                n, pl.ds(start, thin), :
            ]


def turned(h, peer, where, chips, after):
    rows, channels = h.shape
    wide = channels // (2 * chips)
    plain = pl.BlockSpec((rows, wide), lambda m, where: (0, where[m]))
    other = pl.BlockSpec((rows, wide), lambda m, where: (0, 2 * chips - 1 - where[m]))
    return pl.pallas_call(
        functools.partial(turned_kernel, chips),
        grid_spec=pltpu.PrefetchScalarGridSpec(
            num_scalar_prefetch=1,
            grid=(chips,),
            in_specs=[plain, other, plain, other, ORDER],
            out_specs=pl.BlockSpec((wide, 4 * rows), lambda m, where: (m, 0)),
            scratch_shapes=[pltpu.VMEM((4, wide, rows), BF)],
        ),
        out_shape=jax.ShapeDtypeStruct((chips * wide, 4 * rows), BF),
        compiler_params=PARAMS,
        name="turned",
    )(where, h, h, peer, peer, after)


def by_bits(size, bits):
    return sorted(range(size), key=lambda k: [k & bit for bit in bits])


def bits_of(size):
    return [1 << k for k in range(size.bit_length() - 1)]


def term_kernel(orders, cuts, left_ref, own_ref, peer_ref, *outs):
    depth = own_ref.shape[0]
    wide = left_ref.shape[0] // len(orders[0])
    for part, (order, (low, high)) in enumerate(zip(orders, cuts)):
        stay_ref, go_ref = outs[2 * part : 2 * part + 2]
        half = len(order) // 2
        for n, block in enumerate(order):
            left = left_ref[block * wide : (block + 1) * wide]
            term = mm(left[:, :depth], own_ref[:, low:high])
            term = term + mm(left[:, depth:], peer_ref[:, low:high])
            if n < half:
                stay_ref[n * wide : (n + 1) * wide] = term
            else:
                go_ref[(n - half) * wide : (n - half + 1) * wide] = term.astype(BF)


def weight_terms(left, own, peer, orders, cuts):
    rows = left.shape[0] // 2
    shape = lambda cut, kind: jax.ShapeDtypeStruct((rows, cut[1] - cut[0]), kind)
    outs = pl.pallas_call(
        functools.partial(term_kernel, orders, cuts),
        out_shape=[shape(cut, kind) for cut in cuts for kind in (F32, BF)],
        compiler_params=PARAMS,
        name="terms",
    )(left, own, peer)
    return [outs[n : n + 2] for n in range(0, len(outs), 2)]


def fold_kernel(count, final, *refs):
    given, outs = refs[: 2 * count], refs[2 * count :]
    joined = len(outs) < 2 * count
    column = 0
    for n in range(count):
        stay_ref, got_ref = given[2 * n : 2 * n + 2]
        rows, width = stay_ref.shape
        total = stay_ref[...] + got_ref[...].astype(F32)
        columns = slice(column, column + width)
        if final:
            outs[0][:, columns] = total.astype(BF)
        else:
            keep, go = outs[:2] if joined else outs[2 * n : 2 * n + 2]
            keep[:, columns] = total[: rows // 2]
            go[:, columns] = total[rows // 2 :].astype(BF)
        column = column + width if joined else 0


def fold(parts, join=False, final=False):
    rows = parts[0][0].shape[0] if final else parts[0][0].shape[0] // 2
    widths = [stay.shape[1] for stay, _ in parts]
    widths = [sum(widths)] if join else widths
    kinds = [BF] if final else [F32, BF]
    outs = pl.pallas_call(
        functools.partial(fold_kernel, len(parts), final),
        out_shape=[jax.ShapeDtypeStruct((rows, w), kind) for w in widths for kind in kinds],
        compiler_params=PARAMS,
        name="fold",
    )(*[a for part in parts for a in part])
    return outs[0] if final else [outs[n : n + 2] for n in range(0, len(outs), 2)]


def summed(parts, orders):
    dps = lax.axis_size("dp")
    dp_bits = bits_of(dps)
    for n in range(len(orders[0])):
        sent = [send(go, "ctx", 2 * bits[n]) for (_, go), bits in zip(parts, orders)]
        got = [(stay, came) for (stay, _), came in zip(parts, sent)]
        parts = fold(got, join=n == len(orders[0]) - 1)
    for n, bit in enumerate(dp_bits):
        stay, go = parts[0]
        last = n == len(dp_bits) - 1
        parts = fold([(stay, send(go, "dp", bit))], join=True, final=last)
    held, came = parts, None
    for bit in dp_bits[::-1]:
        if came is not None:
            held = jnp.concatenate([held, came])
        came = send(held, "dp", bit)
    return held, came


def place_kernel(chips, where_ref, *refs):
    given, (grad_x_ref, grad_small_ref) = refs[:-2], refs[-2:]
    dps = where_ref.shape[0] - chips
    thin = grad_x_ref.shape[0] // dps
    columns = grad_x_ref.shape[1]
    for k in range(dps):
        target = pl.ds(pl.multiple_of(where_ref[chips + k] * thin, thin), thin)
        column = 0
        for n in range(0, len(given), 2):
            ref, at = (given[n], k) if k < dps // 2 else (given[n + 1], k - dps // 2)
            piece = ref[at * thin : (at + 1) * thin].astype(F32)
            width = min(piece.shape[1], columns - column)
            grad_x_ref[target, column : column + width] = piece[:, :width]
            column += width
            if piece.shape[1] > width:
                grad_small_ref[target, :] = piece[:, width:]


def placed(chips, where, given, wide, channels, small):
    vmem = pl.BlockSpec(memory_space=pltpu.VMEM)
    return pl.pallas_call(
        functools.partial(place_kernel, chips),
        in_specs=[SCALARS] + [vmem] * len(given),
        out_shape=[
            jax.ShapeDtypeStruct((wide, channels), F32),
            jax.ShapeDtypeStruct((wide, small), F32),
        ],
        compiler_params=PARAMS,
        name="placed",
    )(where, *given)


PIECES = 2


def shards(hidden, x_weight, state_weight, log_rates, step_bias, out_gain, cotangent):
    h, cot = hidden[0], cotangent[0]
    rows, channels = h.shape
    chips = lax.axis_size("ctx") // 2
    place = lax.axis_index("ctx")
    dps, dp_place = lax.axis_size("dp"), lax.axis_index("dp")
    scalars = Scalars(chips).made()
    where = (place ^ (2 * jnp.arange(chips)), dp_place ^ jnp.array(by_bits(dps, bits_of(dps))))
    where = jnp.concatenate(where).astype(jnp.int32)
    peer_h = send(h, "ctx", 1)
    both, nat, lines, cg3, bf3, bt, weight3, tot3 = project_small(
        h, state_weight, log_rates, step_bias
    )
    x, ends = project(both, x_weight, bt, weight3, tot3)
    near = send(ends, "ctx", 1)
    left = turned(h, peer_h, where, chips, ends)
    sums = merge(chips, scalars, ends, near)
    arrived = exchange(chips, sums)
    raw = inner(x, nat, lines, sums[0], left)
    mixed, draw, ry, adj, dc0, s_in, tots = normed(
        raw, cg3, out_gain, cot, scalars, ends, near, arrived
    )
    near = send(adj, "ctx", 1)
    sums = merge(chips, scalars, adj, near, tots)
    arrived = exchange(chips, sums)
    u, db, dc = inner_back(x, draw, nat, lines, sums[0])
    bits = bits_of(chips)
    orders = [bits[n:] + bits[:n] for n in range(2)]
    blocks = [by_bits(chips, order) for order in orders]
    done, before = [], []
    more = [nat, db, dc, dc0, ry, log_rates[None]]
    for n in range(PIECES):
        own, *partial = finish(
            n, PIECES, x, u, bf3, s_in, ends, tots, scalars, near, arrived, more, before
        )
        before = before + partial
        own = own.reshape(2 * rows, -1)
        peer = send(own, "ctx", 1)
        middle = channels // PIECES // 2
        cuts = [(0, middle), (middle, own.shape[1])]
        done += summed(weight_terms(left, own, peer, blocks, cuts), orders)
    wide = channels // (2 * chips)
    grad_x, grad_small = placed(chips, where, done, wide, channels, state_weight.shape[1])
    return (mixed[None], grad_x, grad_small)


def solution(mesh):
    return jax.shard_map(
        shards,
        mesh=mesh,
        in_specs=(P("dp", "ctx", None), P(), P(), P(), P(), P(), P("dp", "ctx", None)),
        out_specs=(P("dp", "ctx", None), P("ctx", None), P("ctx", None)),
        check_vma=False,
    )
```

time: 757 us -> 200 us (0.26); the launches traced: 743 us -> 199 us
  waiting for transfers between devices: 402 us -> 70.8 us
  matrix products: 121 us -> 0 us
  local copies, waits for them, and re-layouts: 99.3 us -> 18.8 us
  Pallas kernels: 0 us -> 78.3 us
  other arithmetic: 75.9 us -> 0.23 us
  starting transfers between devices: 9.26 us -> 29.9 us
  blocking collectives: 19.2 us -> 0 us
  between operations: 15.5 us -> 1.03 us
    reduce_scatter x2 -> x0, waiting for transfers between devices: 132 us -> none  [the longest x1 119 us: shards(): lax.psum_scatter(term_x, 'ctx', scatter_dimension=0, tiled=True)]
    dot_general x32 -> x0, matrix products: 121 us -> none  [the longest x6 53.4 us: forward_y(): inner = jnp.einsum('hts,shp->thp', mixing, per_head, precision=precise)]
    all_gather x4 -> x0, waiting for transfers between devices: 104 us -> none  [carried_in(): everything = jax.tree.map(lambda part: lax.all_gather(part, axis), array)]
    pallas_call x0 -> x21, Pallas kernels: none -> 78.3 us  [the longest x2 12.8 us: finish(): pl.pallas_call(functools.partial(finish_kernel, first, len(arrived), last...]
    psum x1 -> x0, waiting for transfers between devices: 54.9 us -> none  [shards(): grad_x, grad_small = lax.psum((shard_x, shard_small), 'dp')]
    rev x3 -> x0, local copies, waits for them, and re-layouts: 46.7 us -> none  [the longest x1 16.5 us: shards(): own_rc_rows = own_rows[::-1, ::-1]]
    ppermute x6 -> x27, waiting for transfers between devices: 111 us -> 70.8 us  [send(): lax.ppermute(array, axis, [(i, i ^ mask) for i in range(lax.axis_size(axi...]
    select_n x16 -> x0, other arithmetic: 39.9 us -> none  [step(): return jax.tree.map(lambda a, b: jnp.where(reached, a, b), new, before)]
  transfers between devices with their start and end apart: 13 -> 27, of which waited for: 11 -> 17; matrix products, arithmetic and copies ran while one was open for 19% -> 2% of each run, Pallas kernels for 0% -> 19%
where the time goes in v1:
time: 200 us; the launch traced here: 199 us
  Pallas kernels  78.3 us (39%)
  waiting for transfers between devices  70.8 us (35%)
  starting transfers between devices  29.9 us (15%)
  local copies, waits for them, and re-layouts  18.8 us (9%)
    ppermute x27, waiting for transfers between devices, send(): lax.ppermute(array, axis, [(i, i ^ mask) for i in range(lax.axis_size(axi...  70.8 us
    ppermute x27, starting transfers between devices, send(): lax.ppermute(array, axis, [(i, i ^ mask) for i in range(lax.axis_size(axi...  29.9 us
    unnamed x64, local copies, waits for them, and re-layouts  13.4 us
    pallas_call x2, Pallas kernels, finish(): pl.pallas_call(functools.partial(finish_kernel, first, len(arrived), last...  12.8 us
    pallas_call x1, Pallas kernels, inner_back(): pl.pallas_call(inner_back_kernel, grid=(channels // GROUP,), in_specs=[bl...  12.1 us
    pallas_call x1, Pallas kernels, project(): pl.pallas_call(project_kernel, grid=(channels // GROUP,), in_specs=[whole...  11.1 us
    pallas_call x1, Pallas kernels, normed(): pl.pallas_call(functools.partial(normed_kernel, len(arrived), heads), gri...  10.7 us
    pallas_call x2, Pallas kernels, weight_terms(): pl.pallas_call(functools.partial(term_kernel, orders, cuts), out_shape=[s...  10.1 us
  transfers between devices with their start and end apart: 27, of which 17 were waited for; matrix products, arithmetic and copies ran while one was open for 2% of the time, Pallas kernels for 19%

profile of v1, /device:TPU:0, one launch (start us, length us, event | category | flops | bytes accessed | tf_op | source)
XLA Modules:
  0.0 199.1 jit_solution(15283045217319783339)
XLA Ops:
  0.6 1.5 copy.14.ws_ref
  2.2 0.6 copy-done.25
  2.8 0.7 copy-done.27
  3.5 2.6 %small.1 = (bf16[512,2048]{1,0:T(8,128)(2,1)S(1)}, f32[2,256,384]{2,1,0:T(8,128)S(1)}, f32[2,64,256]{2,1,0:T(8,128)S(1)}, bf16[2,256,384]{2,1,0:T(8,128)(2,1)S(1...) custom-call(bf16[256,2048]{1,0:T(8,128)(2,1)S(1)} %bitcast.10, ...), custom_call_target="tpu_custom_call" | custom-call | tf_op jit(solution)/shard_map/small/pallas_call | solution.py:134
  6.1 0.9 copy-done.8
  7.0 11.1 %project.1 = (bf16[2,256,2048]{2,1,0:T(8,128)(2,1)S(1)}, f32[2,72,2048]{2,1,0:T(8,128)S(1)}) custom-call(bf16[512,2048]{1,0:T(8,128)(2,1)S(1)} %get-tuple-element.58.both_ref, bf16[2048,2048]{1,0:T(8,128)(2,1)} %w_ref.1, bf16[2,128,256]{2,1,0:T(8,128)(2,1)S(1)} %get-tuple-element.59.bt_ref, bf16[2,256,96]{2,1,0:T(8,128)(2,1)S(1)} %get-tuple-element.60.weight3_ref, ...), custom_call_target="tpu_custom_call" | custom-call | tf_op jit(solution)/shard_map/project/pallas_call | solution.py:169
  18.1 1.3 copy-done.1
  20.4 3.3 %collective-permute-done.refs_1_.near_ref = f32[2,72,2048]{2,1,0:T(8,128)} collective-permute-done((f32[2,72,2048]{2,1,0:T(8,128)S(1)}, f32[2,72,2048]{2,1,0:T(8,128)}, u32[]{:S(2)}, u32[]{:S(2)}) %collective-permute-start) | collective-permute-done | bytes 1179680 | tf_op jit(solution)/shard_map/ppermute | solution.py:22
  23.6 2.5 %merge.2 = (bf16[112,2048]{1,0:T(8,128)(2,1)}, bf16[112,2048]{1,0:T(8,128)(2,1)}) custom-call(f32[28]{0:T(128)S(1)} %convert_element_type.3.scalars_ref.refs_6_, f32[2,72,2048]{2,1,0:T(8,128)S(1)} %get-tuple-element.65.refs_0_.after.own_ref.refs_4_, f32[2,72,2048]{2,1,0:T(8,128)} %collective-permute-done.refs_1_.near_ref), custom_call_target="tpu_custom_call" | custom-call | tf_op jit(solution)/shard_map/merge/pallas_call | solution.py:311
  26.1 3.3 %collective-permute-start.2 = (bf16[112,2048]{1,0:T(8,128)(2,1)}, bf16[112,2048]{1,0:T(8,128)(2,1)}, u32[]{:S(2)}, u32[]{:S(2)}) collective-permute-start(bf16[112,2048]{1,0:T(8,128)(2,1)} %get-tuple-element.66.sent), channel_id=1, source_target_pairs={{0,2},{1,3},{2,0},{3,1},{4,6},{5,7},{6,4},{7,5},{8,10},{9,11},{10,... | collective-permute-start | bytes 1376264 | tf_op jit(solution)/shard_map/ppermute | solution.py:22
  29.4 1.5 collective-permute-start.4
  31.0 1.0 copy-done.11
  32.0 1.3 copy-done.7
  33.2 1.2 copy-done.12
  34.5 2.6 %turned.1.left.left_ref = bf16[1024,1024]{1,0:T(8,128)(2,1)S(1)} custom-call(s32[8]{0:T(128)S(1)} %pad_add_fusion.where_ref, bf16[256,2048]{1,0:T(8,128)(2,1)S(1)} %bitcast.12, bf16[256,2048]{1,0:T(8,128)(2,1)S(1)} %bitcast.13, bf16[256,2048]{1,0:T(8,128)(2,1)S(1)} %copy-done.12, bf16[256,2048]{1,0:T(8,128)(2,1)S(1)} %copy-done.12, ...), custom_call_target="tpu_custom_call" | custom-call | tf_op jit(solution)/shard_map/turned/pallas_call | solution.py:636
  37.2 7.9 %inner.1.raw_ref = f32[2,256,2048]{2,1,0:T(8,128)} custom-call(bf16[2,256,2048]{2,1,0:T(8,128)(2,1)S(1)} %copy-done.2, f32[2,256,384]{2,1,0:T(8,128)S(1)} %copy-done.9, f32[2,64,256]{2,1,0:T(8,128)S(1)} %get-tuple-element.64.lines_ref, bf16[112,2048]{1,0:T(8,128)(2,1)} %get-tuple-element.66.sent, bf16[1024,1024]{1,0:T(8,128)(2,1)S(1)} %turned.1.left.left_ref), custom_call_target="tpu_custom_call" | custom-call | tf_op jit(solution)/shard_map/inner/pallas_call | solution.py:234
  45.1 6.6 %collective-permute-done.4.refs_2_ = bf16[112,2048]{1,0:T(8,128)(2,1)} collective-permute-done((bf16[112,2048]{1,0:T(8,128)(2,1)}, bf16[112,2048]{1,0:T(8,128)(2,1)}, u32[]{:S(2)}, u32[]{:S(2)}) %collective-permute-start.4) | collective-permute-done | bytes 458784 | tf_op jit(solution)/shard_map/ppermute | solution.py:22
  51.7 1.4 collective-permute-done.3.refs_1_
  53.0 10.7 %normed.1 = (bf16[256,2048]{1,0:T(8,128)(2,1)}, bf16[2,256,2048]{2,1,0:T(8,128)(2,1)}, f32[2,256,32]{2,1,0:T(8,128)S(1)}, f32[2,64,2048]{2,1,0:T(8,128)S(1)}, f3...) custom-call(f32[2,256,2048]{2,1,0:T(8,128)} %inner.1.raw_ref, ...), custom_call_target="tpu_custom_call" | custom-call | tf_op jit(solution)/shard_map/normed/pallas_call | solution.py:403
  63.8 2.7 %collective-permute-done.5.refs_2_.refs_7_ = f32[2,64,2048]{2,1,0:T(8,128)S(1)} collective-permute-done((f32[2,64,2048]{2,1,0:T(8,128)S(1)}, f32[2,64,2048]{2,1,0:T(8,128)S(1)}, u32[]{:S(2)}, u32[]{:S(2)}) %collective-permute-start.5) | collective-permute-done | bytes 1048608 | tf_op jit(solution)/shard_map/ppermute | solution.py:22
  66.4 0.8 merge.3
  67.2 1.6 collective-permute-start.6
  69.1 1.7 collective-permute-start.7
  70.8 12.1 %inner_back.1 = (f32[2,256,2048]{2,1,0:T(8,128)}, f32[2,256,64]{2,1,0:T(8,128)S(1)}, f32[2,256,64]{2,1,0:T(8,128)S(1)}) custom-call(bf16[2,256,2048]{2,1,0:T(8,128)(2,1)S(1)} %copy-done.2, bf16[2,256,2048]{2,1,0:T(8,128)(2,1)S(1)} %copy-done.13, f32[2,256,384]{2,1,0:T(8,128)S(1)} %copy-done.9, f32[2,64,256]{2,1,0:T(8,128)S(1)} %get-tuple-element.64.lines_ref, ...), custom_call_target="tpu_custom_call" | custom-call | tf_op jit(solution)/shard_map/inner_back/pallas_call | solution.py:490
  82.9 5.7 %finish.2 = (bf16[2,256,1024]{2,1,0:T(8,128)(2,1)}, f32[2,256,64]{2,1,0:T(8,128)S(1)}, f32[2,256,32]{2,1,0:T(8,128)S(1)}, f32[2,1,32]{2,1,0:T(1,128)S(1)}) custom-call(bf16[2,256,2048]{2,1,0:T(8,128)(2,1)} %copy-done.1, f32[2,256,2048]{2,1,0:T(8,128)} %get-tuple-element.74.refs_1_, bf16[2,256,384]{2,1,0:T(8,128)(2,1)S(1)} %copy-done.15, ...), custom_call_target="tpu_custom_call" | custom-call | tf_op jit(solution)/shard_map/finish/pallas_call | solution.py:593
  88.7 7.1 %finish.3 = (bf16[2,256,1184]{2,1,0:T(8,128)(2,1)}, f32[2,256,64]{2,1,0:T(8,128)}, f32[2,256,32]{2,1,0:T(8,128)}, f32[2,1,32]{2,1,0:T(1,128)}) custom-call(bf16[2,256,2048]{2,1,0:T(8,128)(2,1)} %copy-done.1, f32[2,256,2048]{2,1,0:T(8,128)} %get-tuple-element.74.refs_1_, bf16[2,256,384]{2,1,0:T(8,128)(2,1)S(1)} %copy-done.15, ...), custom_call_target="tpu_custom_call" | custom-call | tf_op jit(solution)/shard_map/finish/pallas_call | solution.py:593
  95.8 1.7 copy.15
  98.0 3.4 %collective-permute-done.18 = bf16[512,1184]{0,1:T(8,128)(2,1)} collective-permute-done((bf16[512,1184]{0,1:T(8,128)(2,1)S(1)}, bf16[512,1184]{0,1:T(8,128)(2,1)}, u32[]{:S(2)}, u32[]{:S(2)}) %collective-permute-start.18) | collective-permute-done | bytes 1212448 | tf_op jit(solution)/shard_map/ppermute | solution.py:22
  101.5 1.8 copy.16.peer_ref
  103.3 4.8 %terms.3 = (f32[512,512]{1,0:T(8,128)S(1)}, bf16[512,512]{1,0:T(8,128)(2,1)S(1)}, f32[512,672]{1,0:T(8,128)}, bf16[512,672]{1,0:T(8,128)(2,1)S(1)}) custom-call(bf16[1024,1024]{1,0:T(8,128)(2,1)} %copy-done, bf16[512,1184]{1,0:T(8,128)(2,1)S(1)} %bitcast.15, bf16[512,1184]{1,0:T(8,128)(2,1)S(1)} %copy.16.peer_ref), custom_call_target="tpu_custom_call" | custom-call | tf_op jit(solution)/shard_map/terms/pallas_call | solution.py:678
  108.1 1.0 copy-done.19
  109.1 0.8 copy-done.28
  110.2 1.4 collective-permute-start.20
  111.6 1.5 collective-permute-start.19
  113.1 5.3 %terms.2 = (f32[512,512]{1,0:T(8,128)S(1)}, bf16[512,512]{1,0:T(8,128)(2,1)}, f32[512,512]{1,0:T(8,128)S(1)}, bf16[512,512]{1,0:T(8,128)(2,1)}) custom-call(bf16[1024,1024]{1,0:T(8,128)(2,1)} %copy-done, bf16[512,1024]{1,0:T(8,128)(2,1)} %bitcast.8.own_ref, bf16[512,1024]{1,0:T(8,128)(2,1)} %collective-permute-done.9.peer_ref), custom_call_target="tpu_custom_call" | custom-call | tf_op jit(solution)/shard_map/terms/pallas_call | solution.py:678
  118.4 1.0 copy-done.17
  119.9 0.7 collective-permute-start.11
  120.6 8.0 %collective-permute-done.20 = bf16[512,672]{0,1:T(8,128)(2,1)} collective-permute-done((bf16[512,672]{0,1:T(8,128)(2,1)S(1)}, bf16[512,672]{0,1:T(8,128)(2,1)}, u32[]{:S(2)}, u32[]{:S(2)}) %collective-permute-start.20) | collective-permute-done | bytes 688160 | tf_op jit(solution)/shard_map/ppermute | solution.py:22
  128.6 1.4 copy.18.refs_3_
  130.1 1.3 copy-done.20
  131.4 1.3 fold.12
  132.6 1.6 collective-permute-start.22
  134.2 1.3 collective-permute-start.21
  135.5 2.4 %collective-permute-done.10.refs_1_ = bf16[512,512]{1,0:T(8,128)(2,1)} collective-permute-done((bf16[512,512]{1,0:T(8,128)(2,1)}, bf16[512,512]{1,0:T(8,128)(2,1)}, u32[]{:S(2)}, u32[]{:S(2)}) %collective-permute-start.10) | collective-permute-done | bytes 524320 | tf_op jit(solution)/shard_map/ppermute | solution.py:22
  137.9 2.0 collective-permute-done.11.refs_3_
  139.9 1.4 fold.8
  141.3 1.4 collective-permute-start.12
  142.6 1.5 collective-permute-start.13
  144.1 1.3 collective-permute-done.21.refs_1_
  145.4 0.9 collective-permute-done.22.refs_3_
  146.4 1.6 collective-permute-start.23
  148.0 2.2 %collective-permute-done.12.refs_1_ = bf16[256,512]{1,0:T(8,128)(2,1)S(1)} collective-permute-done((bf16[256,512]{1,0:T(8,128)(2,1)S(1)}, bf16[256,512]{1,0:T(8,128)(2,1)S(1)}, u32[]{:S(2)}, u32[]{:S(2)}) %collective-permute-start.12) | collective-permute-done | bytes 262176 | tf_op jit(solution)/shard_map/ppermute | solution.py:22
  150.2 0.5 collective-permute-done.13.refs_3_
  150.8 1.6 collective-permute-start.14
  152.5 4.5 %collective-permute-done.23.refs_1_ = bf16[128,1184]{1,0:T(8,128)(2,1)S(1)} collective-permute-done((bf16[128,1184]{1,0:T(8,128)(2,1)S(1)}, bf16[128,1184]{1,0:T(8,128)(2,1)S(1)}, u32[]{:S(2)}, u32[]{:S(2)}) %collective-permute-start.23) | collective-permute-done | bytes 303136 | tf_op jit(solution)/shard_map/ppermute | solution.py:22
  157.1 1.6 collective-permute-start.24
  158.7 8.4 %collective-permute-done.24.refs_1_ = bf16[64,1184]{1,0:T(8,128)(2,1)S(1)} collective-permute-done((bf16[64,1184]{1,0:T(8,128)(2,1)S(1)}, bf16[64,1184]{1,0:T(8,128)(2,1)S(1)}, u32[]{:S(2)}, u32[]{:S(2)}) %collective-permute-start.24) | collective-permute-done | bytes 151584 | tf_op jit(solution)/shard_map/ppermute | solution.py:22
  167.2 3.0 %collective-permute-start.15 = (bf16[64,1024]{1,0:T(8,128)(2,1)S(1)}, bf16[64,1024]{1,0:T(8,128)(2,1)S(1)}, u32[]{:S(2)}, u32[]{:S(2)}) collective-permute-start(bf16[64,1024]{1,0:T(8,128)(2,1)S(1)} %get-tuple-element.90), channel_id=1, source_target_pairs={{0,16},{8,24},{16,0},{24,8},{1,17},{9,25},{17,1},{25,9},{2,18},{10... | collective-permute-start | bytes 393224 | tf_op jit(solution)/shard_map/ppermute | solution.py:22
  170.2 8.6 %collective-permute-done.15.refs_1_ = bf16[64,1024]{1,0:T(8,128)(2,1)S(1)} collective-permute-done((bf16[64,1024]{1,0:T(8,128)(2,1)S(1)}, bf16[64,1024]{1,0:T(8,128)(2,1)S(1)}, u32[]{:S(2)}, u32[]{:S(2)}) %collective-permute-start.15) | collective-permute-done | bytes 131104 | tf_op jit(solution)/shard_map/ppermute | solution.py:22
  178.9 2.6 %collective-permute-start.26 = (bf16[128,1184]{1,0:T(8,128)(2,1)S(1)}, bf16[128,1184]{1,0:T(8,128)(2,1)S(1)}, u32[]{:S(2)}, u32[]{:S(2)}) collective-permute-start(bf16[128,1184]{1,0:T(8,128)(2,1)S(1)} %pad_maximum_fusion.refs_2_), channel_id=1, source_target_pairs={{0,8},{8,0},{16,24},{24,16},{1,9},{9,1},{17,25},{25,17},{2,10},{10... | collective-permute-start | bytes 909320 | tf_op jit(solution)/shard_map/ppermute | solution.py:22
  181.6 4.6 %collective-permute-done.16 = bf16[64,1024]{1,0:T(8,128)(2,1)S(1)} collective-permute-done((bf16[64,1024]{1,0:T(8,128)(2,1)S(1)}, bf16[64,1024]{1,0:T(8,128)(2,1)S(1)}, u32[]{:S(2)}, u32[]{:S(2)}) %collective-permute-start.16) | collective-permute-done | bytes 131104 | tf_op jit(solution)/shard_map/ppermute | solution.py:22
  186.3 10.1 %collective-permute-done.17.refs_1_ = bf16[128,1024]{1,0:T(8,128)(2,1)S(1)} collective-permute-done((bf16[128,1024]{1,0:T(8,128)(2,1)S(1)}, bf16[128,1024]{1,0:T(8,128)(2,1)S(1)}, u32[]{:S(2)}, u32[]{:S(2)}) %collective-permute-start.17) | collective-permute-done | bytes 262176 | tf_op jit(solution)/shard_map/ppermute | solution.py:22
  196.3 2.0 %placed.1 = (f32[256,2048]{1,0:T(8,128)}, f32[256,160]{1,0:T(8,128)S(1)}) custom-call(s32[8]{0:T(128)S(1)} %pad_add_fusion.where_ref, bf16[128,1024]{1,0:T(8,128)(2,1)S(1)} %pad_maximum_fusion.1.refs_0_, bf16[128,1024]{1,0:T(8,128)(2,1)S(1)} %collective-permute-done.17.refs_1_, bf16[128,1184]{1,0:T(8,128)(2,1)S(1)} %pad_maximum_fusion.refs_2_, ...), custom_call_target="tpu_custom_call" | custom-call | tf_op jit(solution)/shard_map/placed/pallas_call | solution.py:758
  198.4 0.8 copy.19
  (91 shorter events, 3.4 us)
Async XLA Ops:
  0.6 1.5 copy-start.6
  2.2 0.7 copy-start.25
  2.8 0.7 copy-start.27
  6.1 0.9 copy-start.8
  7.0 11.1 %copy-start.14 = (bf16[2,256,384]{2,1,0:T(8,128)(2,1)}, bf16[2,256,384]{2,1,0:T(8,128)(2,1)S(1)}, u32[]{:S(2)}) copy-start(bf16[2,256,384]{2,1,0:T(8,128)(2,1)S(1)} %get-tuple-element.75.refs_2_) | copy-start | bytes 1179652
  7.0 11.1 %copy-start.22 = (bf16[2,256,384]{2,1,0:T(8,128)(2,1)}, bf16[2,256,384]{2,1,0:T(8,128)(2,1)S(1)}, u32[]{:S(2)}) copy-start(bf16[2,256,384]{2,1,0:T(8,128)(2,1)S(1)} %get-tuple-element.67.cg3_ref) | copy-start | bytes 1179652
  7.0 13.2 %copy-start.30 = (s32[2]{0:T(128)S(1)}, s32[2]{0:T(128)}, u32[]{:S(2)}) copy-start(s32[2]{0:T(128)} %constant.40.clone) | copy-start | bytes 28
  18.1 1.3 copy-start.1
  19.5 17.6 %copy-start.3 = (f32[2,72,2048]{2,1,0:T(8,128)}, f32[2,72,2048]{2,1,0:T(8,128)S(1)}, u32[]{:S(2)}) copy-start(f32[2,72,2048]{2,1,0:T(8,128)S(1)} %get-tuple-element.65.refs_0_.after.own_ref.refs_4_) | copy-start | bytes 3538948
  19.5 11.5 %copy-start.29 = (s32[4]{0:T(128)S(1)}, s32[4]{0:T(128)}, u32[]{:S(2)}) copy-start(s32[4]{0:T(128)} %constant.41.clone) | copy-start | bytes 52
  19.5 4.1 %collective-permute-start = (f32[2,72,2048]{2,1,0:T(8,128)S(1)}, f32[2,72,2048]{2,1,0:T(8,128)}, u32[]{:S(2)}, u32[]{:S(2)}) collective-permute-start(f32[2,72,2048]{2,1,0:T(8,128)S(1)} %get-tuple-element.65.refs_0_.after.own_ref.refs_4_), channel_id=1, source_target_pairs={{0,1},{1,0},{2,3},{3,2},{4,5},{5,4},{6,7},{7,6},{8,9},{9,8},{10,11... | collective-permute-start | bytes 3538952 | tf_op jit(solution)/shard_map/ppermute | solution.py:22
  19.9 11.1 %collective-permute-start.1 = (bf16[256,2048]{1,0:T(8,128)(2,1)S(1)}, bf16[256,2048]{1,0:T(8,128)(2,1)S(1)}, u32[]{:S(2)}, u32[]{:S(2)}) collective-permute-start(bf16[256,2048]{1,0:T(8,128)(2,1)S(1)} %bitcast.11), channel_id=1, source_target_pairs={{0,1},{1,0},{2,3},{3,2},{4,5},{5,4},{6,7},{7,6},{8,9},{9,8},{10,11... | collective-permute-start | bytes 3145736 | tf_op jit(solution)/shard_map/ppermute | solution.py:22
  26.1 18.9 %collective-permute-start.2 = (bf16[112,2048]{1,0:T(8,128)(2,1)}, bf16[112,2048]{1,0:T(8,128)(2,1)}, u32[]{:S(2)}, u32[]{:S(2)}) collective-permute-start(bf16[112,2048]{1,0:T(8,128)(2,1)} %get-tuple-element.66.sent), channel_id=1, source_target_pairs={{0,2},{1,3},{2,0},{3,1},{4,6},{5,7},{6,4},{7,5},{8,10},{9,11},{10,... | collective-permute-start | bytes 1376264 | tf_op jit(solution)/shard_map/ppermute | solution.py:22
  29.4 22.3 %collective-permute-start.4 = (bf16[112,2048]{1,0:T(8,128)(2,1)}, bf16[112,2048]{1,0:T(8,128)(2,1)}, u32[]{:S(2)}, u32[]{:S(2)}) collective-permute-start(bf16[112,2048]{1,0:T(8,128)(2,1)} %get-tuple-element.68), channel_id=1, source_target_pairs={{0,6},{1,7},{2,4},{3,5},{4,2},{5,3},{6,0},{7,1},{8,14},{9,15},{10,... | collective-permute-start | bytes 1376264 | tf_op jit(solution)/shard_map/ppermute | solution.py:22
  30.9 22.1 %collective-permute-start.3 = (bf16[112,2048]{1,0:T(8,128)(2,1)}, bf16[112,2048]{1,0:T(8,128)(2,1)}, u32[]{:S(2)}, u32[]{:S(2)}) collective-permute-start(bf16[112,2048]{1,0:T(8,128)(2,1)} %get-tuple-element.68), channel_id=1, source_target_pairs={{0,4},{1,5},{2,6},{3,7},{4,0},{5,1},{6,2},{7,3},{8,12},{9,13},{10,... | collective-permute-start | bytes 1376264 | tf_op jit(solution)/shard_map/ppermute | solution.py:22
  31.0 6.1 %copy-start.2 = (bf16[2,256,2048]{2,1,0:T(8,128)(2,1)S(1)}, bf16[2,256,2048]{2,1,0:T(8,128)(2,1)}, u32[]{:S(2)}) copy-start(bf16[2,256,2048]{2,1,0:T(8,128)(2,1)} %copy-done.1) | copy-start | bytes 6291460
  31.0 1.0 copy-start.11
  32.0 1.3 copy-start.7
  33.2 1.2 copy-start.12
  34.5 2.7 %copy-start.9 = (f32[2,256,384]{2,1,0:T(8,128)S(1)}, f32[2,256,384]{2,1,0:T(8,128)}, u32[]{:S(2)}) copy-start(f32[2,256,384]{2,1,0:T(8,128)} %copy-done.8) | copy-start | bytes 2359300
  37.1 8.0 %copy-start = (bf16[1024,1024]{1,0:T(8,128)(2,1)}, bf16[1024,1024]{1,0:T(8,128)(2,1)S(1)}, u32[]{:S(2)}) copy-start(bf16[1024,1024]{1,0:T(8,128)(2,1)S(1)} %turned.1.left.left_ref) | copy-start | bytes 6291460
  37.1 15.9 %copy-start.21 = (bf16[1,256,2048]{2,1,0:T(8,128)(2,1)S(1)}, bf16[1,256,2048]{2,1,0:T(8,128)(2,1)}, u32[]{:S(2)}) copy-start(bf16[1,256,2048]{2,1,0:T(8,128)(2,1)} %param.15) | copy-start | bytes 3145732
  37.1 15.9 %copy-start.23 = (bf16[2,256,384]{2,1,0:T(8,128)(2,1)S(1)}, bf16[2,256,384]{2,1,0:T(8,128)(2,1)}, u32[]{:S(2)}) copy-start(bf16[2,256,384]{2,1,0:T(8,128)(2,1)} %copy-done.22) | copy-start | bytes 1179652
  37.2 15.9 %copy-start.24 = (f32[2048]{0:T(1024)S(1)}, f32[2048]{0:T(1024)}, u32[]{:S(2)}) copy-start(f32[2048]{0:T(1024)} %param.14) | copy-start | bytes 24580
  63.7 7.1 %copy-start.13 = (bf16[2,256,2048]{2,1,0:T(8,128)(2,1)S(1)}, bf16[2,256,2048]{2,1,0:T(8,128)(2,1)}, u32[]{:S(2)}) copy-start(bf16[2,256,2048]{2,1,0:T(8,128)(2,1)} %get-tuple-element.70.draw_ref) | copy-start | bytes 6291460
  63.8 2.7 %collective-permute-start.5 = (f32[2,64,2048]{2,1,0:T(8,128)S(1)}, f32[2,64,2048]{2,1,0:T(8,128)S(1)}, u32[]{:S(2)}, u32[]{:S(2)}) collective-permute-start(f32[2,64,2048]{2,1,0:T(8,128)S(1)} %get-tuple-element.72.refs_1_), channel_id=1, source_target_pairs={{0,1},{1,0},{2,3},{3,2},{4,5},{5,4},{6,7},{7,6},{8,9},{9,8},{10,11... | collective-permute-start | bytes 3145736 | tf_op jit(solution)/shard_map/ppermute | solution.py:22
  66.4 16.5 %copy-start.5 = (f32[2,64,2048]{2,1,0:T(8,128)}, f32[2,64,2048]{2,1,0:T(8,128)S(1)}, u32[]{:S(2)}) copy-start(f32[2,64,2048]{2,1,0:T(8,128)S(1)} %collective-permute-done.5.refs_2_.refs_7_) | copy-start | bytes 3145732
  67.2 15.6 %collective-permute-start.6 = (bf16[64,2048]{1,0:T(8,128)(2,1)S(1)}, bf16[64,2048]{1,0:T(8,128)(2,1)S(1)}, u32[]{:S(2)}, u32[]{:S(2)}) collective-permute-start(bf16[64,2048]{1,0:T(8,128)(2,1)S(1)} %get-tuple-element.73.after), channel_id=1, source_target_pairs={{0,2},{1,3},{2,0},{3,1},{4,6},{5,7},{6,4},{7,5},{8,10},{9,11},{10,... | collective-permute-start | bytes 786440 | tf_op jit(solution)/shard_map/ppermute | solution.py:22
  68.8 14.1 %collective-permute-start.8 = (bf16[64,2048]{1,0:T(8,128)(2,1)S(1)}, bf16[64,2048]{1,0:T(8,128)(2,1)S(1)}, u32[]{:S(2)}, u32[]{:S(2)}) collective-permute-start(bf16[64,2048]{1,0:T(8,128)(2,1)S(1)} %get-tuple-element.77), channel_id=1, source_target_pairs={{0,6},{1,7},{2,4},{3,5},{4,2},{5,3},{6,0},{7,1},{8,14},{9,15},{10,... | collective-permute-start | bytes 786440 | tf_op jit(solution)/shard_map/ppermute | solution.py:22
  69.1 13.8 %collective-permute-start.7 = (bf16[64,2048]{1,0:T(8,128)(2,1)S(1)}, bf16[64,2048]{1,0:T(8,128)(2,1)S(1)}, u32[]{:S(2)}, u32[]{:S(2)}) collective-permute-start(bf16[64,2048]{1,0:T(8,128)(2,1)S(1)} %get-tuple-element.77), channel_id=1, source_target_pairs={{0,4},{1,5},{2,6},{3,7},{4,0},{5,1},{6,2},{7,3},{8,12},{9,13},{10,... | collective-permute-start | bytes 786440 | tf_op jit(solution)/shard_map/ppermute | solution.py:22
  70.8 12.1 %copy-start.4 = (f32[2,72,2048]{2,1,0:T(8,128)S(1)}, f32[2,72,2048]{2,1,0:T(8,128)}, u32[]{:S(2)}) copy-start(f32[2,72,2048]{2,1,0:T(8,128)} %copy-done.3) | copy-start | bytes 3538948
  70.8 12.1 %copy-start.15 = (bf16[2,256,384]{2,1,0:T(8,128)(2,1)S(1)}, bf16[2,256,384]{2,1,0:T(8,128)(2,1)}, u32[]{:S(2)}) copy-start(bf16[2,256,384]{2,1,0:T(8,128)(2,1)} %copy-done.14) | copy-start | bytes 1179652
  82.9 5.7 %copy-start.26 = (f32[32]{0:T(128)S(1)}, f32[32]{0:T(128)}, u32[]{:S(2)}) copy-start(f32[32]{0:T(128)} %param.12) | copy-start | bytes 388
  95.8 7.5 %copy-start.10 = (bf16[2,256,1184]{2,1,0:T(8,128)(2,1)S(1)}, bf16[2,256,1184]{2,1,0:T(8,128)(2,1)}, u32[]{:S(2)}) copy-start(bf16[2,256,1184]{2,1,0:T(8,128)(2,1)} %get-tuple-element.98) | copy-start | bytes 3637252
  97.5 4.0 %collective-permute-start.18 = (bf16[512,1184]{0,1:T(8,128)(2,1)S(1)}, bf16[512,1184]{0,1:T(8,128)(2,1)}, u32[]{:S(2)}, u32[]{:S(2)}) collective-permute-start(bf16[512,1184]{0,1:T(8,128)(2,1)S(1)} %copy.15), channel_id=1, source_target_pairs={{0,1},{1,0},{2,3},{3,2},{4,5},{5,4},{6,7},{7,6},{8,9},{9,8},{10,11... | collective-permute-start | bytes 3637256 | tf_op jit(solution)/shard_map/ppermute | solution.py:22
  97.5 15.5 %collective-permute-start.9 = (bf16[512,1024]{1,0:T(8,128)(2,1)}, bf16[512,1024]{1,0:T(8,128)(2,1)}, u32[]{:S(2)}, u32[]{:S(2)}) collective-permute-start(bf16[512,1024]{1,0:T(8,128)(2,1)} %bitcast.8.own_ref), channel_id=1, source_target_pairs={{0,1},{1,0},{2,3},{3,2},{4,5},{5,4},{6,7},{7,6},{8,9},{9,8},{10,11... | collective-permute-start | bytes 3145736 | tf_op jit(solution)/shard_map/ppermute | solution.py:22
  108.1 1.0 copy-start.19
  109.1 0.8 copy-start.28
  110.2 18.4 %collective-permute-start.20 = (bf16[512,672]{0,1:T(8,128)(2,1)S(1)}, bf16[512,672]{0,1:T(8,128)(2,1)}, u32[]{:S(2)}, u32[]{:S(2)}) collective-permute-start(bf16[512,672]{0,1:T(8,128)(2,1)S(1)} %copy.17), channel_id=1, source_target_pairs={{0,4},{1,5},{2,6},{3,7},{4,0},{5,1},{6,2},{7,3},{8,12},{9,13},{10,... | collective-permute-start | bytes 2064392 | tf_op jit(solution)/shard_map/ppermute | solution.py:22
  111.6 18.5 %copy-start.16 = (f32[512,672]{1,0:T(8,128)S(1)}, f32[512,672]{1,0:T(8,128)}, u32[]{:S(2)}) copy-start(f32[512,672]{1,0:T(8,128)} %get-tuple-element.101.refs_2_) | copy-start | bytes 4128772
  111.6 18.5 %collective-permute-start.19 = (bf16[512,512]{1,0:T(8,128)(2,1)}, bf16[512,512]{1,0:T(8,128)(2,1)}, u32[]{:S(2)}, u32[]{:S(2)}) collective-permute-start(bf16[512,512]{1,0:T(8,128)(2,1)} %copy-done.28), channel_id=1, source_target_pairs={{0,2},{1,3},{2,0},{3,1},{4,6},{5,7},{6,4},{7,5},{8,10},{9,11},{10,... | collective-permute-start | bytes 1572872 | tf_op jit(solution)/shard_map/ppermute | solution.py:22
  118.4 1.0 copy-start.17
  119.4 18.5 %collective-permute-start.10 = (bf16[512,512]{1,0:T(8,128)(2,1)}, bf16[512,512]{1,0:T(8,128)(2,1)}, u32[]{:S(2)}, u32[]{:S(2)}) collective-permute-start(bf16[512,512]{1,0:T(8,128)(2,1)} %get-tuple-element.80), channel_id=1, source_target_pairs={{0,2},{1,3},{2,0},{3,1},{4,6},{5,7},{6,4},{7,5},{8,10},{9,11},{10,... | collective-permute-start | bytes 1572872 | tf_op jit(solution)/shard_map/ppermute | solution.py:22
  119.9 20.0 %collective-permute-start.11 = (bf16[512,512]{1,0:T(8,128)(2,1)}, bf16[512,512]{1,0:T(8,128)(2,1)}, u32[]{:S(2)}, u32[]{:S(2)}) collective-permute-start(bf16[512,512]{1,0:T(8,128)(2,1)} %get-tuple-element.82), channel_id=1, source_target_pairs={{0,4},{1,5},{2,6},{3,7},{4,0},{5,1},{6,2},{7,3},{8,12},{9,13},{10,... | collective-permute-start | bytes 1572872 | tf_op jit(solution)/shard_map/ppermute | solution.py:22
  130.0 9.9 %copy-start.18 = (f32[512,512]{1,0:T(8,128)S(1)}, f32[512,512]{1,0:T(8,128)}, u32[]{:S(2)}) copy-start(f32[512,512]{1,0:T(8,128)} %copy-done.17) | copy-start | bytes 3145732
  130.0 1.3 copy-start.20
  132.6 13.6 %collective-permute-start.22 = (bf16[256,672]{1,0:T(8,128)(2,1)S(1)}, bf16[256,672]{1,0:T(8,128)(2,1)S(1)}, u32[]{:S(2)}, u32[]{:S(2)}) collective-permute-start(bf16[256,672]{1,0:T(8,128)(2,1)S(1)} %get-tuple-element.106), channel_id=1, source_target_pairs={{0,2},{1,3},{2,0},{3,1},{4,6},{5,7},{6,4},{7,5},{8,10},{9,11},{10,... | collective-permute-start | bytes 1032200 | tf_op jit(solution)/shard_map/ppermute | solution.py:22
  134.2 11.2 %collective-permute-start.21 = (bf16[256,512]{1,0:T(8,128)(2,1)S(1)}, bf16[256,512]{1,0:T(8,128)(2,1)S(1)}, u32[]{:S(2)}, u32[]{:S(2)}) collective-permute-start(bf16[256,512]{1,0:T(8,128)(2,1)S(1)} %get-tuple-element.104), channel_id=1, source_target_pairs={{0,4},{1,5},{2,6},{3,7},{4,0},{5,1},{6,2},{7,3},{8,12},{9,13},{10,... | collective-permute-start | bytes 786440 | tf_op jit(solution)/shard_map/ppermute | solution.py:22
  141.3 9.0 %collective-permute-start.12 = (bf16[256,512]{1,0:T(8,128)(2,1)S(1)}, bf16[256,512]{1,0:T(8,128)(2,1)S(1)}, u32[]{:S(2)}, u32[]{:S(2)}) collective-permute-start(bf16[256,512]{1,0:T(8,128)(2,1)S(1)} %get-tuple-element.84), channel_id=1, source_target_pairs={{0,4},{1,5},{2,6},{3,7},{4,0},{5,1},{6,2},{7,3},{8,12},{9,13},{10,... | collective-permute-start | bytes 786440 | tf_op jit(solution)/shard_map/ppermute | solution.py:22
  142.6 8.1 %collective-permute-start.13 = (bf16[256,512]{1,0:T(8,128)(2,1)S(1)}, bf16[256,512]{1,0:T(8,128)(2,1)S(1)}, u32[]{:S(2)}, u32[]{:S(2)}) collective-permute-start(bf16[256,512]{1,0:T(8,128)(2,1)S(1)} %get-tuple-element.86), channel_id=1, source_target_pairs={{0,2},{1,3},{2,0},{3,1},{4,6},{5,7},{6,4},{7,5},{8,10},{9,11},{10,... | collective-permute-start | bytes 786440 | tf_op jit(solution)/shard_map/ppermute | solution.py:22
  146.4 10.7 %collective-permute-start.23 = (bf16[128,1184]{1,0:T(8,128)(2,1)S(1)}, bf16[128,1184]{1,0:T(8,128)(2,1)S(1)}, u32[]{:S(2)}, u32[]{:S(2)}) collective-permute-start(bf16[128,1184]{1,0:T(8,128)(2,1)S(1)} %get-tuple-element.108), channel_id=1, source_target_pairs={{0,8},{8,0},{16,24},{24,16},{1,9},{9,1},{17,25},{25,17},{2,10},{10... | collective-permute-start | bytes 909320 | tf_op jit(solution)/shard_map/ppermute | solution.py:22
  150.8 16.3 %collective-permute-start.14 = (bf16[128,1024]{1,0:T(8,128)(2,1)S(1)}, bf16[128,1024]{1,0:T(8,128)(2,1)S(1)}, u32[]{:S(2)}, u32[]{:S(2)}) collective-permute-start(bf16[128,1024]{1,0:T(8,128)(2,1)S(1)} %get-tuple-element.88), channel_id=1, source_target_pairs={{0,8},{8,0},{16,24},{24,16},{1,9},{9,1},{17,25},{25,17},{2,10},{10... | collective-permute-start | bytes 786440 | tf_op jit(solution)/shard_map/ppermute | solution.py:22
  157.1 10.0 %collective-permute-start.24 = (bf16[64,1184]{1,0:T(8,128)(2,1)S(1)}, bf16[64,1184]{1,0:T(8,128)(2,1)S(1)}, u32[]{:S(2)}, u32[]{:S(2)}) collective-permute-start(bf16[64,1184]{1,0:T(8,128)(2,1)S(1)} %get-tuple-element.110), channel_id=1, source_target_pairs={{0,16},{8,24},{16,0},{24,8},{1,17},{9,25},{17,1},{25,9},{2,18},{10... | collective-permute-start | bytes 454664 | tf_op jit(solution)/shard_map/ppermute | solution.py:22
  167.1 11.8 %collective-permute-start.25 = (bf16[64,1184]{1,0:T(8,128)(2,1)S(1)}, bf16[64,1184]{1,0:T(8,128)(2,1)S(1)}, u32[]{:S(2)}, u32[]{:S(2)}) collective-permute-start(bf16[64,1184]{1,0:T(8,128)(2,1)S(1)} %fold.15), channel_id=1, source_target_pairs={{0,16},{8,24},{16,0},{24,8},{1,17},{9,25},{17,1},{25,9},{2,18},{10... | collective-permute-start | bytes 454664 | tf_op jit(solution)/shard_map/ppermute | solution.py:22
  167.2 11.6 %collective-permute-start.15 = (bf16[64,1024]{1,0:T(8,128)(2,1)S(1)}, bf16[64,1024]{1,0:T(8,128)(2,1)S(1)}, u32[]{:S(2)}, u32[]{:S(2)}) collective-permute-start(bf16[64,1024]{1,0:T(8,128)(2,1)S(1)} %get-tuple-element.90), channel_id=1, source_target_pairs={{0,16},{8,24},{16,0},{24,8},{1,17},{9,25},{17,1},{25,9},{2,18},{10... | collective-permute-start | bytes 393224 | tf_op jit(solution)/shard_map/ppermute | solution.py:22
  178.8 7.4 %collective-permute-start.16 = (bf16[64,1024]{1,0:T(8,128)(2,1)S(1)}, bf16[64,1024]{1,0:T(8,128)(2,1)S(1)}, u32[]{:S(2)}, u32[]{:S(2)}) collective-permute-start(bf16[64,1024]{1,0:T(8,128)(2,1)S(1)} %fold.11), channel_id=1, source_target_pairs={{0,16},{8,24},{16,0},{24,8},{1,17},{9,25},{17,1},{25,9},{2,18},{10... | collective-permute-start | bytes 393224 | tf_op jit(solution)/shard_map/ppermute | solution.py:22
  178.9 17.4 %collective-permute-start.26 = (bf16[128,1184]{1,0:T(8,128)(2,1)S(1)}, bf16[128,1184]{1,0:T(8,128)(2,1)S(1)}, u32[]{:S(2)}, u32[]{:S(2)}) collective-permute-start(bf16[128,1184]{1,0:T(8,128)(2,1)S(1)} %pad_maximum_fusion.refs_2_), channel_id=1, source_target_pairs={{0,8},{8,0},{16,24},{24,16},{1,9},{9,1},{17,25},{25,17},{2,10},{10... | collective-permute-start | bytes 909320 | tf_op jit(solution)/shard_map/ppermute | solution.py:22
  186.2 10.1 %collective-permute-start.17 = (bf16[128,1024]{1,0:T(8,128)(2,1)S(1)}, bf16[128,1024]{1,0:T(8,128)(2,1)S(1)}, u32[]{:S(2)}, u32[]{:S(2)}) collective-permute-start(bf16[128,1024]{1,0:T(8,128)(2,1)S(1)} %pad_maximum_fusion.1.refs_0_), channel_id=1, source_target_pairs={{0,8},{8,0},{16,24},{24,16},{1,9},{9,1},{17,25},{25,17},{2,10},{10... | collective-permute-start | bytes 786440 | tf_op jit(solution)/shard_map/ppermute | solution.py:22

commit v2 on v1

--- a/solution.py
+++ b/solution.py
@@ -194,7 +194,7 @@
     return jnp.where(lane == k, a.astype(F32), 0.0).astype(BF)
 
 
-def inner_kernel(x_ref, nat_ref, lines_ref, sent, left, raw_ref, score):
+def inner_kernel(branch, x_ref, nat_ref, lines_ref, after, raw_ref, score):
     at = pl.program_id(0)
     rows = x_ref.shape[1]
     heads = lines_ref.shape[1] // 2
@@ -204,43 +204,45 @@
 
     @pl.when(at == 0)
     def _():
-        for branch in range(2):
-            b, c = nat_ref[branch, :, :STATE], nat_ref[branch, :, STATE : 2 * STATE]
-            full = exact(c, b, 1, 1)
-            score[branch] = jnp.where(ordered(rows, branch), full, 0.0)
-
-    for branch in range(2):
-        alone, later = (0, half) if branch == 0 else (half, 0)
-        columns = pltpu.roll(nat_ref[branch, :, CUM:STEP], -(at * per) % LANES, 1)
-        tops, bottoms = 0.0, 0.0
-        for k in range(per):
-            line = lines_ref[branch, pl.ds(at * per + k, 1), :]
-            step = lines_ref[branch, pl.ds(heads + at * per + k, 1), :]
-            xk = own_lanes(x_ref[branch], k, size)
-            own = pl.ds(alone, half)
-            gap = jnp.minimum(columns[alone : alone + half, k : k + 1] - line[:, alone : alone + half], 0.0)
-            m = jnp.exp(gap) * score[branch, own, own] * step[:, alone : alone + half]
-            tops = tops + mm(m.astype(BF), xk[alone : alone + half])
-            gap = jnp.minimum(columns[later : later + half, k : k + 1] - line, 0.0)
-            m = jnp.exp(gap) * score[branch, pl.ds(later, half), :] * step
-            bottoms = bottoms + mm(m.astype(BF), xk)
-        raw_ref[branch, pl.ds(alone, half), :] = tops
-        raw_ref[branch, pl.ds(later, half), :] = bottoms
-
-
-def inner(x, nat, lines, sent, left):
+        b, c = nat_ref[0, :, :STATE], nat_ref[0, :, STATE : 2 * STATE]
+        score[...] = jnp.where(ordered(rows, branch), exact(c, b, 1, 1), 0.0)
+
+    alone, later = (0, half) if branch == 0 else (half, 0)
+    columns = pltpu.roll(nat_ref[0, :, CUM:STEP], -(at * per) % LANES, 1)
+    tops, bottoms = 0.0, 0.0
+    for k in range(per):
+        line = lines_ref[0, pl.ds(at * per + k, 1), :]
+        step = lines_ref[0, pl.ds(heads + at * per + k, 1), :]
+        xk = own_lanes(x_ref[0], k, size)
+        own = pl.ds(alone, half)
+        gap = columns[alone : alone + half, k : k + 1] - line[:, alone : alone + half]
+        m = jnp.exp(jnp.minimum(gap, 0.0)) * score[own, own] * step[:, alone : alone + half]
+        tops = tops + mm(m.astype(BF), xk[alone : alone + half])
+        gap = columns[later : later + half, k : k + 1] - line
+        m = jnp.exp(jnp.minimum(gap, 0.0)) * score[pl.ds(later, half), :] * step
+        bottoms = bottoms + mm(m.astype(BF), xk)
+    raw_ref[pl.ds(alone, half), :] = tops
+    raw_ref[pl.ds(later, half), :] = bottoms
+
+
+def inner(branch, x, nat, lines, after):
     _, rows, channels = x.shape
-    block = pl.BlockSpec((2, rows, GROUP), lambda j: (0, 0, j))
+    one = lambda a: pl.BlockSpec((1, *a.shape[1:]), lambda j: (branch, 0, 0))
     return pl.pallas_call(
-        inner_kernel,
+        functools.partial(inner_kernel, branch),
         grid=(channels // GROUP,),
-        in_specs=[block, whole(nat), whole(lines), ORDER, ORDER],
-        out_specs=block,
-        out_shape=jax.ShapeDtypeStruct(x.shape, F32),
-        scratch_shapes=[pltpu.VMEM((2, rows, rows), F32)],
+        in_specs=[
+            pl.BlockSpec((1, rows, GROUP), lambda j: (branch, 0, j)),
+            one(nat),
+            one(lines),
+            ORDER,
+        ],
+        out_specs=pl.BlockSpec((rows, GROUP), lambda j: (0, j)),
+        out_shape=jax.ShapeDtypeStruct((rows, channels), F32),
+        scratch_shapes=[pltpu.VMEM((rows, rows), F32)],
         compiler_params=PARAMS,
         name="inner",
-    )(x, nat, lines, sent, left)
+    )(x, nat, lines, after)
 
 
 class Scalars:
@@ -273,7 +275,7 @@
         return self.ref[2 + len(self.bits) + 2 * most + (slot * most + m) * most + k]
 
 
-def merge_kernel(chips, turned, scalars_ref, *refs):
+def merge_kernel(chips, turned, scalars_ref, after, *refs):
     scalars = Scalars(chips, scalars_ref)
     if turned:
         tots_ref, own_ref, near_ref, *outs = refs
@@ -294,27 +296,27 @@
         up = scalars.up(n)
         out[:STATE] = (up * sums[0] + (1.0 - up) * sums[1]).astype(BF)
         if not turned:
-            extra = jnp.concatenate(tots + [jnp.zeros((6, tots[0].shape[1]), F32)], axis=0)
-            high, rest = split(extra)
-            middle, low = split(extra - high.astype(F32))
-            for k, part in enumerate((high, middle, low)):
-                out[STATE + 16 * k : STATE + 16 * (k + 1)] = jnp.concatenate(
-                    [part, jnp.zeros_like(part)], axis=0
-                )
-
-
-def merge(chips, scalars, own, near, tots=None):
+            rows = []
+            for tot in tots:
+                high, rest = split(tot)
+                middle, low = split(tot - high.astype(F32))
+                rows += [part.astype(F32) for part in (high, middle, low)]
+            rows.append(jnp.zeros((16 - len(rows), rows[0].shape[1]), F32))
+            out[STATE:] = jnp.concatenate(rows, axis=0).astype(BF)
+
+
+def merge(chips, scalars, after, own, near, tots=None):
     channels = own.shape[2]
-    rows = STATE if tots is not None else STATE + 48
+    rows = STATE if tots is not None else STATE + 16
     given = [own, near] if tots is None else [tots, own, near]
     bits = bits_of(chips)
     return pl.pallas_call(
         functools.partial(merge_kernel, chips, tots is not None),
-        in_specs=[SCALARS] + [pl.BlockSpec(memory_space=pltpu.VMEM)] * len(given),
+        in_specs=[SCALARS, ORDER] + [pl.BlockSpec(memory_space=pltpu.VMEM)] * len(given),
         out_shape=[jax.ShapeDtypeStruct((rows, channels), BF) for _ in bits],
         compiler_params=PARAMS,
         name="merge",
-    )(scalars, *given)
+    )(scalars, after, *given)
 
 
 def exchange(chips, sums):
@@ -337,11 +339,14 @@
 TILE = 128
 
 
-def normed_kernel(count, heads, raw_ref, cg3_ref, gain_ref, cot_ref, scalars_ref, own_ref, near_ref, *refs):
+def normed_kernel(
+    count, heads, raw_fwd_ref, raw_rc_ref, cg3_ref, gain_ref, cot_ref, scalars_ref,
+    x_fwd_ref, x_rc_ref, nat_fwd_ref, nat_rc_ref, own_ref, near_ref, *refs,
+):
     arrived, refs = refs[:count], refs[count:]
-    mixed_ref, draw_ref, ry_ref, adj_ref, dc_ref, s_ref, tots_ref, s3 = refs
+    mixed_ref, draw_ref, ry_ref, adj_ref, dc_ref, s_ref, tots_ref, start_ref, s3 = refs
     at = pl.program_id(0)
-    channels = raw_ref.shape[2]
+    channels = raw_fwd_ref.shape[1]
     copier = spread(heads, channels, None, 3)
 
     @pl.when(at == 0)
@@ -349,9 +354,8 @@
         rows = [own_ref[0, :1], own_ref[1, :1]]
         rows += [near_ref[0, STATE : STATE + 1], near_ref[1, STATE : STATE + 1]]
         for ref in arrived:
-            parts = [ref[STATE + 16 * k : STATE + 16 * (k + 1)].astype(F32) for k in range(3)]
-            both = parts[0] + parts[1] + parts[2]
-            rows += [both[:1], both[1:2]]
+            parts = ref[STATE:].astype(F32)
+            rows += [parts[n : n + 1] + parts[n + 1 : n + 2] + parts[n + 2 : n + 3] for n in (0, 3)]
         fill = tots_ref.shape[0] - len(rows)
         tots_ref[...] = jnp.concatenate(rows + [jnp.zeros((fill, channels), F32)], axis=0)
 
@@ -372,7 +376,8 @@
     for branch in range(2):
         c3 = cg3_ref[branch, :, : 3 * STATE]
         grow = mm(cg3_ref[branch, :, 3 * STATE : 3 * STATE + 3 * heads], copier)
-        r = raw_ref[branch] + grow * mm(c3, s3[branch])
+        raw_ref = raw_fwd_ref if branch == 0 else raw_rc_ref
+        r = raw_ref[...] + grow * mm(c3, s3[branch])
         scale = lax.rsqrt(jnp.sum(r * r, axis=1, keepdims=True) * (1.0 / channels) + 1e-05)
         n = r * scale
         ys.append(n * gain_ref[...])
@@ -381,6 +386,19 @@
         mean = jnp.sum(dz * n, axis=1, keepdims=True) * (1.0 / channels)
         draw = scale * (dz - n * mean)
         draw_ref[branch] = draw.astype(BF)
+
+        x_ref, nat_ref = ((x_fwd_ref, nat_fwd_ref), (x_rc_ref, nat_rc_ref))[branch]
+        row, edge = (0, 0) if branch == 0 else (TILE - 1, x_ref.shape[1] - 1)
+
+        @pl.when(at == (0 if branch == 0 else pl.num_programs(0) - 1))
+        def _(branch=branch, x_ref=x_ref, nat_ref=nat_ref, row=row, edge=edge, scale=scale, dz=dz):
+            step = mm(split_three(nat_ref[0, :, STEP : STEP + heads], 1), copier)
+            step = step[0:1] if branch == 0 else step[7:8]
+            x = x_ref[0].astype(F32)[edge : edge + 1]
+            total = jnp.sum(step * x * dz[row : row + 1], axis=1, keepdims=True)
+            value = 1e-05 * scale[row : row + 1] ** 3 * total
+            start_ref[branch] = jnp.broadcast_to(value, start_ref.shape[1:])
+
         high, low = split(draw * r)
         ry_ref[branch] = mm(high, one, 1, 1) + mm(low, one, 1, 1)
         grown = (grow * draw).astype(BF)
@@ -392,8 +410,8 @@
     mixed_ref[...] = (ys[0] + back.astype(F32)).astype(BF)
 
 
-def normed(raw, cg3, gain, cot, scalars, ends, near, arrived):
-    _, rows, channels = raw.shape
+def normed(raws, x, nat, cg3, gain, cot, scalars, ends, near, arrived):
+    rows, channels = raws[0].shape
     heads = (cg3.shape[2] - 3 * STATE) // 6
     band = lambda n: pl.BlockSpec((2, TILE, n), lambda j: (0, j, 0))
     flat = pl.BlockSpec((TILE, channels), lambda j: (j, 0))
@@ -403,11 +421,20 @@
     return pl.pallas_call(
         functools.partial(normed_kernel, len(arrived), heads),
         grid=(rows // TILE,),
-        in_specs=[band(channels), band(cg3.shape[2]), whole(gain), flat, SCALARS]
-        + [pl.BlockSpec((2, 8, channels), lambda j: (0, STATE // 8, 0))]
+        in_specs=[flat, flat, band(cg3.shape[2]), whole(gain), flat, SCALARS]
+        + [
+            pl.BlockSpec((1, 16, channels), lambda j: (0, 0, 0)),
+            pl.BlockSpec((1, 16, channels), lambda j: (1, rows // 16 - 1, 0)),
+            pl.BlockSpec((1, 8, nat.shape[2]), lambda j: (0, 0, 0)),
+            pl.BlockSpec((1, 8, nat.shape[2]), lambda j: (1, rows // 8 - 1, 0)),
+            pl.BlockSpec((2, 8, channels), lambda j: (0, STATE // 8, 0)),
+        ]
         + [whole(a) for a in (near, *arrived)],
         out_specs=[flat, band(channels), band(heads), state, band(STATE), state]
-        + [pl.BlockSpec((tots, channels), lambda j: (0, 0))],
+        + [
+            pl.BlockSpec((tots, channels), lambda j: (0, 0)),
+            pl.BlockSpec((2, 8, LANES), lambda j: (0, 0, 0)),
+        ],
         out_shape=[
             jax.ShapeDtypeStruct((rows, channels), BF),
             jax.ShapeDtypeStruct((2, rows, channels), BF),
@@ -416,15 +443,16 @@
             jax.ShapeDtypeStruct((2, rows, STATE), F32),
             jax.ShapeDtypeStruct((2, STATE, channels), F32),
             jax.ShapeDtypeStruct((tots, channels), F32),
+            jax.ShapeDtypeStruct((2, 8, LANES), F32),
         ],
         scratch_shapes=[pltpu.VMEM((2, 3 * STATE, channels), BF)],
         compiler_params=PARAMS,
         name="normed",
-    )(raw, cg3, gain, cot, scalars, ends, near, *arrived)
+    )(*raws, cg3, gain, cot, scalars, x, x, nat, nat, ends, near, *arrived)
 
 
 def inner_back_kernel(
-    x_ref, draw_ref, nat_ref, lines_ref, after, u_ref, db_ref, dc_ref, score, ds_all, ds_own,
+    x_ref, draw_ref, nat_ref, lines_ref, start_ref, edges_ref, after, u_ref, db_ref, dc_ref, score, ds_all, ds_own,
 ):
     at = pl.program_id(0)
     rows = x_ref.shape[1]
@@ -473,7 +501,10 @@
             alone, first = (half, 0) if branch == 0 else (0, half)
             place, column = iota((half, rows), 0) + first, iota((half, rows), 1)
             seen = (place <= column) if branch == 0 else (place >= column)
-            all_part = jnp.where(seen, ds_all[branch], 0.0)
+            corner = 0 if branch == 0 else rows - 1
+            corner = (place == corner) & (column == corner) & (edges_ref[branch] > 0)
+            all_part = jnp.where(corner, start_ref[branch, :1, :1], ds_all[branch])
+            all_part = jnp.where(seen, all_part, 0.0)
             own_part = jnp.where(ordered(half, 1 - branch), ds_own[branch], 0.0)
             b, c = nat_ref[branch, :, :STATE], nat_ref[branch, :, STATE : 2 * STATE]
             db_ref[branch, pl.ds(first, half), :] = exact(all_part, c)
@@ -484,13 +515,13 @@
             dc_ref[branch, pl.ds(alone, half), :] = dc_own
 
 
-def inner_back(x, draw, nat, lines, after):
+def inner_back(x, draw, nat, lines, starts, edges, after):
     _, rows, channels = x.shape
     block = pl.BlockSpec((2, rows, GROUP), lambda j: (0, 0, j))
     return pl.pallas_call(
         inner_back_kernel,
         grid=(channels // GROUP,),
-        in_specs=[block, block, whole(nat), whole(lines), ORDER],
+        in_specs=[block, block, whole(nat), whole(lines), whole(starts), SCALARS, ORDER],
         out_specs=[block] + [pl.BlockSpec((2, rows, STATE), lambda j: (0, 0, 0))] * 2,
         out_shape=[
             jax.ShapeDtypeStruct(x.shape, F32),
@@ -504,12 +535,12 @@
         ],
         compiler_params=PARAMS,
         name="inner_back",
-    )(x, draw, nat, lines, after)
+    )(x, draw, nat, lines, starts, edges, after)
 
 
 def finish_kernel(first, count, last, heads, channels, *refs):
     x_ref, u_ref, bf3_ref, s_ref, end_ref, tots_ref, scalars_ref, near_ref, *refs = refs
-    arrived, refs = refs[:count], refs[count:]
+    arrived, refs = refs[:count], refs[count + 1 :]
     if last:
         nat_ref, db_ref, dc_ref, dc0_ref, ry_ref, rate_ref, *refs = refs
         before, refs = refs[: len(refs) - 4], refs[len(refs) - 4 :]
@@ -519,6 +550,7 @@
     one = spread(heads, channels, start, 1)
     copier = spread(heads, channels, start, 3)
     columns = pl.ds(pl.multiple_of(at * GROUP, GROUP), GROUP)
+    rows = x_ref.shape[1]
 
     def per_head(a):
         high, low = split(a)
@@ -543,10 +575,11 @@
         both = u_ref[branch] + fade * us
         xf = x_ref[branch].astype(F32)
         dx = (step * both).astype(BF)
+        band = slice(branch * rows, (branch + 1) * rows)
         if last:
-            out_ref[branch, :, columns] = dx
+            out_ref[band, columns] = dx
         else:
-            out_ref[branch] = dx
+            out_ref[band] = dx
         direct_ref[branch] += per_head(xf * both)
         weighted = (fade * step * xf).astype(BF)
         sums = mm(weighted, jnp.concatenate([g_high, g_low], axis=0), 1, 1)
@@ -562,7 +595,7 @@
 
         @pl.when(at == pl.num_programs(0) - 1)
         def _():
-            rows, width = direct_ref.shape[1], out_ref.shape[2] - 2 * STATE - heads
+            width = out_ref.shape[1] - GROUP
             for branch in range(2):
                 dbs, direct, dtot = dbs_ref[branch], direct_ref[branch], dtot_ref[branch]
                 for n in range(0, len(before), 3):
@@ -574,39 +607,40 @@
                 dcum = ry_ref[branch] - step * direct
                 dla = exact(ordered(rows, 1 - branch).astype(F32), dcum) + dtot
                 dpre = (direct - jnp.exp(rate_ref[...]) * dla) * jax.nn.sigmoid(pre)
-                small = [db_ref[branch] + dbs, dc_ref[branch] + dc0_ref[branch], dpre]
-                out_ref[branch, :, width:] = jnp.concatenate(small, axis=1).astype(BF)
-
-
-def finish(piece, pieces, x, u, bf3, s_in, ends, tots, scalars, near, arrived, more, before):
+                fill = jnp.zeros((rows, GROUP - 2 * STATE - heads), F32)
+                small = [db_ref[branch] + dbs, dc_ref[branch] + dc0_ref[branch], dpre, fill]
+                small = jnp.concatenate(small, axis=1).astype(BF)
+                out_ref[branch * rows : (branch + 1) * rows, width:] = small
+
+
+def finish(first, groups, x, u, bf3, s_in, ends, tots, scalars, near, arrived, after, more, before):
     _, rows, channels = x.shape
     heads = (bf3.shape[2] - 3 * STATE) // 6
-    last = piece == pieces - 1
-    groups = channels // GROUP // pieces
-    first = piece * groups
+    last = (first + groups) * GROUP == channels
     block = pl.BlockSpec((2, rows, GROUP), lambda j: (0, 0, first + j))
     state = pl.BlockSpec((2, STATE, GROUP), lambda j: (0, 0, first + j))
     flat = lambda n: pl.BlockSpec((n, GROUP), lambda j: (0, first + j))
     extra = [*more, *before] if last else []
-    width = groups * GROUP + (2 * STATE + heads if last else 0)
+    width = (groups + 1 if last else groups) * GROUP
     sums = [(2, rows, STATE), (2, rows, heads), (2, 1, heads)]
     return pl.pallas_call(
         functools.partial(finish_kernel, first, len(arrived), last, heads, channels),
         grid=(groups,),
         in_specs=[block, block, whole(bf3), state, state, flat(tots.shape[0]), SCALARS, state]
         + [flat(STATE)] * len(arrived)
+        + [ORDER]
         + [whole(a) for a in extra],
         out_specs=[
-            pl.BlockSpec((2, rows, width), lambda j: (0, 0, 0))
+            pl.BlockSpec((2 * rows, width), lambda j: (0, 0))
             if last
-            else pl.BlockSpec((2, rows, GROUP), lambda j: (0, 0, j))
+            else pl.BlockSpec((2 * rows, GROUP), lambda j: (0, j))
         ]
         + [pl.BlockSpec(shape, lambda j: (0, 0, 0)) for shape in sums],
-        out_shape=[jax.ShapeDtypeStruct((2, rows, width), BF)]
+        out_shape=[jax.ShapeDtypeStruct((2 * rows, width), BF)]
         + [jax.ShapeDtypeStruct(shape, F32) for shape in sums],
         compiler_params=PARAMS,
         name="finish",
-    )(x, u, bf3, s_in, ends, tots, scalars, near, *arrived, *extra)
+    )(x, u, bf3, s_in, ends, tots, scalars, near, *arrived, after, *extra)
 
 
 def turned_kernel(
@@ -656,83 +690,113 @@
     return [1 << k for k in range(size.bit_length() - 1)]
 
 
-def term_kernel(orders, cuts, left_ref, own_ref, peer_ref, *outs):
+def tile(rows, start=0, count=None):
+    if count is None:
+        return pl.BlockSpec((rows, GROUP), lambda j: (0, j))
+    return pl.BlockSpec((rows, GROUP), lambda j: (0, jnp.clip(j - start, 0, count - 1)))
+
+
+def spans(widths):
+    counts = [width // GROUP for width in widths]
+    return [(sum(counts[:n]), count) for n, count in enumerate(counts)]
+
+
+def in_span(span):
+    at = pl.program_id(0)
+    return (at >= span[0]) & (at < span[0] + span[1])
+
+
+def term_kernel(picked, pieces, left_ref, own_ref, peer_ref, after, *outs):
     depth = own_ref.shape[0]
-    wide = left_ref.shape[0] // len(orders[0])
-    for part, (order, (low, high)) in enumerate(zip(orders, cuts)):
-        stay_ref, go_ref = outs[2 * part : 2 * part + 2]
-        half = len(order) // 2
-        for n, block in enumerate(order):
-            left = left_ref[block * wide : (block + 1) * wide]
-            term = mm(left[:, :depth], own_ref[:, low:high])
-            term = term + mm(left[:, depth:], peer_ref[:, low:high])
-            if n < half:
-                stay_ref[n * wide : (n + 1) * wide] = term
+    for out, blocks, span in zip(outs, picked, pieces):
+
+        @pl.when(in_span(span))
+        def _(out=out, blocks=blocks):
+            wide = out.shape[0] // len(blocks)
+            for n, block in enumerate(blocks):
+                left = left_ref[block * wide : (block + 1) * wide]
+                term = mm(left[:, :depth], own_ref[...]) + mm(left[:, depth:], peer_ref[...])
+                out[n * wide : (n + 1) * wide] = term.astype(out.dtype)
+
+
+def weight_terms(left, own, peer, picked, widths, kind, after):
+    rows, pieces = left.shape[0] // 2, spans(widths)
+    return pl.pallas_call(
+        functools.partial(term_kernel, picked, pieces),
+        grid=(own.shape[1] // GROUP,),
+        in_specs=[whole(left), tile(own.shape[0]), tile(own.shape[0]), ORDER],
+        out_specs=[tile(rows, *span) for span in pieces],
+        out_shape=[jax.ShapeDtypeStruct((rows, width), kind) for width in widths],
+        compiler_params=PARAMS,
+        name="terms",
+    )(left, own, peer, after)
+
+
+def fold_kernel(pieces, join, final, after, *refs):
+    given, outs = refs[: 2 * len(pieces)], refs[2 * len(pieces) :]
+    for n, span in enumerate(pieces):
+        stay_ref, got_ref = given[2 * n : 2 * n + 2]
+        mine = outs if join else outs[2 * n : 2 * n + 2]
+
+        @pl.when(in_span(span))
+        def _(stay_ref=stay_ref, got_ref=got_ref, mine=mine):
+            total = stay_ref[...] + got_ref[...].astype(F32)
+            if final:
+                mine[0][...] = total.astype(BF)
             else:
-                go_ref[(n - half) * wide : (n - half + 1) * wide] = term.astype(BF)
-
-
-def weight_terms(left, own, peer, orders, cuts):
-    rows = left.shape[0] // 2
-    shape = lambda cut, kind: jax.ShapeDtypeStruct((rows, cut[1] - cut[0]), kind)
+                rows = stay_ref.shape[0] // 2
+                mine[0][...] = total[:rows]
+                mine[1][...] = total[rows:].astype(BF)
+
+
+def fold(parts, turn, join=False, final=False):
+    height = parts[0][0].shape[0]
+    rows = height if final else height // 2
+    widths = [stay.shape[1] for stay, _ in parts]
+    pieces = spans(widths)
+    kinds = [BF] if final else [F32, BF]
+    total = sum(widths)
     outs = pl.pallas_call(
-        functools.partial(term_kernel, orders, cuts),
-        out_shape=[shape(cut, kind) for cut in cuts for kind in (F32, BF)],
-        compiler_params=PARAMS,
-        name="terms",
-    )(left, own, peer)
-    return [outs[n : n + 2] for n in range(0, len(outs), 2)]
-
-
-def fold_kernel(count, final, *refs):
-    given, outs = refs[: 2 * count], refs[2 * count :]
-    joined = len(outs) < 2 * count
-    column = 0
-    for n in range(count):
-        stay_ref, got_ref = given[2 * n : 2 * n + 2]
-        rows, width = stay_ref.shape
-        total = stay_ref[...] + got_ref[...].astype(F32)
-        columns = slice(column, column + width)
-        if final:
-            outs[0][:, columns] = total.astype(BF)
-        else:
-            keep, go = outs[:2] if joined else outs[2 * n : 2 * n + 2]
-            keep[:, columns] = total[: rows // 2]
-            go[:, columns] = total[rows // 2 :].astype(BF)
-        column = column + width if joined else 0
-
-
-def fold(parts, join=False, final=False):
-    rows = parts[0][0].shape[0] if final else parts[0][0].shape[0] // 2
-    widths = [stay.shape[1] for stay, _ in parts]
-    widths = [sum(widths)] if join else widths
-    kinds = [BF] if final else [F32, BF]
-    outs = pl.pallas_call(
-        functools.partial(fold_kernel, len(parts), final),
-        out_shape=[jax.ShapeDtypeStruct((rows, w), kind) for w in widths for kind in kinds],
+        functools.partial(fold_kernel, pieces, join, final),
+        grid=(total // GROUP,),
+        in_specs=[ORDER] + [tile(height, *span) for span in pieces for _ in range(2)],
+        out_specs=[tile(rows) for _ in kinds]
+        if join
+        else [tile(rows, *span) for span in pieces for _ in kinds],
+        out_shape=[
+            jax.ShapeDtypeStruct((rows, width), kind)
+            for width in ([total] if join else widths)
+            for kind in kinds
+        ],
         compiler_params=PARAMS,
         name="fold",
-    )(*[a for part in parts for a in part])
+    )(turn[0], *[a for part in parts for a in part])
+    turn[0] = outs[0]
     return outs[0] if final else [outs[n : n + 2] for n in range(0, len(outs), 2)]
 
 
-def summed(parts, orders):
+def summing(stays, came, orders, turn):
     dps = lax.axis_size("dp")
     dp_bits = bits_of(dps)
-    for n in range(len(orders[0])):
-        sent = [send(go, "ctx", 2 * bits[n]) for (_, go), bits in zip(parts, orders)]
-        got = [(stay, came) for (stay, _), came in zip(parts, sent)]
-        parts = fold(got, join=n == len(orders[0]) - 1)
+    for n in range(1, len(orders[0])):
+        parts = fold(list(zip(stays, came)), turn)
+        stays = [stay for stay, _ in parts]
+        came = yield [send(go, "ctx", 2 * bits[n]) for (_, go), bits in zip(parts, orders)]
+    parts = fold(list(zip(stays, came)), turn, join=True)
     for n, bit in enumerate(dp_bits):
         stay, go = parts[0]
-        last = n == len(dp_bits) - 1
-        parts = fold([(stay, send(go, "dp", bit))], join=True, final=last)
-    held, came = parts, None
+        came = yield [send(go, "dp", bit)]
+        parts = fold([(stay, came[0])], turn, join=True, final=n == len(dp_bits) - 1)
+    held, came = parts, []
     for bit in dp_bits[::-1]:
-        if came is not None:
-            held = jnp.concatenate([held, came])
-        came = send(held, "dp", bit)
-    return held, came
+        held = jnp.concatenate([held, *came])
+        came = yield [send(held, "dp", bit)]
+    yield (held, *came)
+
+
+def together(*groups):
+    flat = lax.optimization_barrier([part for group in groups for part in group])
+    return [[flat.pop(0) for _ in group] for group in groups]
 
 
 def place_kernel(chips, where_ref, *refs):
@@ -750,7 +814,7 @@
             grad_x_ref[target, column : column + width] = piece[:, :width]
             column += width
             if piece.shape[1] > width:
-                grad_small_ref[target, :] = piece[:, width:]
+                grad_small_ref[target, :] = piece[:, width : width + grad_small_ref.shape[1]]
 
 
 def placed(chips, where, given, wide, channels, small):
@@ -767,7 +831,9 @@
     )(where, *given)
 
 
-PIECES = 2
+def cut_groups(groups):
+    sizes = [groups // 2, groups - groups // 2]
+    return [(sum(sizes[:n]), size) for n, size in enumerate(sizes)]
 
 
 def shards(hidden, x_weight, state_weight, log_rates, step_bias, out_gain, cotangent):
@@ -785,32 +851,67 @@
     )
     x, ends = project(both, x_weight, bt, weight3, tot3)
     near = send(ends, "ctx", 1)
-    left = turned(h, peer_h, where, chips, ends)
-    sums = merge(chips, scalars, ends, near)
+    raw_fwd = inner(0, x, nat, lines, ends)
+    sums = merge(chips, scalars, raw_fwd, ends, near)
     arrived = exchange(chips, sums)
-    raw = inner(x, nat, lines, sums[0], left)
-    mixed, draw, ry, adj, dc0, s_in, tots = normed(
-        raw, cg3, out_gain, cot, scalars, ends, near, arrived
+    left = turned(h, peer_h, where, chips, sums[0])
+    raw_rc = inner(1, x, nat, lines, left)
+    mixed, draw, ry, adj, dc0, s_in, tots, starts = normed(
+        (raw_fwd, raw_rc), x, nat, cg3, out_gain, cot, scalars, ends, near, arrived
     )
     near = send(adj, "ctx", 1)
-    sums = merge(chips, scalars, adj, near, tots)
+    sums = merge(chips, scalars, adj, adj, near, tots)
     arrived = exchange(chips, sums)
-    u, db, dc = inner_back(x, draw, nat, lines, sums[0])
+    edges = jnp.stack([place == 0, place == 2 * chips - 1]).astype(jnp.int32)
+    u, db, dc = inner_back(x, draw, nat, lines, starts, edges, sums[0])
+
     bits = bits_of(chips)
     orders = [bits[n:] + bits[:n] for n in range(2)]
     blocks = [by_bits(chips, order) for order in orders]
-    done, before = [], []
+    staying, going = [b[: chips // 2] for b in blocks], [b[chips // 2 :] for b in blocks]
     more = [nat, db, dc, dc0, ry, log_rates[None]]
-    for n in range(PIECES):
+    before = []
+
+    def finished(first, groups, after):
         own, *partial = finish(
-            n, PIECES, x, u, bf3, s_in, ends, tots, scalars, near, arrived, more, before
+            first, groups, x, u, bf3, s_in, ends, tots, scalars, near, arrived, after, more, before
         )
-        before = before + partial
-        own = own.reshape(2 * rows, -1)
-        peer = send(own, "ctx", 1)
-        middle = channels // PIECES // 2
-        cuts = [(0, middle), (middle, own.shape[1])]
-        done += summed(weight_terms(left, own, peer, blocks, cuts), orders)
+        before.extend(partial)
+        return own
+
+    def terms(own, peer, size, picked, kind):
+        cuts = [size * GROUP // 2, own.shape[1] - size * GROUP // 2]
+        outs = weight_terms(left, own, peer, picked, cuts, kind, turn[0])
+        turn[0] = outs[0]
+        return outs
+
+    def first_hop(go):
+        return [send(part, "ctx", 2 * order[0]) for part, order in zip(go, orders)]
+
+    (start, size), (start_next, size_next) = cut_groups(channels // GROUP)
+    own = finished(start, size, db)
+    turn = [before[-1]]
+    peer = send(own, "ctx", 1)
+    came = first_hop(terms(own, peer, size, going, BF))
+    own_next = finished(start_next, size_next, turn[0])
+    (own_next,), came = together([own_next], came)
+    turn[0] = own_next
+    peer_next = send(own_next, "ctx", 1)
+    ahead = summing(terms(own, peer, size, staying, F32), came, orders, turn)
+    hop = next(ahead)
+    go, hop = together(terms(own_next, peer_next, size_next, going, BF), hop)
+    came = first_hop(go)
+    hop = ahead.send(hop)
+    stay = terms(own_next, peer_next, size_next, staying, F32)
+    hop, came = together(hop, came)
+    behind = summing(stay, came, orders, turn)
+    hop, hop_next = ahead.send(hop), next(behind)
+    while isinstance(hop, list):
+        hop, hop_next = together(hop, hop_next)
+        hop, hop_next = ahead.send(hop), behind.send(hop_next)
+    while isinstance(hop_next, list):
+        hop_next = behind.send(hop_next)
+    done = [*hop, *hop_next]
     wide = channels // (2 * chips)
     grad_x, grad_small = placed(chips, where, done, wide, channels, state_weight.shape[1])
     return (mixed[None], grad_x, grad_small)

time: 200 us -> 194 us (0.970)
  waiting for transfers between devices: 70.8 us -> 56 us
  Pallas kernels: 78.3 us -> 90 us
  local copies, waits for them, and re-layouts: 18.8 us -> 13.6 us
  starting transfers between devices: 29.9 us -> 32.7 us
    ppermute x27, waiting for transfers between devices: 70.8 us -> 56 us  [send(): lax.ppermute(array, axis, [(i, i ^ mask) for i in range(lax.axis_size(axi...]
    pallas_call x11 -> x14, Pallas kernels: 21 us -> 29.6 us  [the longest x4 14.8 us: weight_terms(): pl.pallas_call(functools.partial(term_kernel, picked, pieces), grid=(own....]
    ppermute x2 -> x0, local copies, waits for them, and re-layouts: 3.17 us -> none  [send(): lax.ppermute(array, axis, [(i, i ^ mask) for i in range(lax.axis_size(axi...]
    ppermute x27, starting transfers between devices: 29.9 us -> 32.7 us  [send(): lax.ppermute(array, axis, [(i, i ^ mask) for i in range(lax.axis_size(axi...]
    unnamed x64 -> x68, local copies, waits for them, and re-layouts: 13.4 us -> 13.4 us
  transfers between devices with their start and end apart: 27 -> 27, of which waited for: 17 -> 17; matrix products, arithmetic and copies ran while one was open for 2% -> 0% of each run, Pallas kernels for 19% -> 26%
where the time goes in v2:
time: 194 us
  Pallas kernels  90 us (46%)
  waiting for transfers between devices  56 us (29%)
  starting transfers between devices  32.7 us (17%)
  local copies, waits for them, and re-layouts  13.6 us (7%)
    ppermute x27, waiting for transfers between devices, send(): lax.ppermute(array, axis, [(i, i ^ mask) for i in range(lax.axis_size(axi...  56 us
    ppermute x27, starting transfers between devices, send(): lax.ppermute(array, axis, [(i, i ^ mask) for i in range(lax.axis_size(axi...  32.7 us
    pallas_call x4, Pallas kernels, weight_terms(): pl.pallas_call(functools.partial(term_kernel, picked, pieces), grid=(own....  14.8 us
    unnamed x68, local copies, waits for them, and re-layouts  13.4 us
    pallas_call x1, Pallas kernels, inner_back(): pl.pallas_call(inner_back_kernel, grid=(channels // GROUP,), in_specs=[bl...  12.5 us
    pallas_call x2, Pallas kernels, finish(): pl.pallas_call(functools.partial(finish_kernel, first, len(arrived), last...  12.5 us
    pallas_call x1, Pallas kernels, project(): pl.pallas_call(project_kernel, grid=(channels // GROUP,), in_specs=[whole...  11.4 us
    pallas_call x1, Pallas kernels, normed(): pl.pallas_call(functools.partial(normed_kernel, len(arrived), heads), gri...  11.4 us
  transfers between devices with their start and end apart: 27, of which 17 were waited for; matrix products, arithmetic and copies ran while one was open for 0% of the time, Pallas kernels for 26%

profile of v2, /device:TPU:0, one launch (start us, length us, event | category | flops | bytes accessed | tf_op | source)
XLA Modules:
  0.0 193.6 jit_solution(15059598071301769735)
XLA Ops:
  0.6 1.4 copy.12.ws_ref
  2.1 0.6 copy-done.28
  2.7 0.7 copy-done.30
  3.4 3.9 %small.1 = (bf16[512,2048]{1,0:T(8,128)(2,1)S(1)}, f32[2,256,384]{2,1,0:T(8,128)S(1)}, f32[2,64,256]{2,1,0:T(8,128)S(1)}, bf16[2,256,384]{2,1,0:T(8,128)(2,1)S(1...) custom-call(bf16[256,2048]{1,0:T(8,128)(2,1)} %bitcast.h_ref.own_ref, ...), custom_call_target="tpu_custom_call" | custom-call | tf_op jit(solution)/shard_map/small/pallas_call | solution.py:134
  7.3 11.4 %project.1 = (bf16[2,256,2048]{2,1,0:T(8,128)(2,1)S(1)}, f32[2,72,2048]{2,1,0:T(8,128)S(1)}) custom-call(bf16[512,2048]{1,0:T(8,128)(2,1)S(1)} %get-tuple-element.76.both_ref, bf16[2048,2048]{1,0:T(8,128)(2,1)} %w_ref.1, bf16[2,128,256]{2,1,0:T(8,128)(2,1)S(1)} %get-tuple-element.77.bt_ref, bf16[2,256,96]{2,1,0:T(8,128)(2,1)S(1)} %get-tuple-element.78.weight3_ref, ...), custom_call_target="tpu_custom_call" | custom-call | tf_op jit(solution)/shard_map/project/pallas_call | solution.py:169
  18.7 1.3 copy-done
  20.9 6.5 %inner.2.after.raw_fwd_ref = f32[256,2048]{1,0:T(8,128)S(1)} custom-call(bf16[2,256,2048]{2,1,0:T(8,128)(2,1)} %copy-done, f32[2,256,384]{2,1,0:T(8,128)S(1)} %get-tuple-element.81.nat_ref.nat_fwd_ref.nat_rc_ref.refs_12_, f32[2,64,256]{2,1,0:T(8,128)S(1)} %get-tuple-element.82.lines_ref, f32[2,72,2048]{2,1,0:T(8,128)S(1)} %get-tuple-element.83.after.refs_0_.own_ref.refs_4_), custom_call_target="tpu_custom_call" | custom-call | tf_op jit(solution)/shard_map/inner/pallas_call | solution.py:231
  27.4 0.9 merge.2
  29.1 3.9 %collective-permute-start.4 = (bf16[80,2048]{1,0:T(8,128)(2,1)S(1)}, bf16[80,2048]{1,0:T(8,128)(2,1)S(1)}, u32[]{:S(2)}, u32[]{:S(2)}) collective-permute-start(bf16[80,2048]{1,0:T(8,128)(2,1)S(1)} %get-tuple-element.86), channel_id=1, source_target_pairs={{0,6},{1,7},{2,4},{3,5},{4,2},{5,3},{6,0},{7,1},{8,14},{9,15},{10,... | collective-permute-start | bytes 983048 | tf_op jit(solution)/shard_map/ppermute | solution.py:22
  33.7 4.4 %turned.1.after.left_ref = bf16[1024,1024]{1,0:T(8,128)(2,1)S(1)} custom-call(s32[8]{0:T(128)S(1)} %pad_add_fusion.where_ref, bf16[256,2048]{1,0:T(8,128)(2,1)} %bitcast.h_ref.own_ref.own_mirror_ref, bf16[256,2048]{1,0:T(8,128)(2,1)} %bitcast.h_ref.own_ref.own_mirror_ref, bf16[256,2048]{1,0:T(8,128)(2,1)} %collective-permute-done.peer_ref.peer_mirror_ref, ...), custom_call_target="tpu_custom_call" | custom-call | tf_op jit(solution)/shard_map/turned/pallas_call | solution.py:670
  38.0 1.4 copy-done.3
  39.4 4.4 %inner.3.raw_rc_ref = f32[256,2048]{1,0:T(8,128)S(1)} custom-call(bf16[2,256,2048]{2,1,0:T(8,128)(2,1)S(1)} %copy-done.1, f32[2,256,384]{2,1,0:T(8,128)S(1)} %copy-done.7, f32[2,64,256]{2,1,0:T(8,128)S(1)} %get-tuple-element.82.lines_ref, bf16[1024,1024]{1,0:T(8,128)(2,1)} %copy-done.3), custom_call_target="tpu_custom_call" | custom-call | tf_op jit(solution)/shard_map/inner/pallas_call | solution.py:231
  43.9 1.4 copy-done.13
  45.3 2.9 %collective-permute-done.2.refs_0_ = bf16[80,2048]{1,0:T(8,128)(2,1)S(1)} collective-permute-done((bf16[80,2048]{1,0:T(8,128)(2,1)S(1)}, bf16[80,2048]{1,0:T(8,128)(2,1)S(1)}, u32[]{:S(2)}, u32[]{:S(2)}) %collective-permute-start.2) | collective-permute-done | bytes 327712 | tf_op jit(solution)/shard_map/ppermute | solution.py:22
  48.2 11.4 %normed.1 = (bf16[256,2048]{1,0:T(8,128)(2,1)}, bf16[2,256,2048]{2,1,0:T(8,128)(2,1)}, f32[2,256,32]{2,1,0:T(8,128)S(1)}, f32[2,64,2048]{2,1,0:T(8,128)S(1)}, f3...) custom-call(f32[256,2048]{1,0:T(8,128)} %copy-done.8, ...), custom_call_target="tpu_custom_call" | custom-call | tf_op jit(solution)/shard_map/normed/pallas_call | solution.py:421
  59.6 1.0 copy-done.15
  60.6 2.7 %collective-permute-done.5.refs_2_.refs_7_ = f32[2,64,2048]{2,1,0:T(8,128)S(1)} collective-permute-done((f32[2,64,2048]{2,1,0:T(8,128)S(1)}, f32[2,64,2048]{2,1,0:T(8,128)S(1)}, u32[]{:S(2)}, u32[]{:S(2)}) %collective-permute-start.5) | collective-permute-done | bytes 1048608 | tf_op jit(solution)/shard_map/ppermute | solution.py:22
  63.3 1.6 merge.3
  64.9 1.0 copy-done.11
  65.9 1.5 collective-permute-start.6
  67.4 1.4 collective-permute-start.8
  68.7 0.6 collective-permute-start.7
  69.4 1.6 copy-done.17
  71.0 12.5 %inner_back.1 = (f32[2,256,2048]{2,1,0:T(8,128)}, f32[2,256,64]{2,1,0:T(8,128)S(1)}, f32[2,256,64]{2,1,0:T(8,128)S(1)}) custom-call(bf16[2,256,2048]{2,1,0:T(8,128)(2,1)S(1)} %copy-done.2, bf16[2,256,2048]{2,1,0:T(8,128)(2,1)S(1)} %copy-done.17, f32[2,256,384]{2,1,0:T(8,128)S(1)} %copy-done.7, f32[2,64,256]{2,1,0:T(8,128)S(1)} %get-tuple-element.82.lines_ref, ...), custom_call_target="tpu_custom_call" | custom-call | tf_op jit(solution)/shard_map/inner_back/pallas_call | solution.py:521
  83.6 5.3 %finish.2 = (bf16[512,1024]{1,0:T(8,128)(2,1)S(1)}, f32[2,256,64]{2,1,0:T(8,128)S(1)}, f32[2,256,32]{2,1,0:T(8,128)S(1)}, f32[2,1,32]{2,1,0:T(1,128)S(1)}) custom-call(bf16[2,256,2048]{2,1,0:T(8,128)(2,1)} %copy-done, f32[2,256,2048]{2,1,0:T(8,128)} %get-tuple-element.93.refs_1_, bf16[2,256,384]{2,1,0:T(8,128)(2,1)S(1)} %copy-done.19, ...), custom_call_target="tpu_custom_call" | custom-call | tf_op jit(solution)/shard_map/finish/pallas_call | solution.py:626
  89.0 2.6 %collective-permute-done.9.peer_ref = bf16[512,1024]{1,0:T(8,128)(2,1)S(1)} collective-permute-done((bf16[512,1024]{1,0:T(8,128)(2,1)S(1)}, bf16[512,1024]{1,0:T(8,128)(2,1)S(1)}, u32[]{:S(2)}, u32[]{:S(2)}) %collective-permute-start.9) | collective-permute-done | bytes 1048608 | tf_op jit(solution)/shard_map/ppermute | solution.py:22
  91.7 2.3 %terms.4 = (bf16[512,512]{1,0:T(8,128)(2,1)S(1)}, bf16[512,512]{1,0:T(8,128)(2,1)S(1)}) custom-call(bf16[1024,1024]{1,0:T(8,128)(2,1)S(1)} %copy-done.4, bf16[512,1024]{1,0:T(8,128)(2,1)S(1)} %get-tuple-element.98.own_ref, bf16[512,1024]{1,0:T(8,128)(2,1)S(1)} %collective-permute-done.9.peer_ref, f32[2,1,32]{2,1,0:T(1,128)S(1)} %get-tuple-element.99.after.refs_20_), custom_call_target="tpu_custom_call" | custom-call | tf_op jit(solution)/shard_map/terms/pallas_call | solution.py:724
  94.0 1.5 collective-permute-start.11
  95.4 0.6 collective-permute-start.10
  96.1 7.2 %finish.3 = (bf16[512,1280]{1,0:T(8,128)(2,1)}, f32[2,256,64]{2,1,0:T(8,128)}, f32[2,256,32]{2,1,0:T(8,128)}, f32[2,1,32]{2,1,0:T(1,128)}) custom-call(bf16[2,256,2048]{2,1,0:T(8,128)(2,1)} %copy-done, f32[2,256,2048]{2,1,0:T(8,128)} %get-tuple-element.93.refs_1_, bf16[2,256,384]{2,1,0:T(8,128)(2,1)S(1)} %copy-done.19, f32[2,64,2048]{2,1,0:T(8,128)S(1)} %copy-done.16, ...), custom_call_target="tpu_custom_call" | custom-call | tf_op jit(solution)/shard_map/finish/pallas_call | solution.py:626
  103.2 4.8 %collective-permute-done.11.refs_3_ = bf16[512,512]{1,0:T(8,128)(2,1)S(1)} collective-permute-done((bf16[512,512]{1,0:T(8,128)(2,1)S(1)}, bf16[512,512]{1,0:T(8,128)(2,1)S(1)}, u32[]{:S(2)}, u32[]{:S(2)}) %collective-permute-start.11) | collective-permute-done | bytes 524320 | tf_op jit(solution)/shard_map/ppermute | solution.py:22
  108.0 1.1 collective-permute-done.10.refs_1_
  109.1 1.3 copy-done.9
  110.5 3.9 %terms.5 = (f32[512,512]{1,0:T(8,128)S(1)}, f32[512,512]{1,0:T(8,128)S(1)}) custom-call(bf16[1024,1024]{1,0:T(8,128)(2,1)} %copy-done.3, bf16[512,1024]{1,0:T(8,128)(2,1)S(1)} %get-tuple-element.98.own_ref, bf16[512,1024]{1,0:T(8,128)(2,1)S(1)} %collective-permute-done.9.peer_ref, bf16[512,1280]{1,0:T(8,128)(2,1)S(1)} %copy-done.9), custom_call_target="tpu_custom_call" | custom-call | tf_op jit(solution)/shard_map/terms/pallas_call | solution.py:724
  114.4 0.8 fold.8
  115.2 0.7 collective-permute-start.13
  115.8 1.5 collective-permute-start.14
  117.3 4.2 %terms.6 = (bf16[512,512]{1,0:T(8,128)(2,1)S(1)}, bf16[512,768]{1,0:T(8,128)(2,1)S(1)}) custom-call(bf16[1024,1024]{1,0:T(8,128)(2,1)} %copy-done.3, bf16[512,1280]{1,0:T(8,128)(2,1)S(1)} %copy-done.10, bf16[512,1280]{1,0:T(8,128)(2,1)S(1)} %collective-permute-done.12.peer_ref, f32[256,512]{1,0:T(8,128)S(1)} %get-tuple-element.113.after.refs_0_), custom_call_target="tpu_custom_call" | custom-call | tf_op jit(solution)/shard_map/terms/pallas_call | solution.py:724
  121.6 2.3 %collective-permute-done.13.refs_1_ = bf16[256,512]{1,0:T(8,128)(2,1)S(1)} collective-permute-done((bf16[256,512]{1,0:T(8,128)(2,1)S(1)}, bf16[256,512]{1,0:T(8,128)(2,1)S(1)}, u32[]{:S(2)}, u32[]{:S(2)}) %collective-permute-start.13) | collective-permute-done | bytes 262176 | tf_op jit(solution)/shard_map/ppermute | solution.py:22
  124.3 1.4 collective-permute-start.17
  125.7 0.6 collective-permute-start.16
  126.7 1.8 collective-permute-start.15
  128.6 4.3 %terms.7 = (f32[512,512]{1,0:T(8,128)S(1)}, f32[512,768]{1,0:T(8,128)S(1)}) custom-call(bf16[1024,1024]{1,0:T(8,128)(2,1)} %copy-done.3, bf16[512,1280]{1,0:T(8,128)(2,1)S(1)} %copy-done.10, bf16[512,1280]{1,0:T(8,128)(2,1)S(1)} %collective-permute-done.12.peer_ref, f32[128,1024]{1,0:T(8,128)S(1)} %get-tuple-element.121.after.refs_0_), custom_call_target="tpu_custom_call" | custom-call | tf_op jit(solution)/shard_map/terms/pallas_call | solution.py:724
  132.9 1.1 collective-permute-done.15.refs_1_
  134.0 4.7 %collective-permute-done.16.refs_1_ = bf16[512,512]{1,0:T(8,128)(2,1)S(1)} collective-permute-done((bf16[512,512]{1,0:T(8,128)(2,1)S(1)}, bf16[512,512]{1,0:T(8,128)(2,1)S(1)}, u32[]{:S(2)}, u32[]{:S(2)}) %collective-permute-start.16) | collective-permute-done | bytes 524320 | tf_op jit(solution)/shard_map/ppermute | solution.py:22
  138.6 4.5 %collective-permute-done.17.refs_3_ = bf16[512,768]{1,0:T(8,128)(2,1)S(1)} collective-permute-done((bf16[512,768]{1,0:T(8,128)(2,1)S(1)}, bf16[512,768]{1,0:T(8,128)(2,1)S(1)}, u32[]{:S(2)}, u32[]{:S(2)}) %collective-permute-start.17) | collective-permute-done | bytes 786464 | tf_op jit(solution)/shard_map/ppermute | solution.py:22
  143.4 1.0 fold.11
  144.4 1.6 collective-permute-start.20
  146.0 0.6 collective-permute-start.19
  146.6 2.7 %collective-permute-start.18 = (bf16[64,1024]{1,0:T(8,128)(2,1)S(1)}, bf16[64,1024]{1,0:T(8,128)(2,1)S(1)}, u32[]{:S(2)}, u32[]{:S(2)}) collective-permute-start(bf16[64,1024]{1,0:T(8,128)(2,1)S(1)} %get-tuple-element.132), channel_id=1, source_target_pairs={{0,16},{8,24},{16,0},{24,8},{1,17},{9,25},{17,1},{25,9},{2,18},{10... | collective-permute-start | bytes 393224 | tf_op jit(solution)/shard_map/ppermute | solution.py:22
  149.3 4.6 %collective-permute-done.18.refs_1_ = bf16[64,1024]{1,0:T(8,128)(2,1)S(1)} collective-permute-done((bf16[64,1024]{1,0:T(8,128)(2,1)S(1)}, bf16[64,1024]{1,0:T(8,128)(2,1)S(1)}, u32[]{:S(2)}, u32[]{:S(2)}) %collective-permute-start.18) | collective-permute-done | bytes 131104 | tf_op jit(solution)/shard_map/ppermute | solution.py:22
  154.2 0.6 fold.13
  154.8 1.7 collective-permute-start.22
  156.4 2.6 %collective-permute-start.21 = (bf16[64,1024]{1,0:T(8,128)(2,1)S(1)}, bf16[64,1024]{1,0:T(8,128)(2,1)S(1)}, u32[]{:S(2)}, u32[]{:S(2)}) collective-permute-start(bf16[64,1024]{1,0:T(8,128)(2,1)S(1)} %fold.12.after), channel_id=1, source_target_pairs={{0,16},{8,24},{16,0},{24,8},{1,17},{9,25},{17,1},{25,9},{2,18},{10... | collective-permute-start | bytes 393224 | tf_op jit(solution)/shard_map/ppermute | solution.py:22
  159.0 4.9 %collective-permute-done.21 = bf16[64,1024]{1,0:T(8,128)(2,1)S(1)} collective-permute-done((bf16[64,1024]{1,0:T(8,128)(2,1)S(1)}, bf16[64,1024]{1,0:T(8,128)(2,1)S(1)}, u32[]{:S(2)}, u32[]{:S(2)}) %collective-permute-start.21) | collective-permute-done | bytes 131104 | tf_op jit(solution)/shard_map/ppermute | solution.py:22
  163.9 0.9 collective-permute-done.22.refs_1_
  164.9 2.6 %collective-permute-start.23 = (bf16[128,1024]{1,0:T(8,128)(2,1)S(1)}, bf16[128,1024]{1,0:T(8,128)(2,1)S(1)}, u32[]{:S(2)}, u32[]{:S(2)}) collective-permute-start(bf16[128,1024]{1,0:T(8,128)(2,1)S(1)} %pad_maximum_fusion.1.refs_0_), channel_id=1, source_target_pairs={{0,8},{8,0},{16,24},{24,16},{1,9},{9,1},{17,25},{25,17},{2,10},{10... | collective-permute-start | bytes 786440 | tf_op jit(solution)/shard_map/ppermute | solution.py:22
  167.9 1.6 collective-permute-start.24
  169.5 5.2 %collective-permute-done.24.refs_1_ = bf16[64,1280]{1,0:T(8,128)(2,1)S(1)} collective-permute-done((bf16[64,1280]{1,0:T(8,128)(2,1)S(1)}, bf16[64,1280]{1,0:T(8,128)(2,1)S(1)}, u32[]{:S(2)}, u32[]{:S(2)}) %collective-permute-start.24) | collective-permute-done | bytes 163872 | tf_op jit(solution)/shard_map/ppermute | solution.py:22
  175.0 2.5 %collective-permute-start.25 = (bf16[64,1280]{1,0:T(8,128)(2,1)S(1)}, bf16[64,1280]{1,0:T(8,128)(2,1)S(1)}, u32[]{:S(2)}, u32[]{:S(2)}) collective-permute-start(bf16[64,1280]{1,0:T(8,128)(2,1)S(1)} %fold.15), channel_id=1, source_target_pairs={{0,16},{8,24},{16,0},{24,8},{1,17},{9,25},{17,1},{25,9},{2,18},{10... | collective-permute-start | bytes 491528 | tf_op jit(solution)/shard_map/ppermute | solution.py:22
  177.4 6.2 %collective-permute-done.25 = bf16[64,1280]{1,0:T(8,128)(2,1)S(1)} collective-permute-done((bf16[64,1280]{1,0:T(8,128)(2,1)S(1)}, bf16[64,1280]{1,0:T(8,128)(2,1)S(1)}, u32[]{:S(2)}, u32[]{:S(2)}) %collective-permute-start.25) | collective-permute-done | bytes 163872 | tf_op jit(solution)/shard_map/ppermute | solution.py:22
  183.9 6.9 %collective-permute-done.26.refs_3_ = bf16[128,1280]{1,0:T(8,128)(2,1)S(1)} collective-permute-done((bf16[128,1280]{1,0:T(8,128)(2,1)S(1)}, bf16[128,1280]{1,0:T(8,128)(2,1)S(1)}, u32[]{:S(2)}, u32[]{:S(2)}) %collective-permute-start.26) | collective-permute-done | bytes 327712 | tf_op jit(solution)/shard_map/ppermute | solution.py:22
  190.8 2.0 %placed.1 = (f32[256,2048]{1,0:T(8,128)}, f32[256,160]{1,0:T(8,128)S(1)}) custom-call(s32[8]{0:T(128)S(1)} %pad_add_fusion.where_ref, bf16[128,1024]{1,0:T(8,128)(2,1)S(1)} %pad_maximum_fusion.1.refs_0_, bf16[128,1024]{1,0:T(8,128)(2,1)S(1)} %collective-permute-done.23.refs_1_, bf16[128,1280]{1,0:T(8,128)(2,1)S(1)} %pad_maximum_fusion.refs_2_, ...), custom_call_target="tpu_custom_call" | custom-call | tf_op jit(solution)/shard_map/placed/pallas_call | solution.py:822
  192.9 0.8 copy.13
  (95 shorter events, 4.9 us)
Async XLA Ops:
  2.0 0.7 copy-start.28
  2.7 0.7 copy-start.30
  7.2 11.4 %copy-start.18 = (bf16[2,256,384]{2,1,0:T(8,128)(2,1)}, bf16[2,256,384]{2,1,0:T(8,128)(2,1)S(1)}, u32[]{:S(2)}) copy-start(bf16[2,256,384]{2,1,0:T(8,128)(2,1)S(1)} %get-tuple-element.94.refs_2_) | copy-start | bytes 1179652
  7.2 11.4 %copy-start.21 = (bf16[2,256,384]{2,1,0:T(8,128)(2,1)}, bf16[2,256,384]{2,1,0:T(8,128)(2,1)S(1)}, u32[]{:S(2)}) copy-start(bf16[2,256,384]{2,1,0:T(8,128)(2,1)S(1)} %get-tuple-element.85.cg3_ref) | copy-start | bytes 1179652
  7.2 13.6 %copy-start.6 = (f32[2,256,384]{2,1,0:T(8,128)}, f32[2,256,384]{2,1,0:T(8,128)S(1)}, u32[]{:S(2)}) copy-start(f32[2,256,384]{2,1,0:T(8,128)S(1)} %get-tuple-element.81.nat_ref.nat_fwd_ref.nat_rc_ref.refs_12_) | copy-start | bytes 2359300
  7.3 13.5 %copy-start.32 = (s32[2]{0:T(128)S(1)}, s32[2]{0:T(128)}, u32[]{:S(2)}) copy-start(s32[2]{0:T(128)} %constant.42.clone) | copy-start | bytes 28
  18.7 1.3 copy-start
  20.0 7.4 %copy-start.5 = (f32[2,72,2048]{2,1,0:T(8,128)}, f32[2,72,2048]{2,1,0:T(8,128)S(1)}, u32[]{:S(2)}) copy-start(f32[2,72,2048]{2,1,0:T(8,128)S(1)} %get-tuple-element.83.after.refs_0_.own_ref.refs_4_) | copy-start | bytes 3538948
  20.0 7.4 %collective-permute-start.1 = (f32[2,72,2048]{2,1,0:T(8,128)S(1)}, f32[2,72,2048]{2,1,0:T(8,128)S(1)}, u32[]{:S(2)}, u32[]{:S(2)}) collective-permute-start(f32[2,72,2048]{2,1,0:T(8,128)S(1)} %get-tuple-element.83.after.refs_0_.own_ref.refs_4_), channel_id=1, source_target_pairs={{0,1},{1,0},{2,3},{3,2},{4,5},{5,4},{6,7},{7,6},{8,9},{9,8},{10,11... | collective-permute-start | bytes 3538952 | tf_op jit(solution)/shard_map/ppermute | solution.py:22
  20.4 13.2 %collective-permute-start = (bf16[256,2048]{1,0:T(8,128)(2,1)}, bf16[256,2048]{1,0:T(8,128)(2,1)}, u32[]{:S(2)}, u32[]{:S(2)}) collective-permute-start(bf16[256,2048]{1,0:T(8,128)(2,1)} %bitcast.h_ref.own_ref.own_mirror_ref), channel_id=1, source_target_pairs={{0,1},{1,0},{2,3},{3,2},{4,5},{5,4},{6,7},{7,6},{8,9},{9,8},{10,11... | collective-permute-start | bytes 3145736 | tf_op jit(solution)/shard_map/ppermute | solution.py:22
  27.4 1.4 copy-start.8
  27.4 6.2 %copy-start.31 = (s32[4]{0:T(128)S(1)}, s32[4]{0:T(128)}, u32[]{:S(2)}) copy-start(s32[4]{0:T(128)} %constant.43.clone) | copy-start | bytes 52
  27.4 1.7 copy-start.14
  29.1 19.1 %collective-permute-start.4 = (bf16[80,2048]{1,0:T(8,128)(2,1)S(1)}, bf16[80,2048]{1,0:T(8,128)(2,1)S(1)}, u32[]{:S(2)}, u32[]{:S(2)}) collective-permute-start(bf16[80,2048]{1,0:T(8,128)(2,1)S(1)} %get-tuple-element.86), channel_id=1, source_target_pairs={{0,6},{1,7},{2,4},{3,5},{4,2},{5,3},{6,0},{7,1},{8,14},{9,15},{10,... | collective-permute-start | bytes 983048 | tf_op jit(solution)/shard_map/ppermute | solution.py:22
  33.0 15.2 %collective-permute-start.3 = (bf16[80,2048]{1,0:T(8,128)(2,1)S(1)}, bf16[80,2048]{1,0:T(8,128)(2,1)S(1)}, u32[]{:S(2)}, u32[]{:S(2)}) collective-permute-start(bf16[80,2048]{1,0:T(8,128)(2,1)S(1)} %get-tuple-element.86), channel_id=1, source_target_pairs={{0,4},{1,5},{2,6},{3,7},{4,0},{5,1},{6,2},{7,3},{8,12},{9,13},{10,... | collective-permute-start | bytes 983048 | tf_op jit(solution)/shard_map/ppermute | solution.py:22
  33.5 14.7 %collective-permute-start.2 = (bf16[80,2048]{1,0:T(8,128)(2,1)S(1)}, bf16[80,2048]{1,0:T(8,128)(2,1)S(1)}, u32[]{:S(2)}, u32[]{:S(2)}) collective-permute-start(bf16[80,2048]{1,0:T(8,128)(2,1)S(1)} %get-tuple-element.84.after), channel_id=1, source_target_pairs={{0,2},{1,3},{2,0},{3,1},{4,6},{5,7},{6,4},{7,5},{8,10},{9,11},{10,... | collective-permute-start | bytes 983048 | tf_op jit(solution)/shard_map/ppermute | solution.py:22
  33.6 5.7 %copy-start.1 = (bf16[2,256,2048]{2,1,0:T(8,128)(2,1)S(1)}, bf16[2,256,2048]{2,1,0:T(8,128)(2,1)}, u32[]{:S(2)}) copy-start(bf16[2,256,2048]{2,1,0:T(8,128)(2,1)} %copy-done) | copy-start | bytes 6291460
  33.6 5.7 %copy-start.7 = (f32[2,256,384]{2,1,0:T(8,128)S(1)}, f32[2,256,384]{2,1,0:T(8,128)}, u32[]{:S(2)}) copy-start(f32[2,256,384]{2,1,0:T(8,128)} %copy-done.6) | copy-start | bytes 2359300
  38.0 1.4 copy-start.3
  39.4 8.8 %copy-start.20 = (bf16[1,256,2048]{2,1,0:T(8,128)(2,1)S(1)}, bf16[1,256,2048]{2,1,0:T(8,128)(2,1)}, u32[]{:S(2)}) copy-start(bf16[1,256,2048]{2,1,0:T(8,128)(2,1)} %param.15) | copy-start | bytes 3145732
  39.4 8.8 %copy-start.22 = (bf16[2,256,384]{2,1,0:T(8,128)(2,1)S(1)}, bf16[2,256,384]{2,1,0:T(8,128)(2,1)}, u32[]{:S(2)}) copy-start(bf16[2,256,384]{2,1,0:T(8,128)(2,1)} %copy-done.21) | copy-start | bytes 1179652
  39.4 8.8 %copy-start.27 = (f32[2048]{0:T(1024)S(1)}, f32[2048]{0:T(1024)}, u32[]{:S(2)}) copy-start(f32[2048]{0:T(1024)} %param.14) | copy-start | bytes 24580
  43.9 1.4 copy-start.13
  59.6 1.0 copy-start.15
  60.6 4.2 %copy-start.23 = (f32[2,256,32]{2,1,0:T(8,128)}, f32[2,256,32]{2,1,0:T(8,128)S(1)}, u32[]{:S(2)}) copy-start(f32[2,256,32]{2,1,0:T(8,128)S(1)} %get-tuple-element.103.refs_16_) | copy-start | bytes 196612
  60.6 5.2 %copy-start.25 = (f32[2,256,64]{2,1,0:T(8,128)}, f32[2,256,64]{2,1,0:T(8,128)S(1)}, u32[]{:S(2)}) copy-start(f32[2,256,64]{2,1,0:T(8,128)S(1)} %get-tuple-element.102.refs_15_) | copy-start | bytes 393220
  60.6 8.8 %copy-start.2 = (bf16[2,256,2048]{2,1,0:T(8,128)(2,1)S(1)}, bf16[2,256,2048]{2,1,0:T(8,128)(2,1)}, u32[]{:S(2)}) copy-start(bf16[2,256,2048]{2,1,0:T(8,128)(2,1)} %copy-done) | copy-start | bytes 6291460
  60.6 2.7 %collective-permute-start.5 = (f32[2,64,2048]{2,1,0:T(8,128)S(1)}, f32[2,64,2048]{2,1,0:T(8,128)S(1)}, u32[]{:S(2)}, u32[]{:S(2)}) collective-permute-start(f32[2,64,2048]{2,1,0:T(8,128)S(1)} %get-tuple-element.90.after.refs_1_), channel_id=1, source_target_pairs={{0,1},{1,0},{2,3},{3,2},{4,5},{5,4},{6,7},{7,6},{8,9},{9,8},{10,11... | collective-permute-start | bytes 3145736 | tf_op jit(solution)/shard_map/ppermute | solution.py:22
  64.9 1.0 copy-start.11
  65.9 17.7 %collective-permute-start.6 = (bf16[64,2048]{1,0:T(8,128)(2,1)}, bf16[64,2048]{1,0:T(8,128)(2,1)S(1)}, u32[]{:S(2)}, u32[]{:S(2)}) collective-permute-start(bf16[64,2048]{1,0:T(8,128)(2,1)} %get-tuple-element.92.after), channel_id=1, source_target_pairs={{0,2},{1,3},{2,0},{3,1},{4,6},{5,7},{6,4},{7,5},{8,10},{9,11},{10,... | collective-permute-start | bytes 786440 | tf_op jit(solution)/shard_map/ppermute | solution.py:22
  67.4 16.2 %collective-permute-start.8 = (bf16[64,2048]{1,0:T(8,128)(2,1)}, bf16[64,2048]{1,0:T(8,128)(2,1)}, u32[]{:S(2)}, u32[]{:S(2)}) collective-permute-start(bf16[64,2048]{1,0:T(8,128)(2,1)} %get-tuple-element.96), channel_id=1, source_target_pairs={{0,6},{1,7},{2,4},{3,5},{4,2},{5,3},{6,0},{7,1},{8,14},{9,15},{10,... | collective-permute-start | bytes 786440 | tf_op jit(solution)/shard_map/ppermute | solution.py:22
  68.7 14.8 %collective-permute-start.7 = (bf16[64,2048]{1,0:T(8,128)(2,1)}, bf16[64,2048]{1,0:T(8,128)(2,1)}, u32[]{:S(2)}, u32[]{:S(2)}) collective-permute-start(bf16[64,2048]{1,0:T(8,128)(2,1)} %get-tuple-element.96), channel_id=1, source_target_pairs={{0,4},{1,5},{2,6},{3,7},{4,0},{5,1},{6,2},{7,3},{8,12},{9,13},{10,... | collective-permute-start | bytes 786440 | tf_op jit(solution)/shard_map/ppermute | solution.py:22
  69.4 1.6 copy-start.17
  71.0 12.6 %copy-start.12 = (f32[2,64,2048]{2,1,0:T(8,128)S(1)}, f32[2,64,2048]{2,1,0:T(8,128)}, u32[]{:S(2)}) copy-start(f32[2,64,2048]{2,1,0:T(8,128)} %copy-done.11) | copy-start | bytes 3145732
  71.0 12.6 %copy-start.16 = (f32[2,64,2048]{2,1,0:T(8,128)S(1)}, f32[2,64,2048]{2,1,0:T(8,128)}, u32[]{:S(2)}) copy-start(f32[2,64,2048]{2,1,0:T(8,128)} %copy-done.15) | copy-start | bytes 3145732
  71.0 12.6 %copy-start.19 = (bf16[2,256,384]{2,1,0:T(8,128)(2,1)S(1)}, bf16[2,256,384]{2,1,0:T(8,128)(2,1)}, u32[]{:S(2)}) copy-start(bf16[2,256,384]{2,1,0:T(8,128)(2,1)} %copy-done.18) | copy-start | bytes 1179652
  83.6 8.0 %copy-start.4 = (bf16[1024,1024]{1,0:T(8,128)(2,1)S(1)}, bf16[1024,1024]{1,0:T(8,128)(2,1)}, u32[]{:S(2)}) copy-start(bf16[1024,1024]{1,0:T(8,128)(2,1)} %copy-done.3) | copy-start | bytes 6291460
  88.9 2.7 %collective-permute-start.9 = (bf16[512,1024]{1,0:T(8,128)(2,1)S(1)}, bf16[512,1024]{1,0:T(8,128)(2,1)S(1)}, u32[]{:S(2)}, u32[]{:S(2)}) collective-permute-start(bf16[512,1024]{1,0:T(8,128)(2,1)S(1)} %get-tuple-element.98.own_ref), channel_id=1, source_target_pairs={{0,1},{1,0},{2,3},{3,2},{4,5},{5,4},{6,7},{7,6},{8,9},{9,8},{10,11... | collective-permute-start | bytes 3145736 | tf_op jit(solution)/shard_map/ppermute | solution.py:22
  91.7 4.4 %copy-start.24 = (f32[2,256,32]{2,1,0:T(8,128)S(1)}, f32[2,256,32]{2,1,0:T(8,128)}, u32[]{:S(2)}) copy-start(f32[2,256,32]{2,1,0:T(8,128)} %copy-done.23) | copy-start | bytes 196612
  91.7 4.4 %copy-start.26 = (f32[2,256,64]{2,1,0:T(8,128)S(1)}, f32[2,256,64]{2,1,0:T(8,128)}, u32[]{:S(2)}) copy-start(f32[2,256,64]{2,1,0:T(8,128)} %copy-done.25) | copy-start | bytes 393220
  91.7 4.4 %copy-start.29 = (f32[32]{0:T(128)S(1)}, f32[32]{0:T(128)}, u32[]{:S(2)}) copy-start(f32[32]{0:T(128)} %param.12) | copy-start | bytes 388
  94.0 14.0 %collective-permute-start.11 = (bf16[512,512]{1,0:T(8,128)(2,1)S(1)}, bf16[512,512]{1,0:T(8,128)(2,1)S(1)}, u32[]{:S(2)}, u32[]{:S(2)}) collective-permute-start(bf16[512,512]{1,0:T(8,128)(2,1)S(1)} %get-tuple-element.107), channel_id=1, source_target_pairs={{0,4},{1,5},{2,6},{3,7},{4,0},{5,1},{6,2},{7,3},{8,12},{9,13},{10,... | collective-permute-start | bytes 1572872 | tf_op jit(solution)/shard_map/ppermute | solution.py:22
  95.4 13.7 %collective-permute-start.10 = (bf16[512,512]{1,0:T(8,128)(2,1)S(1)}, bf16[512,512]{1,0:T(8,128)(2,1)S(1)}, u32[]{:S(2)}, u32[]{:S(2)}) collective-permute-start(bf16[512,512]{1,0:T(8,128)(2,1)S(1)} %get-tuple-element.100.refs_11_), channel_id=1, source_target_pairs={{0,2},{1,3},{2,0},{3,1},{4,6},{5,7},{6,4},{7,5},{8,10},{9,11},{10,... | collective-permute-start | bytes 1572872 | tf_op jit(solution)/shard_map/ppermute | solution.py:22
  109.1 8.2 %collective-permute-start.12 = (bf16[512,1280]{1,0:T(8,128)(2,1)}, bf16[512,1280]{1,0:T(8,128)(2,1)S(1)}, u32[]{:S(2)}, u32[]{:S(2)}) collective-permute-start(bf16[512,1280]{1,0:T(8,128)(2,1)} %get-tuple-element.108.after.own_ref), channel_id=1, source_target_pairs={{0,1},{1,0},{2,3},{3,2},{4,5},{5,4},{6,7},{7,6},{8,9},{9,8},{10,11... | collective-permute-start | bytes 3932168 | tf_op jit(solution)/shard_map/ppermute | solution.py:22
  109.1 1.3 copy-start.9
  114.3 3.0 %copy-start.10 = (bf16[512,1280]{1,0:T(8,128)(2,1)S(1)}, bf16[512,1280]{1,0:T(8,128)(2,1)}, u32[]{:S(2)}) copy-start(bf16[512,1280]{1,0:T(8,128)(2,1)} %get-tuple-element.108.after.own_ref) | copy-start | bytes 3932164
  115.2 8.8 %collective-permute-start.13 = (bf16[256,512]{1,0:T(8,128)(2,1)S(1)}, bf16[256,512]{1,0:T(8,128)(2,1)S(1)}, u32[]{:S(2)}, u32[]{:S(2)}) collective-permute-start(bf16[256,512]{1,0:T(8,128)(2,1)S(1)} %get-tuple-element.116), channel_id=1, source_target_pairs={{0,4},{1,5},{2,6},{3,7},{4,0},{5,1},{6,2},{7,3},{8,12},{9,13},{10,... | collective-permute-start | bytes 786440 | tf_op jit(solution)/shard_map/ppermute | solution.py:22
  115.8 8.4 %collective-permute-start.14 = (bf16[256,512]{1,0:T(8,128)(2,1)S(1)}, bf16[256,512]{1,0:T(8,128)(2,1)S(1)}, u32[]{:S(2)}, u32[]{:S(2)}) collective-permute-start(bf16[256,512]{1,0:T(8,128)(2,1)S(1)} %get-tuple-element.117), channel_id=1, source_target_pairs={{0,2},{1,3},{2,0},{3,1},{4,6},{5,7},{6,4},{7,5},{8,10},{9,11},{10,... | collective-permute-start | bytes 786440 | tf_op jit(solution)/shard_map/ppermute | solution.py:22
  124.3 18.8 %collective-permute-start.17 = (bf16[512,768]{1,0:T(8,128)(2,1)S(1)}, bf16[512,768]{1,0:T(8,128)(2,1)S(1)}, u32[]{:S(2)}, u32[]{:S(2)}) collective-permute-start(bf16[512,768]{1,0:T(8,128)(2,1)S(1)} %get-tuple-element.125), channel_id=1, source_target_pairs={{0,4},{1,5},{2,6},{3,7},{4,0},{5,1},{6,2},{7,3},{8,12},{9,13},{10,... | collective-permute-start | bytes 2359304 | tf_op jit(solution)/shard_map/ppermute | solution.py:22
  125.7 13.0 %collective-permute-start.16 = (bf16[512,512]{1,0:T(8,128)(2,1)S(1)}, bf16[512,512]{1,0:T(8,128)(2,1)S(1)}, u32[]{:S(2)}, u32[]{:S(2)}) collective-permute-start(bf16[512,512]{1,0:T(8,128)(2,1)S(1)} %get-tuple-element.124.after), channel_id=1, source_target_pairs={{0,2},{1,3},{2,0},{3,1},{4,6},{5,7},{6,4},{7,5},{8,10},{9,11},{10,... | collective-permute-start | bytes 1572872 | tf_op jit(solution)/shard_map/ppermute | solution.py:22
  126.7 7.2 %collective-permute-start.15 = (bf16[128,1024]{1,0:T(8,128)(2,1)S(1)}, bf16[128,1024]{1,0:T(8,128)(2,1)S(1)}, u32[]{:S(2)}, u32[]{:S(2)}) collective-permute-start(bf16[128,1024]{1,0:T(8,128)(2,1)S(1)} %get-tuple-element.123), channel_id=1, source_target_pairs={{0,8},{8,0},{16,24},{24,16},{1,9},{9,1},{17,25},{25,17},{2,10},{10... | collective-permute-start | bytes 786440 | tf_op jit(solution)/shard_map/ppermute | solution.py:22
  144.4 9.6 %collective-permute-start.20 = (bf16[256,768]{1,0:T(8,128)(2,1)S(1)}, bf16[256,768]{1,0:T(8,128)(2,1)S(1)}, u32[]{:S(2)}, u32[]{:S(2)}) collective-permute-start(bf16[256,768]{1,0:T(8,128)(2,1)S(1)} %get-tuple-element.134), channel_id=1, source_target_pairs={{0,2},{1,3},{2,0},{3,1},{4,6},{5,7},{6,4},{7,5},{8,10},{9,11},{10,... | collective-permute-start | bytes 1179656 | tf_op jit(solution)/shard_map/ppermute | solution.py:22
  146.0 7.9 %collective-permute-start.19 = (bf16[256,512]{1,0:T(8,128)(2,1)S(1)}, bf16[256,512]{1,0:T(8,128)(2,1)S(1)}, u32[]{:S(2)}, u32[]{:S(2)}) collective-permute-start(bf16[256,512]{1,0:T(8,128)(2,1)S(1)} %get-tuple-element.133), channel_id=1, source_target_pairs={{0,4},{1,5},{2,6},{3,7},{4,0},{5,1},{6,2},{7,3},{8,12},{9,13},{10,... | collective-permute-start | bytes 786440 | tf_op jit(solution)/shard_map/ppermute | solution.py:22
  146.6 7.3 %collective-permute-start.18 = (bf16[64,1024]{1,0:T(8,128)(2,1)S(1)}, bf16[64,1024]{1,0:T(8,128)(2,1)S(1)}, u32[]{:S(2)}, u32[]{:S(2)}) collective-permute-start(bf16[64,1024]{1,0:T(8,128)(2,1)S(1)} %get-tuple-element.132), channel_id=1, source_target_pairs={{0,16},{8,24},{16,0},{24,8},{1,17},{9,25},{17,1},{25,9},{2,18},{10... | collective-permute-start | bytes 393224 | tf_op jit(solution)/shard_map/ppermute | solution.py:22
  154.8 10.1 %collective-permute-start.22 = (bf16[128,1280]{1,0:T(8,128)(2,1)S(1)}, bf16[128,1280]{1,0:T(8,128)(2,1)S(1)}, u32[]{:S(2)}, u32[]{:S(2)}) collective-permute-start(bf16[128,1280]{1,0:T(8,128)(2,1)S(1)} %get-tuple-element.139), channel_id=1, source_target_pairs={{0,8},{8,0},{16,24},{24,16},{1,9},{9,1},{17,25},{25,17},{2,10},{10... | collective-permute-start | bytes 983048 | tf_op jit(solution)/shard_map/ppermute | solution.py:22
  156.4 7.5 %collective-permute-start.21 = (bf16[64,1024]{1,0:T(8,128)(2,1)S(1)}, bf16[64,1024]{1,0:T(8,128)(2,1)S(1)}, u32[]{:S(2)}, u32[]{:S(2)}) collective-permute-start(bf16[64,1024]{1,0:T(8,128)(2,1)S(1)} %fold.12.after), channel_id=1, source_target_pairs={{0,16},{8,24},{16,0},{24,8},{1,17},{9,25},{17,1},{25,9},{2,18},{10... | collective-permute-start | bytes 393224 | tf_op jit(solution)/shard_map/ppermute | solution.py:22
  164.9 9.8 %collective-permute-start.23 = (bf16[128,1024]{1,0:T(8,128)(2,1)S(1)}, bf16[128,1024]{1,0:T(8,128)(2,1)S(1)}, u32[]{:S(2)}, u32[]{:S(2)}) collective-permute-start(bf16[128,1024]{1,0:T(8,128)(2,1)S(1)} %pad_maximum_fusion.1.refs_0_), channel_id=1, source_target_pairs={{0,8},{8,0},{16,24},{24,16},{1,9},{9,1},{17,25},{25,17},{2,10},{10... | collective-permute-start | bytes 786440 | tf_op jit(solution)/shard_map/ppermute | solution.py:22
  167.9 6.8 %collective-permute-start.24 = (bf16[64,1280]{1,0:T(8,128)(2,1)S(1)}, bf16[64,1280]{1,0:T(8,128)(2,1)S(1)}, u32[]{:S(2)}, u32[]{:S(2)}) collective-permute-start(bf16[64,1280]{1,0:T(8,128)(2,1)S(1)} %get-tuple-element.143), channel_id=1, source_target_pairs={{0,16},{8,24},{16,0},{24,8},{1,17},{9,25},{17,1},{25,9},{2,18},{10... | collective-permute-start | bytes 491528 | tf_op jit(solution)/shard_map/ppermute | solution.py:22
  175.0 8.7 %collective-permute-start.25 = (bf16[64,1280]{1,0:T(8,128)(2,1)S(1)}, bf16[64,1280]{1,0:T(8,128)(2,1)S(1)}, u32[]{:S(2)}, u32[]{:S(2)}) collective-permute-start(bf16[64,1280]{1,0:T(8,128)(2,1)S(1)} %fold.15), channel_id=1, source_target_pairs={{0,16},{8,24},{16,0},{24,8},{1,17},{9,25},{17,1},{25,9},{2,18},{10... | collective-permute-start | bytes 491528 | tf_op jit(solution)/shard_map/ppermute | solution.py:22
  183.7 7.1 %collective-permute-start.26 = (bf16[128,1280]{1,0:T(8,128)(2,1)S(1)}, bf16[128,1280]{1,0:T(8,128)(2,1)S(1)}, u32[]{:S(2)}, u32[]{:S(2)}) collective-permute-start(bf16[128,1280]{1,0:T(8,128)(2,1)S(1)} %pad_maximum_fusion.refs_2_), channel_id=1, source_target_pairs={{0,8},{8,0},{16,24},{24,16},{1,9},{9,1},{17,25},{25,17},{2,10},{10... | collective-permute-start | bytes 983048 | tf_op jit(solution)/shard_map/ppermute | solution.py:22

commit v3 on v2

--- a/solution.py
+++ b/solution.py
@@ -10,6 +10,7 @@
 STATE = 64
 GROUP = 256
 LANES = 128
+PROJECTED = 512
 BF = jnp.bfloat16
 F32 = jnp.float32
 precise = lax.Precision.HIGHEST
@@ -96,7 +97,7 @@
         both_ref[rows:, channels - k - GROUP : channels - k] = mm(
             h_ref[:, k : k + GROUP], eye
         ).astype(BF)
-    projected = mm(both_ref[...], ws_ref[...])
+    projected = mm(both_ref[...], ws_ref[...], 1, 1)
     for branch in range(2):
         p = projected[branch * rows : (branch + 1) * rows]
         b, c = p[:, :STATE], p[:, STATE : 2 * STATE]
@@ -145,7 +146,7 @@
         ],
         compiler_params=PARAMS,
         name="small",
-    )(h, ws, log_rates[None], step_bias[None])
+    )(h, ws.T, log_rates[None], step_bias[None])
 
 
 def project_kernel(both_ref, w_ref, bt_ref, weight3_ref, tot3_ref, x_ref, end_ref):
@@ -153,32 +154,35 @@
     rows = x_ref.shape[1]
     heads = weight3_ref.shape[2] // 3
     channels = both_ref.shape[1]
-    copier = spread(heads, channels, at * (GROUP * heads // channels), 3)
     values = mm(both_ref[...], w_ref[...]).astype(BF)
-    for branch in range(2):
-        x = values[branch * rows : (branch + 1) * rows]
-        x_ref[branch] = x
-        weighted = mm(weight3_ref[branch], copier) * x.astype(F32)
-        both = mm(bt_ref[branch], weighted.astype(BF))
-        end_ref[branch, :STATE] = both[:STATE] + both[STATE:]
-        end_ref[branch, STATE:] = mm(tot3_ref[branch], copier)
+    for part in range(PROJECTED // GROUP):
+        here = slice(part * GROUP, (part + 1) * GROUP)
+        group = at * (PROJECTED // GROUP) + part
+        copier = spread(heads, channels, group * (GROUP * heads // channels), 3)
+        for branch in range(2):
+            x = values[branch * rows : (branch + 1) * rows, here]
+            x_ref[branch, :, here] = x
+            weighted = mm(weight3_ref[branch], copier) * x.astype(F32)
+            both = mm(bt_ref[branch], weighted.astype(BF))
+            end_ref[branch, :STATE, here] = both[:STATE] + both[STATE:]
+            end_ref[branch, STATE:, here] = mm(tot3_ref[branch], copier)
 
 
 def project(both, w, bt, weight3, tot3):
     rows, channels = both.shape[0] // 2, both.shape[1]
     return pl.pallas_call(
         project_kernel,
-        grid=(channels // GROUP,),
+        grid=(channels // PROJECTED,),
         in_specs=[
             whole(both),
-            pl.BlockSpec((channels, GROUP), lambda j: (0, j)),
+            pl.BlockSpec((channels, PROJECTED), lambda j: (0, j)),
             whole(bt),
             whole(weight3),
             whole(tot3),
         ],
         out_specs=[
-            pl.BlockSpec((2, rows, GROUP), lambda j: (0, 0, j)),
-            pl.BlockSpec((2, STATE + 8, GROUP), lambda j: (0, 0, j)),
+            pl.BlockSpec((2, rows, PROJECTED), lambda j: (0, 0, j)),
+            pl.BlockSpec((2, STATE + 8, PROJECTED), lambda j: (0, 0, j)),
         ],
         out_shape=[
             jax.ShapeDtypeStruct((2, rows, channels), BF),

time: 194 us -> 194 us (level)
    unnamed x68 -> x69, local copies, waits for them, and re-layouts: 13.4 us -> 13 us
where the time goes in v3:
time: 194 us; the launch traced here: 193 us
  Pallas kernels  89.6 us (46%)
  waiting for transfers between devices  56.1 us (29%)
  starting transfers between devices  32.7 us (17%)
  local copies, waits for them, and re-layouts  13.3 us (7%)
    ppermute x27, waiting for transfers between devices, send(): lax.ppermute(array, axis, [(i, i ^ mask) for i in range(lax.axis_size(axi...  56.1 us
    ppermute x27, starting transfers between devices, send(): lax.ppermute(array, axis, [(i, i ^ mask) for i in range(lax.axis_size(axi...  32.7 us
    pallas_call x4, Pallas kernels, weight_terms(): pl.pallas_call(functools.partial(term_kernel, picked, pieces), grid=(own....  14.7 us
    unnamed x69, local copies, waits for them, and re-layouts  13 us
    pallas_call x2, Pallas kernels, finish(): pl.pallas_call(functools.partial(finish_kernel, first, len(arrived), last...  12.7 us
    pallas_call x1, Pallas kernels, inner_back(): pl.pallas_call(inner_back_kernel, grid=(channels // GROUP,), in_specs=[bl...  12.3 us
    pallas_call x1, Pallas kernels, normed(): pl.pallas_call(functools.partial(normed_kernel, len(arrived), heads), gri...  11.4 us
    pallas_call x1, Pallas kernels, project(): pl.pallas_call(project_kernel, grid=(channels // PROJECTED,), in_specs=[w...  11 us
  transfers between devices with their start and end apart: 27, of which 17 were waited for; matrix products, arithmetic and copies ran while one was open for 0% of the time, Pallas kernels for 26%

profile of v3, /device:TPU:0, one launch (start us, length us, event | category | flops | bytes accessed | tf_op | source)
XLA Modules:
  0.0 192.9 jit_solution(11250225288637540268)
XLA Ops:
  0.6 1.1 copy-done.21
  1.7 0.7 copy-done.29
  2.4 0.7 copy-done.31
  3.0 3.9 %small.1 = (bf16[512,2048]{1,0:T(8,128)(2,1)S(1)}, f32[2,256,384]{2,1,0:T(8,128)S(1)}, f32[2,64,256]{2,1,0:T(8,128)S(1)}, bf16[2,256,384]{2,1,0:T(8,128)(2,1)S(1...) custom-call(bf16[256,2048]{1,0:T(8,128)(2,1)} %bitcast.h_ref.own_ref, ...), custom_call_target="tpu_custom_call" | custom-call | tf_op jit(solution)/shard_map/small/pallas_call | solution.py:135
  6.9 11.0 %project.1 = (bf16[2,256,2048]{2,1,0:T(8,128)(2,1)S(1)}, f32[2,72,2048]{2,1,0:T(8,128)S(1)}) custom-call(bf16[512,2048]{1,0:T(8,128)(2,1)S(1)} %get-tuple-element.76.both_ref, bf16[2048,2048]{1,0:T(8,128)(2,1)} %w_ref.1, bf16[2,128,256]{2,1,0:T(8,128)(2,1)S(1)} %get-tuple-element.77.bt_ref, bf16[2,256,96]{2,1,0:T(8,128)(2,1)S(1)} %get-tuple-element.78.weight3_ref, ...), custom_call_target="tpu_custom_call" | custom-call | tf_op jit(solution)/shard_map/project/pallas_call | solution.py:173
  18.0 1.3 copy-done
  20.2 6.5 %inner.2.after.raw_fwd_ref = f32[256,2048]{1,0:T(8,128)S(1)} custom-call(bf16[2,256,2048]{2,1,0:T(8,128)(2,1)} %copy-done, f32[2,256,384]{2,1,0:T(8,128)S(1)} %get-tuple-element.81.nat_ref.nat_fwd_ref.nat_rc_ref.refs_12_, f32[2,64,256]{2,1,0:T(8,128)S(1)} %get-tuple-element.82.lines_ref, f32[2,72,2048]{2,1,0:T(8,128)S(1)} %get-tuple-element.83.after.refs_0_.own_ref.refs_4_), custom_call_target="tpu_custom_call" | custom-call | tf_op jit(solution)/shard_map/inner/pallas_call | solution.py:235
  26.7 0.9 merge.2
  28.4 3.9 %collective-permute-start.4 = (bf16[80,2048]{1,0:T(8,128)(2,1)S(1)}, bf16[80,2048]{1,0:T(8,128)(2,1)S(1)}, u32[]{:S(2)}, u32[]{:S(2)}) collective-permute-start(bf16[80,2048]{1,0:T(8,128)(2,1)S(1)} %get-tuple-element.86), channel_id=1, source_target_pairs={{0,6},{1,7},{2,4},{3,5},{4,2},{5,3},{6,0},{7,1},{8,14},{9,15},{10,... | collective-permute-start | bytes 983048 | tf_op jit(solution)/shard_map/ppermute | solution.py:23
  32.9 4.4 %turned.1.after.left_ref = bf16[1024,1024]{1,0:T(8,128)(2,1)S(1)} custom-call(s32[8]{0:T(128)S(1)} %pad_add_fusion.where_ref, bf16[256,2048]{1,0:T(8,128)(2,1)} %bitcast.h_ref.own_ref.own_mirror_ref, bf16[256,2048]{1,0:T(8,128)(2,1)} %bitcast.h_ref.own_ref.own_mirror_ref, bf16[256,2048]{1,0:T(8,128)(2,1)} %collective-permute-done.peer_ref.peer_mirror_ref, ...), custom_call_target="tpu_custom_call" | custom-call | tf_op jit(solution)/shard_map/turned/pallas_call | solution.py:674
  37.3 1.3 copy-done.3
  38.7 4.5 %inner.3.raw_rc_ref = f32[256,2048]{1,0:T(8,128)S(1)} custom-call(bf16[2,256,2048]{2,1,0:T(8,128)(2,1)S(1)} %copy-done.1, f32[2,256,384]{2,1,0:T(8,128)S(1)} %copy-done.7, f32[2,64,256]{2,1,0:T(8,128)S(1)} %get-tuple-element.82.lines_ref, bf16[1024,1024]{1,0:T(8,128)(2,1)} %copy-done.3), custom_call_target="tpu_custom_call" | custom-call | tf_op jit(solution)/shard_map/inner/pallas_call | solution.py:235
  43.2 1.4 copy-done.13
  44.5 2.9 %collective-permute-done.2.refs_0_ = bf16[80,2048]{1,0:T(8,128)(2,1)S(1)} collective-permute-done((bf16[80,2048]{1,0:T(8,128)(2,1)S(1)}, bf16[80,2048]{1,0:T(8,128)(2,1)S(1)}, u32[]{:S(2)}, u32[]{:S(2)}) %collective-permute-start.2) | collective-permute-done | bytes 327712 | tf_op jit(solution)/shard_map/ppermute | solution.py:23
  47.5 11.4 %normed.1 = (bf16[256,2048]{1,0:T(8,128)(2,1)}, bf16[2,256,2048]{2,1,0:T(8,128)(2,1)}, f32[2,256,32]{2,1,0:T(8,128)S(1)}, f32[2,64,2048]{2,1,0:T(8,128)S(1)}, f3...) custom-call(f32[256,2048]{1,0:T(8,128)} %copy-done.8, ...), custom_call_target="tpu_custom_call" | custom-call | tf_op jit(solution)/shard_map/normed/pallas_call | solution.py:425
  58.9 1.0 copy-done.15
  59.9 2.7 %collective-permute-done.5.refs_2_.refs_7_ = f32[2,64,2048]{2,1,0:T(8,128)S(1)} collective-permute-done((f32[2,64,2048]{2,1,0:T(8,128)S(1)}, f32[2,64,2048]{2,1,0:T(8,128)S(1)}, u32[]{:S(2)}, u32[]{:S(2)}) %collective-permute-start.5) | collective-permute-done | bytes 1048608 | tf_op jit(solution)/shard_map/ppermute | solution.py:23
  62.6 1.6 merge.3
  64.2 1.0 copy-done.11
  65.2 1.5 collective-permute-start.6
  66.6 1.4 collective-permute-start.8
  68.0 0.6 collective-permute-start.7
  68.7 1.6 copy-done.17
  70.3 12.3 %inner_back.1 = (f32[2,256,2048]{2,1,0:T(8,128)}, f32[2,256,64]{2,1,0:T(8,128)S(1)}, f32[2,256,64]{2,1,0:T(8,128)S(1)}) custom-call(bf16[2,256,2048]{2,1,0:T(8,128)(2,1)S(1)} %copy-done.2, bf16[2,256,2048]{2,1,0:T(8,128)(2,1)S(1)} %copy-done.17, f32[2,256,384]{2,1,0:T(8,128)S(1)} %copy-done.7, f32[2,64,256]{2,1,0:T(8,128)S(1)} %get-tuple-element.82.lines_ref, ...), custom_call_target="tpu_custom_call" | custom-call | tf_op jit(solution)/shard_map/inner_back/pallas_call | solution.py:525
  82.6 5.5 %finish.2 = (bf16[512,1024]{1,0:T(8,128)(2,1)S(1)}, f32[2,256,64]{2,1,0:T(8,128)S(1)}, f32[2,256,32]{2,1,0:T(8,128)S(1)}, f32[2,1,32]{2,1,0:T(1,128)S(1)}) custom-call(bf16[2,256,2048]{2,1,0:T(8,128)(2,1)} %copy-done, f32[2,256,2048]{2,1,0:T(8,128)} %get-tuple-element.93.refs_1_, bf16[2,256,384]{2,1,0:T(8,128)(2,1)S(1)} %copy-done.19, ...), custom_call_target="tpu_custom_call" | custom-call | tf_op jit(solution)/shard_map/finish/pallas_call | solution.py:630
  88.2 2.6 %collective-permute-done.9.peer_ref = bf16[512,1024]{1,0:T(8,128)(2,1)S(1)} collective-permute-done((bf16[512,1024]{1,0:T(8,128)(2,1)S(1)}, bf16[512,1024]{1,0:T(8,128)(2,1)S(1)}, u32[]{:S(2)}, u32[]{:S(2)}) %collective-permute-start.9) | collective-permute-done | bytes 1048608 | tf_op jit(solution)/shard_map/ppermute | solution.py:23
  90.9 2.3 %terms.4 = (bf16[512,512]{1,0:T(8,128)(2,1)S(1)}, bf16[512,512]{1,0:T(8,128)(2,1)S(1)}) custom-call(bf16[1024,1024]{1,0:T(8,128)(2,1)S(1)} %copy-done.4, bf16[512,1024]{1,0:T(8,128)(2,1)S(1)} %get-tuple-element.98.own_ref, bf16[512,1024]{1,0:T(8,128)(2,1)S(1)} %collective-permute-done.9.peer_ref, f32[2,1,32]{2,1,0:T(1,128)S(1)} %get-tuple-element.99.after.refs_20_), custom_call_target="tpu_custom_call" | custom-call | tf_op jit(solution)/shard_map/terms/pallas_call | solution.py:728
  93.2 1.5 collective-permute-start.11
  94.7 0.6 collective-permute-start.10
  95.3 7.2 %finish.3 = (bf16[512,1280]{1,0:T(8,128)(2,1)}, f32[2,256,64]{2,1,0:T(8,128)}, f32[2,256,32]{2,1,0:T(8,128)}, f32[2,1,32]{2,1,0:T(1,128)}) custom-call(bf16[2,256,2048]{2,1,0:T(8,128)(2,1)} %copy-done, f32[2,256,2048]{2,1,0:T(8,128)} %get-tuple-element.93.refs_1_, bf16[2,256,384]{2,1,0:T(8,128)(2,1)S(1)} %copy-done.19, f32[2,64,2048]{2,1,0:T(8,128)S(1)} %copy-done.16, ...), custom_call_target="tpu_custom_call" | custom-call | tf_op jit(solution)/shard_map/finish/pallas_call | solution.py:630
  102.4 4.8 %collective-permute-done.11.refs_3_ = bf16[512,512]{1,0:T(8,128)(2,1)S(1)} collective-permute-done((bf16[512,512]{1,0:T(8,128)(2,1)S(1)}, bf16[512,512]{1,0:T(8,128)(2,1)S(1)}, u32[]{:S(2)}, u32[]{:S(2)}) %collective-permute-start.11) | collective-permute-done | bytes 524320 | tf_op jit(solution)/shard_map/ppermute | solution.py:23
  107.2 1.1 collective-permute-done.10.refs_1_
  108.4 1.3 copy-done.9
  109.7 3.9 %terms.5 = (f32[512,512]{1,0:T(8,128)S(1)}, f32[512,512]{1,0:T(8,128)S(1)}) custom-call(bf16[1024,1024]{1,0:T(8,128)(2,1)} %copy-done.3, bf16[512,1024]{1,0:T(8,128)(2,1)S(1)} %get-tuple-element.98.own_ref, bf16[512,1024]{1,0:T(8,128)(2,1)S(1)} %collective-permute-done.9.peer_ref, bf16[512,1280]{1,0:T(8,128)(2,1)S(1)} %copy-done.9), custom_call_target="tpu_custom_call" | custom-call | tf_op jit(solution)/shard_map/terms/pallas_call | solution.py:728
  113.6 0.8 fold.8
  114.4 0.7 collective-permute-start.13
  115.1 1.5 collective-permute-start.14
  116.6 4.2 %terms.6 = (bf16[512,512]{1,0:T(8,128)(2,1)S(1)}, bf16[512,768]{1,0:T(8,128)(2,1)S(1)}) custom-call(bf16[1024,1024]{1,0:T(8,128)(2,1)} %copy-done.3, bf16[512,1280]{1,0:T(8,128)(2,1)S(1)} %copy-done.10, bf16[512,1280]{1,0:T(8,128)(2,1)S(1)} %collective-permute-done.12.peer_ref, f32[256,512]{1,0:T(8,128)S(1)} %get-tuple-element.113.after.refs_0_), custom_call_target="tpu_custom_call" | custom-call | tf_op jit(solution)/shard_map/terms/pallas_call | solution.py:728
  120.8 2.3 %collective-permute-done.13.refs_1_ = bf16[256,512]{1,0:T(8,128)(2,1)S(1)} collective-permute-done((bf16[256,512]{1,0:T(8,128)(2,1)S(1)}, bf16[256,512]{1,0:T(8,128)(2,1)S(1)}, u32[]{:S(2)}, u32[]{:S(2)}) %collective-permute-start.13) | collective-permute-done | bytes 262176 | tf_op jit(solution)/shard_map/ppermute | solution.py:23
  123.5 1.4 collective-permute-start.17
  124.9 0.6 collective-permute-start.16
  126.0 1.8 collective-permute-start.15
  127.8 4.3 %terms.7 = (f32[512,512]{1,0:T(8,128)S(1)}, f32[512,768]{1,0:T(8,128)S(1)}) custom-call(bf16[1024,1024]{1,0:T(8,128)(2,1)} %copy-done.3, bf16[512,1280]{1,0:T(8,128)(2,1)S(1)} %copy-done.10, bf16[512,1280]{1,0:T(8,128)(2,1)S(1)} %collective-permute-done.12.peer_ref, f32[128,1024]{1,0:T(8,128)S(1)} %get-tuple-element.121.after.refs_0_), custom_call_target="tpu_custom_call" | custom-call | tf_op jit(solution)/shard_map/terms/pallas_call | solution.py:728
  132.1 1.1 collective-permute-done.15.refs_1_
  133.2 4.7 %collective-permute-done.16.refs_1_ = bf16[512,512]{1,0:T(8,128)(2,1)S(1)} collective-permute-done((bf16[512,512]{1,0:T(8,128)(2,1)S(1)}, bf16[512,512]{1,0:T(8,128)(2,1)S(1)}, u32[]{:S(2)}, u32[]{:S(2)}) %collective-permute-start.16) | collective-permute-done | bytes 524320 | tf_op jit(solution)/shard_map/ppermute | solution.py:23
  137.9 4.5 %collective-permute-done.17.refs_3_ = bf16[512,768]{1,0:T(8,128)(2,1)S(1)} collective-permute-done((bf16[512,768]{1,0:T(8,128)(2,1)S(1)}, bf16[512,768]{1,0:T(8,128)(2,1)S(1)}, u32[]{:S(2)}, u32[]{:S(2)}) %collective-permute-start.17) | collective-permute-done | bytes 786464 | tf_op jit(solution)/shard_map/ppermute | solution.py:23
  142.7 1.0 fold.11
  143.6 1.5 collective-permute-start.20
  145.2 0.6 collective-permute-start.19
  145.8 2.7 %collective-permute-start.18 = (bf16[64,1024]{1,0:T(8,128)(2,1)S(1)}, bf16[64,1024]{1,0:T(8,128)(2,1)S(1)}, u32[]{:S(2)}, u32[]{:S(2)}) collective-permute-start(bf16[64,1024]{1,0:T(8,128)(2,1)S(1)} %get-tuple-element.132), channel_id=1, source_target_pairs={{0,16},{8,24},{16,0},{24,8},{1,17},{9,25},{17,1},{25,9},{2,18},{10... | collective-permute-start | bytes 393224 | tf_op jit(solution)/shard_map/ppermute | solution.py:23
  148.5 4.6 %collective-permute-done.18.refs_1_ = bf16[64,1024]{1,0:T(8,128)(2,1)S(1)} collective-permute-done((bf16[64,1024]{1,0:T(8,128)(2,1)S(1)}, bf16[64,1024]{1,0:T(8,128)(2,1)S(1)}, u32[]{:S(2)}, u32[]{:S(2)}) %collective-permute-start.18) | collective-permute-done | bytes 131104 | tf_op jit(solution)/shard_map/ppermute | solution.py:23
  153.4 0.6 fold.13
  154.0 1.6 collective-permute-start.22
  155.7 2.6 %collective-permute-start.21 = (bf16[64,1024]{1,0:T(8,128)(2,1)S(1)}, bf16[64,1024]{1,0:T(8,128)(2,1)S(1)}, u32[]{:S(2)}, u32[]{:S(2)}) collective-permute-start(bf16[64,1024]{1,0:T(8,128)(2,1)S(1)} %fold.12.after), channel_id=1, source_target_pairs={{0,16},{8,24},{16,0},{24,8},{1,17},{9,25},{17,1},{25,9},{2,18},{10... | collective-permute-start | bytes 393224 | tf_op jit(solution)/shard_map/ppermute | solution.py:23
  158.3 4.9 %collective-permute-done.21 = bf16[64,1024]{1,0:T(8,128)(2,1)S(1)} collective-permute-done((bf16[64,1024]{1,0:T(8,128)(2,1)S(1)}, bf16[64,1024]{1,0:T(8,128)(2,1)S(1)}, u32[]{:S(2)}, u32[]{:S(2)}) %collective-permute-start.21) | collective-permute-done | bytes 131104 | tf_op jit(solution)/shard_map/ppermute | solution.py:23
  163.2 0.9 collective-permute-done.22.refs_1_
  164.2 2.6 %collective-permute-start.23 = (bf16[128,1024]{1,0:T(8,128)(2,1)S(1)}, bf16[128,1024]{1,0:T(8,128)(2,1)S(1)}, u32[]{:S(2)}, u32[]{:S(2)}) collective-permute-start(bf16[128,1024]{1,0:T(8,128)(2,1)S(1)} %pad_maximum_fusion.1.refs_0_), channel_id=1, source_target_pairs={{0,8},{8,0},{16,24},{24,16},{1,9},{9,1},{17,25},{25,17},{2,10},{10... | collective-permute-start | bytes 786440 | tf_op jit(solution)/shard_map/ppermute | solution.py:23
  167.1 1.6 collective-permute-start.24
  168.8 5.2 %collective-permute-done.24.refs_1_ = bf16[64,1280]{1,0:T(8,128)(2,1)S(1)} collective-permute-done((bf16[64,1280]{1,0:T(8,128)(2,1)S(1)}, bf16[64,1280]{1,0:T(8,128)(2,1)S(1)}, u32[]{:S(2)}, u32[]{:S(2)}) %collective-permute-start.24) | collective-permute-done | bytes 163872 | tf_op jit(solution)/shard_map/ppermute | solution.py:23
  174.2 2.5 %collective-permute-start.25 = (bf16[64,1280]{1,0:T(8,128)(2,1)S(1)}, bf16[64,1280]{1,0:T(8,128)(2,1)S(1)}, u32[]{:S(2)}, u32[]{:S(2)}) collective-permute-start(bf16[64,1280]{1,0:T(8,128)(2,1)S(1)} %fold.15), channel_id=1, source_target_pairs={{0,16},{8,24},{16,0},{24,8},{1,17},{9,25},{17,1},{25,9},{2,18},{10... | collective-permute-start | bytes 491528 | tf_op jit(solution)/shard_map/ppermute | solution.py:23
  176.7 6.2 %collective-permute-done.25 = bf16[64,1280]{1,0:T(8,128)(2,1)S(1)} collective-permute-done((bf16[64,1280]{1,0:T(8,128)(2,1)S(1)}, bf16[64,1280]{1,0:T(8,128)(2,1)S(1)}, u32[]{:S(2)}, u32[]{:S(2)}) %collective-permute-start.25) | collective-permute-done | bytes 163872 | tf_op jit(solution)/shard_map/ppermute | solution.py:23
  183.2 6.9 %collective-permute-done.26.refs_3_ = bf16[128,1280]{1,0:T(8,128)(2,1)S(1)} collective-permute-done((bf16[128,1280]{1,0:T(8,128)(2,1)S(1)}, bf16[128,1280]{1,0:T(8,128)(2,1)S(1)}, u32[]{:S(2)}, u32[]{:S(2)}) %collective-permute-start.26) | collective-permute-done | bytes 327712 | tf_op jit(solution)/shard_map/ppermute | solution.py:23
  190.1 2.0 %placed.1 = (f32[256,2048]{1,0:T(8,128)}, f32[256,160]{1,0:T(8,128)S(1)}) custom-call(s32[8]{0:T(128)S(1)} %pad_add_fusion.where_ref, bf16[128,1024]{1,0:T(8,128)(2,1)S(1)} %pad_maximum_fusion.1.refs_0_, bf16[128,1024]{1,0:T(8,128)(2,1)S(1)} %collective-permute-done.23.refs_1_, bf16[128,1280]{1,0:T(8,128)(2,1)S(1)} %pad_maximum_fusion.refs_2_, ...), custom_call_target="tpu_custom_call" | custom-call | tf_op jit(solution)/shard_map/placed/pallas_call | solution.py:826
  192.1 0.8 copy.12
  (96 shorter events, 4.9 us)
Async XLA Ops:
  0.6 1.1 copy-start.21
  1.7 0.7 copy-start.29
  2.4 0.7 copy-start.31
  6.9 11.0 %copy-start.18 = (bf16[2,256,384]{2,1,0:T(8,128)(2,1)}, bf16[2,256,384]{2,1,0:T(8,128)(2,1)S(1)}, u32[]{:S(2)}) copy-start(bf16[2,256,384]{2,1,0:T(8,128)(2,1)S(1)} %get-tuple-element.94.refs_2_) | copy-start | bytes 1179652
  6.9 11.0 %copy-start.22 = (bf16[2,256,384]{2,1,0:T(8,128)(2,1)}, bf16[2,256,384]{2,1,0:T(8,128)(2,1)S(1)}, u32[]{:S(2)}) copy-start(bf16[2,256,384]{2,1,0:T(8,128)(2,1)S(1)} %get-tuple-element.85.cg3_ref) | copy-start | bytes 1179652
  6.9 13.3 %copy-start.6 = (f32[2,256,384]{2,1,0:T(8,128)}, f32[2,256,384]{2,1,0:T(8,128)S(1)}, u32[]{:S(2)}) copy-start(f32[2,256,384]{2,1,0:T(8,128)S(1)} %get-tuple-element.81.nat_ref.nat_fwd_ref.nat_rc_ref.refs_12_) | copy-start | bytes 2359300
  6.9 13.1 %copy-start.33 = (s32[2]{0:T(128)S(1)}, s32[2]{0:T(128)}, u32[]{:S(2)}) copy-start(s32[2]{0:T(128)} %constant.42.clone) | copy-start | bytes 28
  18.0 1.3 copy-start
  19.3 7.4 %copy-start.5 = (f32[2,72,2048]{2,1,0:T(8,128)}, f32[2,72,2048]{2,1,0:T(8,128)S(1)}, u32[]{:S(2)}) copy-start(f32[2,72,2048]{2,1,0:T(8,128)S(1)} %get-tuple-element.83.after.refs_0_.own_ref.refs_4_) | copy-start | bytes 3538948
  19.3 7.4 %collective-permute-start.1 = (f32[2,72,2048]{2,1,0:T(8,128)S(1)}, f32[2,72,2048]{2,1,0:T(8,128)S(1)}, u32[]{:S(2)}, u32[]{:S(2)}) collective-permute-start(f32[2,72,2048]{2,1,0:T(8,128)S(1)} %get-tuple-element.83.after.refs_0_.own_ref.refs_4_), channel_id=1, source_target_pairs={{0,1},{1,0},{2,3},{3,2},{4,5},{5,4},{6,7},{7,6},{8,9},{9,8},{10,11... | collective-permute-start | bytes 3538952 | tf_op jit(solution)/shard_map/ppermute | solution.py:23
  19.7 13.2 %collective-permute-start = (bf16[256,2048]{1,0:T(8,128)(2,1)}, bf16[256,2048]{1,0:T(8,128)(2,1)}, u32[]{:S(2)}, u32[]{:S(2)}) collective-permute-start(bf16[256,2048]{1,0:T(8,128)(2,1)} %bitcast.h_ref.own_ref.own_mirror_ref), channel_id=1, source_target_pairs={{0,1},{1,0},{2,3},{3,2},{4,5},{5,4},{6,7},{7,6},{8,9},{9,8},{10,11... | collective-permute-start | bytes 3145736 | tf_op jit(solution)/shard_map/ppermute | solution.py:23
  26.7 1.4 copy-start.8
  26.7 6.2 %copy-start.32 = (s32[4]{0:T(128)S(1)}, s32[4]{0:T(128)}, u32[]{:S(2)}) copy-start(s32[4]{0:T(128)} %constant.43.clone) | copy-start | bytes 52
  26.7 1.7 copy-start.14
  28.4 19.1 %collective-permute-start.4 = (bf16[80,2048]{1,0:T(8,128)(2,1)S(1)}, bf16[80,2048]{1,0:T(8,128)(2,1)S(1)}, u32[]{:S(2)}, u32[]{:S(2)}) collective-permute-start(bf16[80,2048]{1,0:T(8,128)(2,1)S(1)} %get-tuple-element.86), channel_id=1, source_target_pairs={{0,6},{1,7},{2,4},{3,5},{4,2},{5,3},{6,0},{7,1},{8,14},{9,15},{10,... | collective-permute-start | bytes 983048 | tf_op jit(solution)/shard_map/ppermute | solution.py:23
  32.3 15.2 %collective-permute-start.3 = (bf16[80,2048]{1,0:T(8,128)(2,1)S(1)}, bf16[80,2048]{1,0:T(8,128)(2,1)S(1)}, u32[]{:S(2)}, u32[]{:S(2)}) collective-permute-start(bf16[80,2048]{1,0:T(8,128)(2,1)S(1)} %get-tuple-element.86), channel_id=1, source_target_pairs={{0,4},{1,5},{2,6},{3,7},{4,0},{5,1},{6,2},{7,3},{8,12},{9,13},{10,... | collective-permute-start | bytes 983048 | tf_op jit(solution)/shard_map/ppermute | solution.py:23
  32.8 14.7 %collective-permute-start.2 = (bf16[80,2048]{1,0:T(8,128)(2,1)S(1)}, bf16[80,2048]{1,0:T(8,128)(2,1)S(1)}, u32[]{:S(2)}, u32[]{:S(2)}) collective-permute-start(bf16[80,2048]{1,0:T(8,128)(2,1)S(1)} %get-tuple-element.84.after), channel_id=1, source_target_pairs={{0,2},{1,3},{2,0},{3,1},{4,6},{5,7},{6,4},{7,5},{8,10},{9,11},{10,... | collective-permute-start | bytes 983048 | tf_op jit(solution)/shard_map/ppermute | solution.py:23
  32.9 5.7 %copy-start.1 = (bf16[2,256,2048]{2,1,0:T(8,128)(2,1)S(1)}, bf16[2,256,2048]{2,1,0:T(8,128)(2,1)}, u32[]{:S(2)}) copy-start(bf16[2,256,2048]{2,1,0:T(8,128)(2,1)} %copy-done) | copy-start | bytes 6291460
  32.9 5.7 %copy-start.7 = (f32[2,256,384]{2,1,0:T(8,128)S(1)}, f32[2,256,384]{2,1,0:T(8,128)}, u32[]{:S(2)}) copy-start(f32[2,256,384]{2,1,0:T(8,128)} %copy-done.6) | copy-start | bytes 2359300
  37.3 1.4 copy-start.3
  38.7 8.8 %copy-start.20 = (bf16[1,256,2048]{2,1,0:T(8,128)(2,1)S(1)}, bf16[1,256,2048]{2,1,0:T(8,128)(2,1)}, u32[]{:S(2)}) copy-start(bf16[1,256,2048]{2,1,0:T(8,128)(2,1)} %param.15) | copy-start | bytes 3145732
  38.7 8.8 %copy-start.23 = (bf16[2,256,384]{2,1,0:T(8,128)(2,1)S(1)}, bf16[2,256,384]{2,1,0:T(8,128)(2,1)}, u32[]{:S(2)}) copy-start(bf16[2,256,384]{2,1,0:T(8,128)(2,1)} %copy-done.22) | copy-start | bytes 1179652
  38.7 8.8 %copy-start.28 = (f32[2048]{0:T(1024)S(1)}, f32[2048]{0:T(1024)}, u32[]{:S(2)}) copy-start(f32[2048]{0:T(1024)} %param.14) | copy-start | bytes 24580
  43.2 1.4 copy-start.13
  58.9 1.0 copy-start.15
  59.9 4.2 %copy-start.24 = (f32[2,256,32]{2,1,0:T(8,128)}, f32[2,256,32]{2,1,0:T(8,128)S(1)}, u32[]{:S(2)}) copy-start(f32[2,256,32]{2,1,0:T(8,128)S(1)} %get-tuple-element.103.refs_16_) | copy-start | bytes 196612
  59.9 5.2 %copy-start.26 = (f32[2,256,64]{2,1,0:T(8,128)}, f32[2,256,64]{2,1,0:T(8,128)S(1)}, u32[]{:S(2)}) copy-start(f32[2,256,64]{2,1,0:T(8,128)S(1)} %get-tuple-element.102.refs_15_) | copy-start | bytes 393220
  59.9 8.8 %copy-start.2 = (bf16[2,256,2048]{2,1,0:T(8,128)(2,1)S(1)}, bf16[2,256,2048]{2,1,0:T(8,128)(2,1)}, u32[]{:S(2)}) copy-start(bf16[2,256,2048]{2,1,0:T(8,128)(2,1)} %copy-done) | copy-start | bytes 6291460
  59.9 2.7 %collective-permute-start.5 = (f32[2,64,2048]{2,1,0:T(8,128)S(1)}, f32[2,64,2048]{2,1,0:T(8,128)S(1)}, u32[]{:S(2)}, u32[]{:S(2)}) collective-permute-start(f32[2,64,2048]{2,1,0:T(8,128)S(1)} %get-tuple-element.90.after.refs_1_), channel_id=1, source_target_pairs={{0,1},{1,0},{2,3},{3,2},{4,5},{5,4},{6,7},{7,6},{8,9},{9,8},{10,11... | collective-permute-start | bytes 3145736 | tf_op jit(solution)/shard_map/ppermute | solution.py:23
  64.2 1.0 copy-start.11
  65.2 17.4 %collective-permute-start.6 = (bf16[64,2048]{1,0:T(8,128)(2,1)}, bf16[64,2048]{1,0:T(8,128)(2,1)S(1)}, u32[]{:S(2)}, u32[]{:S(2)}) collective-permute-start(bf16[64,2048]{1,0:T(8,128)(2,1)} %get-tuple-element.92.after), channel_id=1, source_target_pairs={{0,2},{1,3},{2,0},{3,1},{4,6},{5,7},{6,4},{7,5},{8,10},{9,11},{10,... | collective-permute-start | bytes 786440 | tf_op jit(solution)/shard_map/ppermute | solution.py:23
  66.6 15.9 %collective-permute-start.8 = (bf16[64,2048]{1,0:T(8,128)(2,1)}, bf16[64,2048]{1,0:T(8,128)(2,1)}, u32[]{:S(2)}, u32[]{:S(2)}) collective-permute-start(bf16[64,2048]{1,0:T(8,128)(2,1)} %get-tuple-element.96), channel_id=1, source_target_pairs={{0,6},{1,7},{2,4},{3,5},{4,2},{5,3},{6,0},{7,1},{8,14},{9,15},{10,... | collective-permute-start | bytes 786440 | tf_op jit(solution)/shard_map/ppermute | solution.py:23
  68.0 14.6 %collective-permute-start.7 = (bf16[64,2048]{1,0:T(8,128)(2,1)}, bf16[64,2048]{1,0:T(8,128)(2,1)}, u32[]{:S(2)}, u32[]{:S(2)}) collective-permute-start(bf16[64,2048]{1,0:T(8,128)(2,1)} %get-tuple-element.96), channel_id=1, source_target_pairs={{0,4},{1,5},{2,6},{3,7},{4,0},{5,1},{6,2},{7,3},{8,12},{9,13},{10,... | collective-permute-start | bytes 786440 | tf_op jit(solution)/shard_map/ppermute | solution.py:23
  68.7 1.6 copy-start.17
  70.3 12.3 %copy-start.12 = (f32[2,64,2048]{2,1,0:T(8,128)S(1)}, f32[2,64,2048]{2,1,0:T(8,128)}, u32[]{:S(2)}) copy-start(f32[2,64,2048]{2,1,0:T(8,128)} %copy-done.11) | copy-start | bytes 3145732
  70.3 12.3 %copy-start.16 = (f32[2,64,2048]{2,1,0:T(8,128)S(1)}, f32[2,64,2048]{2,1,0:T(8,128)}, u32[]{:S(2)}) copy-start(f32[2,64,2048]{2,1,0:T(8,128)} %copy-done.15) | copy-start | bytes 3145732
  70.3 12.3 %copy-start.19 = (bf16[2,256,384]{2,1,0:T(8,128)(2,1)S(1)}, bf16[2,256,384]{2,1,0:T(8,128)(2,1)}, u32[]{:S(2)}) copy-start(bf16[2,256,384]{2,1,0:T(8,128)(2,1)} %copy-done.18) | copy-start | bytes 1179652
  82.6 8.3 %copy-start.4 = (bf16[1024,1024]{1,0:T(8,128)(2,1)S(1)}, bf16[1024,1024]{1,0:T(8,128)(2,1)}, u32[]{:S(2)}) copy-start(bf16[1024,1024]{1,0:T(8,128)(2,1)} %copy-done.3) | copy-start | bytes 6291460
  88.1 2.7 %collective-permute-start.9 = (bf16[512,1024]{1,0:T(8,128)(2,1)S(1)}, bf16[512,1024]{1,0:T(8,128)(2,1)S(1)}, u32[]{:S(2)}, u32[]{:S(2)}) collective-permute-start(bf16[512,1024]{1,0:T(8,128)(2,1)S(1)} %get-tuple-element.98.own_ref), channel_id=1, source_target_pairs={{0,1},{1,0},{2,3},{3,2},{4,5},{5,4},{6,7},{7,6},{8,9},{9,8},{10,11... | collective-permute-start | bytes 3145736 | tf_op jit(solution)/shard_map/ppermute | solution.py:23
  90.9 4.4 %copy-start.25 = (f32[2,256,32]{2,1,0:T(8,128)S(1)}, f32[2,256,32]{2,1,0:T(8,128)}, u32[]{:S(2)}) copy-start(f32[2,256,32]{2,1,0:T(8,128)} %copy-done.24) | copy-start | bytes 196612
  90.9 4.4 %copy-start.27 = (f32[2,256,64]{2,1,0:T(8,128)S(1)}, f32[2,256,64]{2,1,0:T(8,128)}, u32[]{:S(2)}) copy-start(f32[2,256,64]{2,1,0:T(8,128)} %copy-done.26) | copy-start | bytes 393220
  90.9 4.4 %copy-start.30 = (f32[32]{0:T(128)S(1)}, f32[32]{0:T(128)}, u32[]{:S(2)}) copy-start(f32[32]{0:T(128)} %param.12) | copy-start | bytes 388
  93.2 14.0 %collective-permute-start.11 = (bf16[512,512]{1,0:T(8,128)(2,1)S(1)}, bf16[512,512]{1,0:T(8,128)(2,1)S(1)}, u32[]{:S(2)}, u32[]{:S(2)}) collective-permute-start(bf16[512,512]{1,0:T(8,128)(2,1)S(1)} %get-tuple-element.107), channel_id=1, source_target_pairs={{0,4},{1,5},{2,6},{3,7},{4,0},{5,1},{6,2},{7,3},{8,12},{9,13},{10,... | collective-permute-start | bytes 1572872 | tf_op jit(solution)/shard_map/ppermute | solution.py:23
  94.7 13.7 %collective-permute-start.10 = (bf16[512,512]{1,0:T(8,128)(2,1)S(1)}, bf16[512,512]{1,0:T(8,128)(2,1)S(1)}, u32[]{:S(2)}, u32[]{:S(2)}) collective-permute-start(bf16[512,512]{1,0:T(8,128)(2,1)S(1)} %get-tuple-element.100.refs_11_), channel_id=1, source_target_pairs={{0,2},{1,3},{2,0},{3,1},{4,6},{5,7},{6,4},{7,5},{8,10},{9,11},{10,... | collective-permute-start | bytes 1572872 | tf_op jit(solution)/shard_map/ppermute | solution.py:23
  108.3 8.2 %collective-permute-start.12 = (bf16[512,1280]{1,0:T(8,128)(2,1)}, bf16[512,1280]{1,0:T(8,128)(2,1)S(1)}, u32[]{:S(2)}, u32[]{:S(2)}) collective-permute-start(bf16[512,1280]{1,0:T(8,128)(2,1)} %get-tuple-element.108.after.own_ref), channel_id=1, source_target_pairs={{0,1},{1,0},{2,3},{3,2},{4,5},{5,4},{6,7},{7,6},{8,9},{9,8},{10,11... | collective-permute-start | bytes 3932168 | tf_op jit(solution)/shard_map/ppermute | solution.py:23
  108.3 1.3 copy-start.9
  113.6 3.0 %copy-start.10 = (bf16[512,1280]{1,0:T(8,128)(2,1)S(1)}, bf16[512,1280]{1,0:T(8,128)(2,1)}, u32[]{:S(2)}) copy-start(bf16[512,1280]{1,0:T(8,128)(2,1)} %get-tuple-element.108.after.own_ref) | copy-start | bytes 3932164
  114.4 8.8 %collective-permute-start.13 = (bf16[256,512]{1,0:T(8,128)(2,1)S(1)}, bf16[256,512]{1,0:T(8,128)(2,1)S(1)}, u32[]{:S(2)}, u32[]{:S(2)}) collective-permute-start(bf16[256,512]{1,0:T(8,128)(2,1)S(1)} %get-tuple-element.116), channel_id=1, source_target_pairs={{0,4},{1,5},{2,6},{3,7},{4,0},{5,1},{6,2},{7,3},{8,12},{9,13},{10,... | collective-permute-start | bytes 786440 | tf_op jit(solution)/shard_map/ppermute | solution.py:23
  115.1 8.4 %collective-permute-start.14 = (bf16[256,512]{1,0:T(8,128)(2,1)S(1)}, bf16[256,512]{1,0:T(8,128)(2,1)S(1)}, u32[]{:S(2)}, u32[]{:S(2)}) collective-permute-start(bf16[256,512]{1,0:T(8,128)(2,1)S(1)} %get-tuple-element.117), channel_id=1, source_target_pairs={{0,2},{1,3},{2,0},{3,1},{4,6},{5,7},{6,4},{7,5},{8,10},{9,11},{10,... | collective-permute-start | bytes 786440 | tf_op jit(solution)/shard_map/ppermute | solution.py:23
  123.5 18.9 %collective-permute-start.17 = (bf16[512,768]{1,0:T(8,128)(2,1)S(1)}, bf16[512,768]{1,0:T(8,128)(2,1)S(1)}, u32[]{:S(2)}, u32[]{:S(2)}) collective-permute-start(bf16[512,768]{1,0:T(8,128)(2,1)S(1)} %get-tuple-element.125), channel_id=1, source_target_pairs={{0,4},{1,5},{2,6},{3,7},{4,0},{5,1},{6,2},{7,3},{8,12},{9,13},{10,... | collective-permute-start | bytes 2359304 | tf_op jit(solution)/shard_map/ppermute | solution.py:23
  124.9 13.0 %collective-permute-start.16 = (bf16[512,512]{1,0:T(8,128)(2,1)S(1)}, bf16[512,512]{1,0:T(8,128)(2,1)S(1)}, u32[]{:S(2)}, u32[]{:S(2)}) collective-permute-start(bf16[512,512]{1,0:T(8,128)(2,1)S(1)} %get-tuple-element.124.after), channel_id=1, source_target_pairs={{0,2},{1,3},{2,0},{3,1},{4,6},{5,7},{6,4},{7,5},{8,10},{9,11},{10,... | collective-permute-start | bytes 1572872 | tf_op jit(solution)/shard_map/ppermute | solution.py:23
  126.0 7.2 %collective-permute-start.15 = (bf16[128,1024]{1,0:T(8,128)(2,1)S(1)}, bf16[128,1024]{1,0:T(8,128)(2,1)S(1)}, u32[]{:S(2)}, u32[]{:S(2)}) collective-permute-start(bf16[128,1024]{1,0:T(8,128)(2,1)S(1)} %get-tuple-element.123), channel_id=1, source_target_pairs={{0,8},{8,0},{16,24},{24,16},{1,9},{9,1},{17,25},{25,17},{2,10},{10... | collective-permute-start | bytes 786440 | tf_op jit(solution)/shard_map/ppermute | solution.py:23
  143.6 9.6 %collective-permute-start.20 = (bf16[256,768]{1,0:T(8,128)(2,1)S(1)}, bf16[256,768]{1,0:T(8,128)(2,1)S(1)}, u32[]{:S(2)}, u32[]{:S(2)}) collective-permute-start(bf16[256,768]{1,0:T(8,128)(2,1)S(1)} %get-tuple-element.134), channel_id=1, source_target_pairs={{0,2},{1,3},{2,0},{3,1},{4,6},{5,7},{6,4},{7,5},{8,10},{9,11},{10,... | collective-permute-start | bytes 1179656 | tf_op jit(solution)/shard_map/ppermute | solution.py:23
  145.2 7.9 %collective-permute-start.19 = (bf16[256,512]{1,0:T(8,128)(2,1)S(1)}, bf16[256,512]{1,0:T(8,128)(2,1)S(1)}, u32[]{:S(2)}, u32[]{:S(2)}) collective-permute-start(bf16[256,512]{1,0:T(8,128)(2,1)S(1)} %get-tuple-element.133), channel_id=1, source_target_pairs={{0,4},{1,5},{2,6},{3,7},{4,0},{5,1},{6,2},{7,3},{8,12},{9,13},{10,... | collective-permute-start | bytes 786440 | tf_op jit(solution)/shard_map/ppermute | solution.py:23
  145.8 7.3 %collective-permute-start.18 = (bf16[64,1024]{1,0:T(8,128)(2,1)S(1)}, bf16[64,1024]{1,0:T(8,128)(2,1)S(1)}, u32[]{:S(2)}, u32[]{:S(2)}) collective-permute-start(bf16[64,1024]{1,0:T(8,128)(2,1)S(1)} %get-tuple-element.132), channel_id=1, source_target_pairs={{0,16},{8,24},{16,0},{24,8},{1,17},{9,25},{17,1},{25,9},{2,18},{10... | collective-permute-start | bytes 393224 | tf_op jit(solution)/shard_map/ppermute | solution.py:23
  154.0 10.1 %collective-permute-start.22 = (bf16[128,1280]{1,0:T(8,128)(2,1)S(1)}, bf16[128,1280]{1,0:T(8,128)(2,1)S(1)}, u32[]{:S(2)}, u32[]{:S(2)}) collective-permute-start(bf16[128,1280]{1,0:T(8,128)(2,1)S(1)} %get-tuple-element.139), channel_id=1, source_target_pairs={{0,8},{8,0},{16,24},{24,16},{1,9},{9,1},{17,25},{25,17},{2,10},{10... | collective-permute-start | bytes 983048 | tf_op jit(solution)/shard_map/ppermute | solution.py:23
  155.7 7.5 %collective-permute-start.21 = (bf16[64,1024]{1,0:T(8,128)(2,1)S(1)}, bf16[64,1024]{1,0:T(8,128)(2,1)S(1)}, u32[]{:S(2)}, u32[]{:S(2)}) collective-permute-start(bf16[64,1024]{1,0:T(8,128)(2,1)S(1)} %fold.12.after), channel_id=1, source_target_pairs={{0,16},{8,24},{16,0},{24,8},{1,17},{9,25},{17,1},{25,9},{2,18},{10... | collective-permute-start | bytes 393224 | tf_op jit(solution)/shard_map/ppermute | solution.py:23
  164.2 9.8 %collective-permute-start.23 = (bf16[128,1024]{1,0:T(8,128)(2,1)S(1)}, bf16[128,1024]{1,0:T(8,128)(2,1)S(1)}, u32[]{:S(2)}, u32[]{:S(2)}) collective-permute-start(bf16[128,1024]{1,0:T(8,128)(2,1)S(1)} %pad_maximum_fusion.1.refs_0_), channel_id=1, source_target_pairs={{0,8},{8,0},{16,24},{24,16},{1,9},{9,1},{17,25},{25,17},{2,10},{10... | collective-permute-start | bytes 786440 | tf_op jit(solution)/shard_map/ppermute | solution.py:23
  167.1 6.9 %collective-permute-start.24 = (bf16[64,1280]{1,0:T(8,128)(2,1)S(1)}, bf16[64,1280]{1,0:T(8,128)(2,1)S(1)}, u32[]{:S(2)}, u32[]{:S(2)}) collective-permute-start(bf16[64,1280]{1,0:T(8,128)(2,1)S(1)} %get-tuple-element.143), channel_id=1, source_target_pairs={{0,16},{8,24},{16,0},{24,8},{1,17},{9,25},{17,1},{25,9},{2,18},{10... | collective-permute-start | bytes 491528 | tf_op jit(solution)/shard_map/ppermute | solution.py:23
  174.2 8.7 %collective-permute-start.25 = (bf16[64,1280]{1,0:T(8,128)(2,1)S(1)}, bf16[64,1280]{1,0:T(8,128)(2,1)S(1)}, u32[]{:S(2)}, u32[]{:S(2)}) collective-permute-start(bf16[64,1280]{1,0:T(8,128)(2,1)S(1)} %fold.15), channel_id=1, source_target_pairs={{0,16},{8,24},{16,0},{24,8},{1,17},{9,25},{17,1},{25,9},{2,18},{10... | collective-permute-start | bytes 491528 | tf_op jit(solution)/shard_map/ppermute | solution.py:23
  183.0 7.1 %collective-permute-start.26 = (bf16[128,1280]{1,0:T(8,128)(2,1)S(1)}, bf16[128,1280]{1,0:T(8,128)(2,1)S(1)}, u32[]{:S(2)}, u32[]{:S(2)}) collective-permute-start(bf16[128,1280]{1,0:T(8,128)(2,1)S(1)} %pad_maximum_fusion.refs_2_), channel_id=1, source_target_pairs={{0,8},{8,0},{16,24},{24,16},{1,9},{9,1},{17,25},{25,17},{2,10},{10... | collective-permute-start | bytes 983048 | tf_op jit(solution)/shard_map/ppermute | solution.py:23

commit v4 on v3

--- a/solution.py
+++ b/solution.py
@@ -897,11 +897,12 @@
     turn = [before[-1]]
     peer = send(own, "ctx", 1)
     came = first_hop(terms(own, peer, size, going, BF))
+    stay = terms(own, peer, size, staying, F32)
     own_next = finished(start_next, size_next, turn[0])
     (own_next,), came = together([own_next], came)
     turn[0] = own_next
     peer_next = send(own_next, "ctx", 1)
-    ahead = summing(terms(own, peer, size, staying, F32), came, orders, turn)
+    ahead = summing(stay, came, orders, turn)
     hop = next(ahead)
     go, hop = together(terms(own_next, peer_next, size_next, going, BF), hop)
     came = first_hop(go)

time: 194 us -> 190 us (0.979)
  waiting for transfers between devices: 56.1 us -> 51.1 us
    ppermute x27, waiting for transfers between devices: 56.1 us -> 51.1 us  [send(): lax.ppermute(array, axis, [(i, i ^ mask) for i in range(lax.axis_size(axi...]
    unnamed x69 -> x73, local copies, waits for them, and re-layouts: 13 us -> 14 us
  transfers between devices with their start and end apart: 27 -> 27, of which waited for: 17 -> 16; matrix products, arithmetic and copies ran while one was open for 0% -> 0% of each run, Pallas kernels for 26% -> 26%
where the time goes in v4:
time: 190 us; the launch traced here: 189 us
  Pallas kernels  89.6 us (47%)
  waiting for transfers between devices  51.1 us (27%)
  starting transfers between devices  32.5 us (17%)
  local copies, waits for them, and re-layouts  14.3 us (8%)
    ppermute x27, waiting for transfers between devices, send(): lax.ppermute(array, axis, [(i, i ^ mask) for i in range(lax.axis_size(axi...  51.1 us
    ppermute x27, starting transfers between devices, send(): lax.ppermute(array, axis, [(i, i ^ mask) for i in range(lax.axis_size(axi...  32.5 us
    pallas_call x4, Pallas kernels, weight_terms(): pl.pallas_call(functools.partial(term_kernel, picked, pieces), grid=(own....  14.7 us
    unnamed x73, local copies, waits for them, and re-layouts  14 us
    pallas_call x2, Pallas kernels, finish(): pl.pallas_call(functools.partial(finish_kernel, first, len(arrived), last...  12.7 us
    pallas_call x1, Pallas kernels, inner_back(): pl.pallas_call(inner_back_kernel, grid=(channels // GROUP,), in_specs=[bl...  12.3 us
    pallas_call x1, Pallas kernels, normed(): pl.pallas_call(functools.partial(normed_kernel, len(arrived), heads), gri...  11.4 us
    pallas_call x1, Pallas kernels, project(): pl.pallas_call(project_kernel, grid=(channels // PROJECTED,), in_specs=[w...  11 us
  transfers between devices with their start and end apart: 27, of which 16 were waited for; matrix products, arithmetic and copies ran while one was open for 0% of the time, Pallas kernels for 26%

profile of v4, /device:TPU:0, one launch (start us, length us, event | category | flops | bytes accessed | tf_op | source)
XLA Modules:
  0.0 188.9 jit_solution(4800760210803042380)
XLA Ops:
  0.6 1.1 copy-done.23
  1.7 0.7 copy-done.31
  2.4 0.7 copy-done.33
  3.0 3.9 %small.1 = (bf16[512,2048]{1,0:T(8,128)(2,1)S(1)}, f32[2,256,384]{2,1,0:T(8,128)S(1)}, f32[2,64,256]{2,1,0:T(8,128)S(1)}, bf16[2,256,384]{2,1,0:T(8,128)(2,1)S(1...) custom-call(bf16[256,2048]{1,0:T(8,128)(2,1)} %bitcast.h_ref.own_ref, ...), custom_call_target="tpu_custom_call" | custom-call | tf_op jit(solution)/shard_map/small/pallas_call | solution.py:135
  6.9 11.0 %project.1 = (bf16[2,256,2048]{2,1,0:T(8,128)(2,1)S(1)}, f32[2,72,2048]{2,1,0:T(8,128)S(1)}) custom-call(bf16[512,2048]{1,0:T(8,128)(2,1)S(1)} %get-tuple-element.76.both_ref, bf16[2048,2048]{1,0:T(8,128)(2,1)} %w_ref.1, bf16[2,128,256]{2,1,0:T(8,128)(2,1)S(1)} %get-tuple-element.77.bt_ref, bf16[2,256,96]{2,1,0:T(8,128)(2,1)S(1)} %get-tuple-element.78.weight3_ref, ...), custom_call_target="tpu_custom_call" | custom-call | tf_op jit(solution)/shard_map/project/pallas_call | solution.py:173
  18.0 1.3 copy-done
  20.2 6.5 %inner.2.after.raw_fwd_ref = f32[256,2048]{1,0:T(8,128)S(1)} custom-call(bf16[2,256,2048]{2,1,0:T(8,128)(2,1)} %copy-done, f32[2,256,384]{2,1,0:T(8,128)S(1)} %get-tuple-element.81.nat_ref.nat_fwd_ref.nat_rc_ref.refs_12_, f32[2,64,256]{2,1,0:T(8,128)S(1)} %get-tuple-element.82.lines_ref, f32[2,72,2048]{2,1,0:T(8,128)S(1)} %get-tuple-element.83.after.refs_0_.own_ref.refs_4_), custom_call_target="tpu_custom_call" | custom-call | tf_op jit(solution)/shard_map/inner/pallas_call | solution.py:235
  26.7 0.9 merge.2
  28.4 3.9 %collective-permute-start.4 = (bf16[80,2048]{1,0:T(8,128)(2,1)S(1)}, bf16[80,2048]{1,0:T(8,128)(2,1)S(1)}, u32[]{:S(2)}, u32[]{:S(2)}) collective-permute-start(bf16[80,2048]{1,0:T(8,128)(2,1)S(1)} %get-tuple-element.86), channel_id=1, source_target_pairs={{0,6},{1,7},{2,4},{3,5},{4,2},{5,3},{6,0},{7,1},{8,14},{9,15},{10,... | collective-permute-start | bytes 983048 | tf_op jit(solution)/shard_map/ppermute | solution.py:23
  32.9 4.4 %turned.1.after.left_ref = bf16[1024,1024]{1,0:T(8,128)(2,1)S(1)} custom-call(s32[8]{0:T(128)S(1)} %pad_add_fusion.where_ref, bf16[256,2048]{1,0:T(8,128)(2,1)} %bitcast.h_ref.own_ref.own_mirror_ref, bf16[256,2048]{1,0:T(8,128)(2,1)} %bitcast.h_ref.own_ref.own_mirror_ref, bf16[256,2048]{1,0:T(8,128)(2,1)} %collective-permute-done.peer_ref.peer_mirror_ref, ...), custom_call_target="tpu_custom_call" | custom-call | tf_op jit(solution)/shard_map/turned/pallas_call | solution.py:674
  37.3 1.3 copy-done.3
  38.7 4.5 %inner.3.raw_rc_ref = f32[256,2048]{1,0:T(8,128)S(1)} custom-call(bf16[2,256,2048]{2,1,0:T(8,128)(2,1)S(1)} %copy-done.1, f32[2,256,384]{2,1,0:T(8,128)S(1)} %copy-done.7, f32[2,64,256]{2,1,0:T(8,128)S(1)} %get-tuple-element.82.lines_ref, bf16[1024,1024]{1,0:T(8,128)(2,1)} %copy-done.3), custom_call_target="tpu_custom_call" | custom-call | tf_op jit(solution)/shard_map/inner/pallas_call | solution.py:235
  43.1 1.4 copy-done.13
  44.5 2.9 %collective-permute-done.2.refs_0_ = bf16[80,2048]{1,0:T(8,128)(2,1)S(1)} collective-permute-done((bf16[80,2048]{1,0:T(8,128)(2,1)S(1)}, bf16[80,2048]{1,0:T(8,128)(2,1)S(1)}, u32[]{:S(2)}, u32[]{:S(2)}) %collective-permute-start.2) | collective-permute-done | bytes 327712 | tf_op jit(solution)/shard_map/ppermute | solution.py:23
  47.5 11.4 %normed.1 = (bf16[256,2048]{1,0:T(8,128)(2,1)}, bf16[2,256,2048]{2,1,0:T(8,128)(2,1)}, f32[2,256,32]{2,1,0:T(8,128)S(1)}, f32[2,64,2048]{2,1,0:T(8,128)S(1)}, f3...) custom-call(f32[256,2048]{1,0:T(8,128)} %copy-done.8, ...), custom_call_target="tpu_custom_call" | custom-call | tf_op jit(solution)/shard_map/normed/pallas_call | solution.py:425
  58.9 1.0 copy-done.17
  59.9 2.7 %collective-permute-done.5.refs_2_.refs_7_ = f32[2,64,2048]{2,1,0:T(8,128)S(1)} collective-permute-done((f32[2,64,2048]{2,1,0:T(8,128)S(1)}, f32[2,64,2048]{2,1,0:T(8,128)S(1)}, u32[]{:S(2)}, u32[]{:S(2)}) %collective-permute-start.5) | collective-permute-done | bytes 1048608 | tf_op jit(solution)/shard_map/ppermute | solution.py:23
  62.6 1.6 merge.3
  64.2 1.0 copy-done.11
  65.1 1.5 collective-permute-start.6
  66.7 1.4 collective-permute-start.8
  68.0 0.6 collective-permute-start.7
  68.7 1.6 copy-done.19
  70.3 12.3 %inner_back.1 = (f32[2,256,2048]{2,1,0:T(8,128)}, f32[2,256,64]{2,1,0:T(8,128)S(1)}, f32[2,256,64]{2,1,0:T(8,128)S(1)}) custom-call(bf16[2,256,2048]{2,1,0:T(8,128)(2,1)S(1)} %copy-done.2, bf16[2,256,2048]{2,1,0:T(8,128)(2,1)S(1)} %copy-done.19, f32[2,256,384]{2,1,0:T(8,128)S(1)} %copy-done.7, f32[2,64,256]{2,1,0:T(8,128)S(1)} %get-tuple-element.82.lines_ref, ...), custom_call_target="tpu_custom_call" | custom-call | tf_op jit(solution)/shard_map/inner_back/pallas_call | solution.py:525
  82.7 5.5 %finish.2 = (bf16[512,1024]{1,0:T(8,128)(2,1)S(1)}, f32[2,256,64]{2,1,0:T(8,128)S(1)}, f32[2,256,32]{2,1,0:T(8,128)S(1)}, f32[2,1,32]{2,1,0:T(1,128)S(1)}) custom-call(bf16[2,256,2048]{2,1,0:T(8,128)(2,1)} %copy-done, f32[2,256,2048]{2,1,0:T(8,128)} %get-tuple-element.93.refs_1_, bf16[2,256,384]{2,1,0:T(8,128)(2,1)S(1)} %copy-done.21, ...), custom_call_target="tpu_custom_call" | custom-call | tf_op jit(solution)/shard_map/finish/pallas_call | solution.py:630
  88.2 2.6 %collective-permute-done.9.peer_ref = bf16[512,1024]{1,0:T(8,128)(2,1)S(1)} collective-permute-done((bf16[512,1024]{1,0:T(8,128)(2,1)S(1)}, bf16[512,1024]{1,0:T(8,128)(2,1)S(1)}, u32[]{:S(2)}, u32[]{:S(2)}) %collective-permute-start.9) | collective-permute-done | bytes 1048608 | tf_op jit(solution)/shard_map/ppermute | solution.py:23
  90.9 2.3 %terms.4 = (bf16[512,512]{1,0:T(8,128)(2,1)S(1)}, bf16[512,512]{1,0:T(8,128)(2,1)S(1)}) custom-call(bf16[1024,1024]{1,0:T(8,128)(2,1)S(1)} %copy-done.4, bf16[512,1024]{1,0:T(8,128)(2,1)S(1)} %get-tuple-element.98.own_ref, bf16[512,1024]{1,0:T(8,128)(2,1)S(1)} %collective-permute-done.9.peer_ref, f32[2,1,32]{2,1,0:T(1,128)S(1)} %get-tuple-element.99.after.refs_20_), custom_call_target="tpu_custom_call" | custom-call | tf_op jit(solution)/shard_map/terms/pallas_call | solution.py:728
  93.2 1.5 collective-permute-start.11
  94.6 0.6 collective-permute-start.10
  95.2 3.9 %terms.5 = (f32[512,512]{1,0:T(8,128)S(1)}, f32[512,512]{1,0:T(8,128)S(1)}) custom-call(bf16[1024,1024]{1,0:T(8,128)(2,1)} %copy-done.3, bf16[512,1024]{1,0:T(8,128)(2,1)S(1)} %get-tuple-element.98.own_ref, bf16[512,1024]{1,0:T(8,128)(2,1)S(1)} %collective-permute-done.9.peer_ref, bf16[512,512]{1,0:T(8,128)(2,1)S(1)} %get-tuple-element.100.after), custom_call_target="tpu_custom_call" | custom-call | tf_op jit(solution)/shard_map/terms/pallas_call | solution.py:728
  99.1 1.0 copy-done.15
  100.2 7.2 %finish.3 = (bf16[512,1280]{1,0:T(8,128)(2,1)}, f32[2,256,64]{2,1,0:T(8,128)}, f32[2,256,32]{2,1,0:T(8,128)}, f32[2,1,32]{2,1,0:T(1,128)}) custom-call(bf16[2,256,2048]{2,1,0:T(8,128)(2,1)} %copy-done, f32[2,256,2048]{2,1,0:T(8,128)} %get-tuple-element.93.refs_1_, bf16[2,256,384]{2,1,0:T(8,128)(2,1)S(1)} %copy-done.21, f32[2,64,2048]{2,1,0:T(8,128)S(1)} %copy-done.18, ...), custom_call_target="tpu_custom_call" | custom-call | tf_op jit(solution)/shard_map/finish/pallas_call | solution.py:630
  107.4 0.9 collective-permute-done.10.refs_1_
  108.3 1.3 copy-done.9
  109.7 0.8 fold.8
  110.4 0.8 collective-permute-start.13
  111.2 1.4 collective-permute-start.14
  112.6 4.2 %terms.6 = (bf16[512,512]{1,0:T(8,128)(2,1)S(1)}, bf16[512,768]{1,0:T(8,128)(2,1)S(1)}) custom-call(bf16[1024,1024]{1,0:T(8,128)(2,1)} %copy-done.3, bf16[512,1280]{1,0:T(8,128)(2,1)S(1)} %copy-done.10, bf16[512,1280]{1,0:T(8,128)(2,1)S(1)} %collective-permute-done.12.peer_ref, f32[256,512]{1,0:T(8,128)S(1)} %get-tuple-element.113.after.refs_0_), custom_call_target="tpu_custom_call" | custom-call | tf_op jit(solution)/shard_map/terms/pallas_call | solution.py:728
  116.9 2.3 %collective-permute-done.13.refs_1_ = bf16[256,512]{1,0:T(8,128)(2,1)S(1)} collective-permute-done((bf16[256,512]{1,0:T(8,128)(2,1)S(1)}, bf16[256,512]{1,0:T(8,128)(2,1)S(1)}, u32[]{:S(2)}, u32[]{:S(2)}) %collective-permute-start.13) | collective-permute-done | bytes 262176 | tf_op jit(solution)/shard_map/ppermute | solution.py:23
  119.6 1.4 collective-permute-start.17
  121.0 0.6 collective-permute-start.16
  122.0 1.8 collective-permute-start.15
  123.9 4.3 %terms.7 = (f32[512,512]{1,0:T(8,128)S(1)}, f32[512,768]{1,0:T(8,128)S(1)}) custom-call(bf16[1024,1024]{1,0:T(8,128)(2,1)} %copy-done.3, bf16[512,1280]{1,0:T(8,128)(2,1)S(1)} %copy-done.10, bf16[512,1280]{1,0:T(8,128)(2,1)S(1)} %collective-permute-done.12.peer_ref, f32[128,1024]{1,0:T(8,128)S(1)} %get-tuple-element.121.after.refs_0_), custom_call_target="tpu_custom_call" | custom-call | tf_op jit(solution)/shard_map/terms/pallas_call | solution.py:728
  128.2 1.1 collective-permute-done.15.refs_1_
  129.3 4.7 %collective-permute-done.16.refs_1_ = bf16[512,512]{1,0:T(8,128)(2,1)S(1)} collective-permute-done((bf16[512,512]{1,0:T(8,128)(2,1)S(1)}, bf16[512,512]{1,0:T(8,128)(2,1)S(1)}, u32[]{:S(2)}, u32[]{:S(2)}) %collective-permute-start.16) | collective-permute-done | bytes 524320 | tf_op jit(solution)/shard_map/ppermute | solution.py:23
  133.9 4.5 %collective-permute-done.17.refs_3_ = bf16[512,768]{1,0:T(8,128)(2,1)S(1)} collective-permute-done((bf16[512,768]{1,0:T(8,128)(2,1)S(1)}, bf16[512,768]{1,0:T(8,128)(2,1)S(1)}, u32[]{:S(2)}, u32[]{:S(2)}) %collective-permute-start.17) | collective-permute-done | bytes 786464 | tf_op jit(solution)/shard_map/ppermute | solution.py:23
  138.7 1.0 fold.11
  139.7 1.5 collective-permute-start.20
  141.3 0.6 collective-permute-start.19
  141.9 2.7 %collective-permute-start.18 = (bf16[64,1024]{1,0:T(8,128)(2,1)S(1)}, bf16[64,1024]{1,0:T(8,128)(2,1)S(1)}, u32[]{:S(2)}, u32[]{:S(2)}) collective-permute-start(bf16[64,1024]{1,0:T(8,128)(2,1)S(1)} %get-tuple-element.132), channel_id=1, source_target_pairs={{0,16},{8,24},{16,0},{24,8},{1,17},{9,25},{17,1},{25,9},{2,18},{10... | collective-permute-start | bytes 393224 | tf_op jit(solution)/shard_map/ppermute | solution.py:23
  144.5 4.6 %collective-permute-done.18.refs_1_ = bf16[64,1024]{1,0:T(8,128)(2,1)S(1)} collective-permute-done((bf16[64,1024]{1,0:T(8,128)(2,1)S(1)}, bf16[64,1024]{1,0:T(8,128)(2,1)S(1)}, u32[]{:S(2)}, u32[]{:S(2)}) %collective-permute-start.18) | collective-permute-done | bytes 131104 | tf_op jit(solution)/shard_map/ppermute | solution.py:23
  149.5 0.6 fold.13
  150.1 1.6 collective-permute-start.22
  151.7 2.6 %collective-permute-start.21 = (bf16[64,1024]{1,0:T(8,128)(2,1)S(1)}, bf16[64,1024]{1,0:T(8,128)(2,1)S(1)}, u32[]{:S(2)}, u32[]{:S(2)}) collective-permute-start(bf16[64,1024]{1,0:T(8,128)(2,1)S(1)} %fold.12.after), channel_id=1, source_target_pairs={{0,16},{8,24},{16,0},{24,8},{1,17},{9,25},{17,1},{25,9},{2,18},{10... | collective-permute-start | bytes 393224 | tf_op jit(solution)/shard_map/ppermute | solution.py:23
  154.3 4.9 %collective-permute-done.21 = bf16[64,1024]{1,0:T(8,128)(2,1)S(1)} collective-permute-done((bf16[64,1024]{1,0:T(8,128)(2,1)S(1)}, bf16[64,1024]{1,0:T(8,128)(2,1)S(1)}, u32[]{:S(2)}, u32[]{:S(2)}) %collective-permute-start.21) | collective-permute-done | bytes 131104 | tf_op jit(solution)/shard_map/ppermute | solution.py:23
  159.2 1.0 collective-permute-done.22.refs_1_
  160.2 2.6 %collective-permute-start.23 = (bf16[128,1024]{1,0:T(8,128)(2,1)S(1)}, bf16[128,1024]{1,0:T(8,128)(2,1)S(1)}, u32[]{:S(2)}, u32[]{:S(2)}) collective-permute-start(bf16[128,1024]{1,0:T(8,128)(2,1)S(1)} %pad_maximum_fusion.1.refs_0_), channel_id=1, source_target_pairs={{0,8},{8,0},{16,24},{24,16},{1,9},{9,1},{17,25},{25,17},{2,10},{10... | collective-permute-start | bytes 786440 | tf_op jit(solution)/shard_map/ppermute | solution.py:23
  163.1 1.6 collective-permute-start.24
  164.8 5.2 %collective-permute-done.24.refs_1_ = bf16[64,1280]{1,0:T(8,128)(2,1)S(1)} collective-permute-done((bf16[64,1280]{1,0:T(8,128)(2,1)S(1)}, bf16[64,1280]{1,0:T(8,128)(2,1)S(1)}, u32[]{:S(2)}, u32[]{:S(2)}) %collective-permute-start.24) | collective-permute-done | bytes 163872 | tf_op jit(solution)/shard_map/ppermute | solution.py:23
  170.2 2.5 %collective-permute-start.25 = (bf16[64,1280]{1,0:T(8,128)(2,1)S(1)}, bf16[64,1280]{1,0:T(8,128)(2,1)S(1)}, u32[]{:S(2)}, u32[]{:S(2)}) collective-permute-start(bf16[64,1280]{1,0:T(8,128)(2,1)S(1)} %fold.15), channel_id=1, source_target_pairs={{0,16},{8,24},{16,0},{24,8},{1,17},{9,25},{17,1},{25,9},{2,18},{10... | collective-permute-start | bytes 491528 | tf_op jit(solution)/shard_map/ppermute | solution.py:23
  172.7 6.2 %collective-permute-done.25 = bf16[64,1280]{1,0:T(8,128)(2,1)S(1)} collective-permute-done((bf16[64,1280]{1,0:T(8,128)(2,1)S(1)}, bf16[64,1280]{1,0:T(8,128)(2,1)S(1)}, u32[]{:S(2)}, u32[]{:S(2)}) %collective-permute-start.25) | collective-permute-done | bytes 163872 | tf_op jit(solution)/shard_map/ppermute | solution.py:23
  179.2 6.9 %collective-permute-done.26.refs_3_ = bf16[128,1280]{1,0:T(8,128)(2,1)S(1)} collective-permute-done((bf16[128,1280]{1,0:T(8,128)(2,1)S(1)}, bf16[128,1280]{1,0:T(8,128)(2,1)S(1)}, u32[]{:S(2)}, u32[]{:S(2)}) %collective-permute-start.26) | collective-permute-done | bytes 327712 | tf_op jit(solution)/shard_map/ppermute | solution.py:23
  186.1 2.0 %placed.1 = (f32[256,2048]{1,0:T(8,128)}, f32[256,160]{1,0:T(8,128)S(1)}) custom-call(s32[8]{0:T(128)S(1)} %pad_add_fusion.where_ref, bf16[128,1024]{1,0:T(8,128)(2,1)S(1)} %pad_maximum_fusion.1.refs_0_, bf16[128,1024]{1,0:T(8,128)(2,1)S(1)} %collective-permute-done.23.refs_1_, bf16[128,1280]{1,0:T(8,128)(2,1)S(1)} %pad_maximum_fusion.refs_2_, ...), custom_call_target="tpu_custom_call" | custom-call | tf_op jit(solution)/shard_map/placed/pallas_call | solution.py:826
  188.1 0.8 copy.12
  (100 shorter events, 5.0 us)
Async XLA Ops:
  0.6 1.1 copy-start.23
  1.7 0.7 copy-start.31
  2.4 0.7 copy-start.33
  6.9 11.0 %copy-start.20 = (bf16[2,256,384]{2,1,0:T(8,128)(2,1)}, bf16[2,256,384]{2,1,0:T(8,128)(2,1)S(1)}, u32[]{:S(2)}) copy-start(bf16[2,256,384]{2,1,0:T(8,128)(2,1)S(1)} %get-tuple-element.94.refs_2_) | copy-start | bytes 1179652
  6.9 11.0 %copy-start.24 = (bf16[2,256,384]{2,1,0:T(8,128)(2,1)}, bf16[2,256,384]{2,1,0:T(8,128)(2,1)S(1)}, u32[]{:S(2)}) copy-start(bf16[2,256,384]{2,1,0:T(8,128)(2,1)S(1)} %get-tuple-element.85.cg3_ref) | copy-start | bytes 1179652
  6.9 13.3 %copy-start.6 = (f32[2,256,384]{2,1,0:T(8,128)}, f32[2,256,384]{2,1,0:T(8,128)S(1)}, u32[]{:S(2)}) copy-start(f32[2,256,384]{2,1,0:T(8,128)S(1)} %get-tuple-element.81.nat_ref.nat_fwd_ref.nat_rc_ref.refs_12_) | copy-start | bytes 2359300
  6.9 13.1 %copy-start.35 = (s32[2]{0:T(128)S(1)}, s32[2]{0:T(128)}, u32[]{:S(2)}) copy-start(s32[2]{0:T(128)} %constant.42.clone) | copy-start | bytes 28
  18.0 1.3 copy-start
  19.3 7.4 %copy-start.5 = (f32[2,72,2048]{2,1,0:T(8,128)}, f32[2,72,2048]{2,1,0:T(8,128)S(1)}, u32[]{:S(2)}) copy-start(f32[2,72,2048]{2,1,0:T(8,128)S(1)} %get-tuple-element.83.after.refs_0_.own_ref.refs_4_) | copy-start | bytes 3538948
  19.3 7.4 %collective-permute-start.1 = (f32[2,72,2048]{2,1,0:T(8,128)S(1)}, f32[2,72,2048]{2,1,0:T(8,128)S(1)}, u32[]{:S(2)}, u32[]{:S(2)}) collective-permute-start(f32[2,72,2048]{2,1,0:T(8,128)S(1)} %get-tuple-element.83.after.refs_0_.own_ref.refs_4_), channel_id=1, source_target_pairs={{0,1},{1,0},{2,3},{3,2},{4,5},{5,4},{6,7},{7,6},{8,9},{9,8},{10,11... | collective-permute-start | bytes 3538952 | tf_op jit(solution)/shard_map/ppermute | solution.py:23
  19.7 13.2 %collective-permute-start = (bf16[256,2048]{1,0:T(8,128)(2,1)}, bf16[256,2048]{1,0:T(8,128)(2,1)}, u32[]{:S(2)}, u32[]{:S(2)}) collective-permute-start(bf16[256,2048]{1,0:T(8,128)(2,1)} %bitcast.h_ref.own_ref.own_mirror_ref), channel_id=1, source_target_pairs={{0,1},{1,0},{2,3},{3,2},{4,5},{5,4},{6,7},{7,6},{8,9},{9,8},{10,11... | collective-permute-start | bytes 3145736 | tf_op jit(solution)/shard_map/ppermute | solution.py:23
  26.7 1.4 copy-start.8
  26.7 6.2 %copy-start.34 = (s32[4]{0:T(128)S(1)}, s32[4]{0:T(128)}, u32[]{:S(2)}) copy-start(s32[4]{0:T(128)} %constant.43.clone) | copy-start | bytes 52
  26.7 1.7 copy-start.14
  28.4 19.1 %collective-permute-start.4 = (bf16[80,2048]{1,0:T(8,128)(2,1)S(1)}, bf16[80,2048]{1,0:T(8,128)(2,1)S(1)}, u32[]{:S(2)}, u32[]{:S(2)}) collective-permute-start(bf16[80,2048]{1,0:T(8,128)(2,1)S(1)} %get-tuple-element.86), channel_id=1, source_target_pairs={{0,6},{1,7},{2,4},{3,5},{4,2},{5,3},{6,0},{7,1},{8,14},{9,15},{10,... | collective-permute-start | bytes 983048 | tf_op jit(solution)/shard_map/ppermute | solution.py:23
  32.3 15.2 %collective-permute-start.3 = (bf16[80,2048]{1,0:T(8,128)(2,1)S(1)}, bf16[80,2048]{1,0:T(8,128)(2,1)S(1)}, u32[]{:S(2)}, u32[]{:S(2)}) collective-permute-start(bf16[80,2048]{1,0:T(8,128)(2,1)S(1)} %get-tuple-element.86), channel_id=1, source_target_pairs={{0,4},{1,5},{2,6},{3,7},{4,0},{5,1},{6,2},{7,3},{8,12},{9,13},{10,... | collective-permute-start | bytes 983048 | tf_op jit(solution)/shard_map/ppermute | solution.py:23
  32.8 14.7 %collective-permute-start.2 = (bf16[80,2048]{1,0:T(8,128)(2,1)S(1)}, bf16[80,2048]{1,0:T(8,128)(2,1)S(1)}, u32[]{:S(2)}, u32[]{:S(2)}) collective-permute-start(bf16[80,2048]{1,0:T(8,128)(2,1)S(1)} %get-tuple-element.84.after), channel_id=1, source_target_pairs={{0,2},{1,3},{2,0},{3,1},{4,6},{5,7},{6,4},{7,5},{8,10},{9,11},{10,... | collective-permute-start | bytes 983048 | tf_op jit(solution)/shard_map/ppermute | solution.py:23
  32.9 5.7 %copy-start.1 = (bf16[2,256,2048]{2,1,0:T(8,128)(2,1)S(1)}, bf16[2,256,2048]{2,1,0:T(8,128)(2,1)}, u32[]{:S(2)}) copy-start(bf16[2,256,2048]{2,1,0:T(8,128)(2,1)} %copy-done) | copy-start | bytes 6291460
  32.9 5.7 %copy-start.7 = (f32[2,256,384]{2,1,0:T(8,128)S(1)}, f32[2,256,384]{2,1,0:T(8,128)}, u32[]{:S(2)}) copy-start(f32[2,256,384]{2,1,0:T(8,128)} %copy-done.6) | copy-start | bytes 2359300
  37.3 1.3 copy-start.3
  38.7 8.8 %copy-start.22 = (bf16[1,256,2048]{2,1,0:T(8,128)(2,1)S(1)}, bf16[1,256,2048]{2,1,0:T(8,128)(2,1)}, u32[]{:S(2)}) copy-start(bf16[1,256,2048]{2,1,0:T(8,128)(2,1)} %param.15) | copy-start | bytes 3145732
  38.7 8.8 %copy-start.25 = (bf16[2,256,384]{2,1,0:T(8,128)(2,1)S(1)}, bf16[2,256,384]{2,1,0:T(8,128)(2,1)}, u32[]{:S(2)}) copy-start(bf16[2,256,384]{2,1,0:T(8,128)(2,1)} %copy-done.24) | copy-start | bytes 1179652
  38.7 8.8 %copy-start.30 = (f32[2048]{0:T(1024)S(1)}, f32[2048]{0:T(1024)}, u32[]{:S(2)}) copy-start(f32[2048]{0:T(1024)} %param.14) | copy-start | bytes 24580
  43.1 1.4 copy-start.13
  58.9 1.0 copy-start.17
  59.9 4.2 %copy-start.26 = (f32[2,256,32]{2,1,0:T(8,128)}, f32[2,256,32]{2,1,0:T(8,128)S(1)}, u32[]{:S(2)}) copy-start(f32[2,256,32]{2,1,0:T(8,128)S(1)} %get-tuple-element.104.refs_16_) | copy-start | bytes 196612
  59.9 5.2 %copy-start.28 = (f32[2,256,64]{2,1,0:T(8,128)}, f32[2,256,64]{2,1,0:T(8,128)S(1)}, u32[]{:S(2)}) copy-start(f32[2,256,64]{2,1,0:T(8,128)S(1)} %get-tuple-element.103.refs_15_) | copy-start | bytes 393220
  59.9 8.8 %copy-start.2 = (bf16[2,256,2048]{2,1,0:T(8,128)(2,1)S(1)}, bf16[2,256,2048]{2,1,0:T(8,128)(2,1)}, u32[]{:S(2)}) copy-start(bf16[2,256,2048]{2,1,0:T(8,128)(2,1)} %copy-done) | copy-start | bytes 6291460
  59.9 2.7 %collective-permute-start.5 = (f32[2,64,2048]{2,1,0:T(8,128)S(1)}, f32[2,64,2048]{2,1,0:T(8,128)S(1)}, u32[]{:S(2)}, u32[]{:S(2)}) collective-permute-start(f32[2,64,2048]{2,1,0:T(8,128)S(1)} %get-tuple-element.90.after.refs_1_), channel_id=1, source_target_pairs={{0,1},{1,0},{2,3},{3,2},{4,5},{5,4},{6,7},{7,6},{8,9},{9,8},{10,11... | collective-permute-start | bytes 3145736 | tf_op jit(solution)/shard_map/ppermute | solution.py:23
  64.2 1.0 copy-start.11
  65.1 17.5 %collective-permute-start.6 = (bf16[64,2048]{1,0:T(8,128)(2,1)}, bf16[64,2048]{1,0:T(8,128)(2,1)S(1)}, u32[]{:S(2)}, u32[]{:S(2)}) collective-permute-start(bf16[64,2048]{1,0:T(8,128)(2,1)} %get-tuple-element.92.after), channel_id=1, source_target_pairs={{0,2},{1,3},{2,0},{3,1},{4,6},{5,7},{6,4},{7,5},{8,10},{9,11},{10,... | collective-permute-start | bytes 786440 | tf_op jit(solution)/shard_map/ppermute | solution.py:23
  66.7 16.0 %collective-permute-start.8 = (bf16[64,2048]{1,0:T(8,128)(2,1)}, bf16[64,2048]{1,0:T(8,128)(2,1)}, u32[]{:S(2)}, u32[]{:S(2)}) collective-permute-start(bf16[64,2048]{1,0:T(8,128)(2,1)} %get-tuple-element.96), channel_id=1, source_target_pairs={{0,6},{1,7},{2,4},{3,5},{4,2},{5,3},{6,0},{7,1},{8,14},{9,15},{10,... | collective-permute-start | bytes 786440 | tf_op jit(solution)/shard_map/ppermute | solution.py:23
  68.0 14.6 %collective-permute-start.7 = (bf16[64,2048]{1,0:T(8,128)(2,1)}, bf16[64,2048]{1,0:T(8,128)(2,1)}, u32[]{:S(2)}, u32[]{:S(2)}) collective-permute-start(bf16[64,2048]{1,0:T(8,128)(2,1)} %get-tuple-element.96), channel_id=1, source_target_pairs={{0,4},{1,5},{2,6},{3,7},{4,0},{5,1},{6,2},{7,3},{8,12},{9,13},{10,... | collective-permute-start | bytes 786440 | tf_op jit(solution)/shard_map/ppermute | solution.py:23
  68.7 1.6 copy-start.19
  70.3 12.3 %copy-start.12 = (f32[2,64,2048]{2,1,0:T(8,128)S(1)}, f32[2,64,2048]{2,1,0:T(8,128)}, u32[]{:S(2)}) copy-start(f32[2,64,2048]{2,1,0:T(8,128)} %copy-done.11) | copy-start | bytes 3145732
  70.3 12.3 %copy-start.18 = (f32[2,64,2048]{2,1,0:T(8,128)S(1)}, f32[2,64,2048]{2,1,0:T(8,128)}, u32[]{:S(2)}) copy-start(f32[2,64,2048]{2,1,0:T(8,128)} %copy-done.17) | copy-start | bytes 3145732
  70.3 12.3 %copy-start.21 = (bf16[2,256,384]{2,1,0:T(8,128)(2,1)S(1)}, bf16[2,256,384]{2,1,0:T(8,128)(2,1)}, u32[]{:S(2)}) copy-start(bf16[2,256,384]{2,1,0:T(8,128)(2,1)} %copy-done.20) | copy-start | bytes 1179652
  82.7 8.2 %copy-start.4 = (bf16[1024,1024]{1,0:T(8,128)(2,1)S(1)}, bf16[1024,1024]{1,0:T(8,128)(2,1)}, u32[]{:S(2)}) copy-start(bf16[1024,1024]{1,0:T(8,128)(2,1)} %copy-done.3) | copy-start | bytes 6291460
  88.2 2.7 %collective-permute-start.9 = (bf16[512,1024]{1,0:T(8,128)(2,1)S(1)}, bf16[512,1024]{1,0:T(8,128)(2,1)S(1)}, u32[]{:S(2)}, u32[]{:S(2)}) collective-permute-start(bf16[512,1024]{1,0:T(8,128)(2,1)S(1)} %get-tuple-element.98.own_ref), channel_id=1, source_target_pairs={{0,1},{1,0},{2,3},{3,2},{4,5},{5,4},{6,7},{7,6},{8,9},{9,8},{10,11... | collective-permute-start | bytes 3145736 | tf_op jit(solution)/shard_map/ppermute | solution.py:23
  93.2 14.2 %collective-permute-start.11 = (bf16[512,512]{1,0:T(8,128)(2,1)S(1)}, bf16[512,512]{1,0:T(8,128)(2,1)S(1)}, u32[]{:S(2)}, u32[]{:S(2)}) collective-permute-start(bf16[512,512]{1,0:T(8,128)(2,1)S(1)} %get-tuple-element.108), channel_id=1, source_target_pairs={{0,4},{1,5},{2,6},{3,7},{4,0},{5,1},{6,2},{7,3},{8,12},{9,13},{10,... | collective-permute-start | bytes 1572872 | tf_op jit(solution)/shard_map/ppermute | solution.py:23
  94.6 5.5 %copy-start.27 = (f32[2,256,32]{2,1,0:T(8,128)S(1)}, f32[2,256,32]{2,1,0:T(8,128)}, u32[]{:S(2)}) copy-start(f32[2,256,32]{2,1,0:T(8,128)} %copy-done.26) | copy-start | bytes 196612
  94.6 5.5 %copy-start.29 = (f32[2,256,64]{2,1,0:T(8,128)S(1)}, f32[2,256,64]{2,1,0:T(8,128)}, u32[]{:S(2)}) copy-start(f32[2,256,64]{2,1,0:T(8,128)} %copy-done.28) | copy-start | bytes 393220
  94.6 5.5 %copy-start.32 = (f32[32]{0:T(128)S(1)}, f32[32]{0:T(128)}, u32[]{:S(2)}) copy-start(f32[32]{0:T(128)} %param.12) | copy-start | bytes 388
  94.6 13.7 %collective-permute-start.10 = (bf16[512,512]{1,0:T(8,128)(2,1)S(1)}, bf16[512,512]{1,0:T(8,128)(2,1)S(1)}, u32[]{:S(2)}, u32[]{:S(2)}) collective-permute-start(bf16[512,512]{1,0:T(8,128)(2,1)S(1)} %get-tuple-element.100.after), channel_id=1, source_target_pairs={{0,2},{1,3},{2,0},{3,1},{4,6},{5,7},{6,4},{7,5},{8,10},{9,11},{10,... | collective-permute-start | bytes 1572872 | tf_op jit(solution)/shard_map/ppermute | solution.py:23
  99.1 1.0 copy-start.15
  100.1 8.2 %copy-start.16 = (f32[512,512]{1,0:T(8,128)S(1)}, f32[512,512]{1,0:T(8,128)}, u32[]{:S(2)}) copy-start(f32[512,512]{1,0:T(8,128)} %copy-done.15) | copy-start | bytes 3145732
  108.3 4.3 %collective-permute-start.12 = (bf16[512,1280]{1,0:T(8,128)(2,1)}, bf16[512,1280]{1,0:T(8,128)(2,1)S(1)}, u32[]{:S(2)}, u32[]{:S(2)}) collective-permute-start(bf16[512,1280]{1,0:T(8,128)(2,1)} %get-tuple-element.109.after.own_ref), channel_id=1, source_target_pairs={{0,1},{1,0},{2,3},{3,2},{4,5},{5,4},{6,7},{7,6},{8,9},{9,8},{10,11... | collective-permute-start | bytes 3932168 | tf_op jit(solution)/shard_map/ppermute | solution.py:23
  108.3 1.3 copy-start.9
  109.7 3.0 %copy-start.10 = (bf16[512,1280]{1,0:T(8,128)(2,1)S(1)}, bf16[512,1280]{1,0:T(8,128)(2,1)}, u32[]{:S(2)}) copy-start(bf16[512,1280]{1,0:T(8,128)(2,1)} %get-tuple-element.109.after.own_ref) | copy-start | bytes 3932164
  110.4 8.8 %collective-permute-start.13 = (bf16[256,512]{1,0:T(8,128)(2,1)S(1)}, bf16[256,512]{1,0:T(8,128)(2,1)S(1)}, u32[]{:S(2)}, u32[]{:S(2)}) collective-permute-start(bf16[256,512]{1,0:T(8,128)(2,1)S(1)} %get-tuple-element.116), channel_id=1, source_target_pairs={{0,4},{1,5},{2,6},{3,7},{4,0},{5,1},{6,2},{7,3},{8,12},{9,13},{10,... | collective-permute-start | bytes 786440 | tf_op jit(solution)/shard_map/ppermute | solution.py:23
  111.2 8.4 %collective-permute-start.14 = (bf16[256,512]{1,0:T(8,128)(2,1)S(1)}, bf16[256,512]{1,0:T(8,128)(2,1)S(1)}, u32[]{:S(2)}, u32[]{:S(2)}) collective-permute-start(bf16[256,512]{1,0:T(8,128)(2,1)S(1)} %get-tuple-element.117), channel_id=1, source_target_pairs={{0,2},{1,3},{2,0},{3,1},{4,6},{5,7},{6,4},{7,5},{8,10},{9,11},{10,... | collective-permute-start | bytes 786440 | tf_op jit(solution)/shard_map/ppermute | solution.py:23
  119.6 18.8 %collective-permute-start.17 = (bf16[512,768]{1,0:T(8,128)(2,1)S(1)}, bf16[512,768]{1,0:T(8,128)(2,1)S(1)}, u32[]{:S(2)}, u32[]{:S(2)}) collective-permute-start(bf16[512,768]{1,0:T(8,128)(2,1)S(1)} %get-tuple-element.125), channel_id=1, source_target_pairs={{0,4},{1,5},{2,6},{3,7},{4,0},{5,1},{6,2},{7,3},{8,12},{9,13},{10,... | collective-permute-start | bytes 2359304 | tf_op jit(solution)/shard_map/ppermute | solution.py:23
  121.0 13.0 %collective-permute-start.16 = (bf16[512,512]{1,0:T(8,128)(2,1)S(1)}, bf16[512,512]{1,0:T(8,128)(2,1)S(1)}, u32[]{:S(2)}, u32[]{:S(2)}) collective-permute-start(bf16[512,512]{1,0:T(8,128)(2,1)S(1)} %get-tuple-element.124.after), channel_id=1, source_target_pairs={{0,2},{1,3},{2,0},{3,1},{4,6},{5,7},{6,4},{7,5},{8,10},{9,11},{10,... | collective-permute-start | bytes 1572872 | tf_op jit(solution)/shard_map/ppermute | solution.py:23
  122.0 7.2 %collective-permute-start.15 = (bf16[128,1024]{1,0:T(8,128)(2,1)S(1)}, bf16[128,1024]{1,0:T(8,128)(2,1)S(1)}, u32[]{:S(2)}, u32[]{:S(2)}) collective-permute-start(bf16[128,1024]{1,0:T(8,128)(2,1)S(1)} %get-tuple-element.123), channel_id=1, source_target_pairs={{0,8},{8,0},{16,24},{24,16},{1,9},{9,1},{17,25},{25,17},{2,10},{10... | collective-permute-start | bytes 786440 | tf_op jit(solution)/shard_map/ppermute | solution.py:23
  139.7 9.6 %collective-permute-start.20 = (bf16[256,768]{1,0:T(8,128)(2,1)S(1)}, bf16[256,768]{1,0:T(8,128)(2,1)S(1)}, u32[]{:S(2)}, u32[]{:S(2)}) collective-permute-start(bf16[256,768]{1,0:T(8,128)(2,1)S(1)} %get-tuple-element.134), channel_id=1, source_target_pairs={{0,2},{1,3},{2,0},{3,1},{4,6},{5,7},{6,4},{7,5},{8,10},{9,11},{10,... | collective-permute-start | bytes 1179656 | tf_op jit(solution)/shard_map/ppermute | solution.py:23
  141.3 7.9 %collective-permute-start.19 = (bf16[256,512]{1,0:T(8,128)(2,1)S(1)}, bf16[256,512]{1,0:T(8,128)(2,1)S(1)}, u32[]{:S(2)}, u32[]{:S(2)}) collective-permute-start(bf16[256,512]{1,0:T(8,128)(2,1)S(1)} %get-tuple-element.133), channel_id=1, source_target_pairs={{0,4},{1,5},{2,6},{3,7},{4,0},{5,1},{6,2},{7,3},{8,12},{9,13},{10,... | collective-permute-start | bytes 786440 | tf_op jit(solution)/shard_map/ppermute | solution.py:23
  141.9 7.3 %collective-permute-start.18 = (bf16[64,1024]{1,0:T(8,128)(2,1)S(1)}, bf16[64,1024]{1,0:T(8,128)(2,1)S(1)}, u32[]{:S(2)}, u32[]{:S(2)}) collective-permute-start(bf16[64,1024]{1,0:T(8,128)(2,1)S(1)} %get-tuple-element.132), channel_id=1, source_target_pairs={{0,16},{8,24},{16,0},{24,8},{1,17},{9,25},{17,1},{25,9},{2,18},{10... | collective-permute-start | bytes 393224 | tf_op jit(solution)/shard_map/ppermute | solution.py:23
  150.1 10.1 %collective-permute-start.22 = (bf16[128,1280]{1,0:T(8,128)(2,1)S(1)}, bf16[128,1280]{1,0:T(8,128)(2,1)S(1)}, u32[]{:S(2)}, u32[]{:S(2)}) collective-permute-start(bf16[128,1280]{1,0:T(8,128)(2,1)S(1)} %get-tuple-element.139), channel_id=1, source_target_pairs={{0,8},{8,0},{16,24},{24,16},{1,9},{9,1},{17,25},{25,17},{2,10},{10... | collective-permute-start | bytes 983048 | tf_op jit(solution)/shard_map/ppermute | solution.py:23
  151.7 7.5 %collective-permute-start.21 = (bf16[64,1024]{1,0:T(8,128)(2,1)S(1)}, bf16[64,1024]{1,0:T(8,128)(2,1)S(1)}, u32[]{:S(2)}, u32[]{:S(2)}) collective-permute-start(bf16[64,1024]{1,0:T(8,128)(2,1)S(1)} %fold.12.after), channel_id=1, source_target_pairs={{0,16},{8,24},{16,0},{24,8},{1,17},{9,25},{17,1},{25,9},{2,18},{10... | collective-permute-start | bytes 393224 | tf_op jit(solution)/shard_map/ppermute | solution.py:23
  160.2 9.7 %collective-permute-start.23 = (bf16[128,1024]{1,0:T(8,128)(2,1)S(1)}, bf16[128,1024]{1,0:T(8,128)(2,1)S(1)}, u32[]{:S(2)}, u32[]{:S(2)}) collective-permute-start(bf16[128,1024]{1,0:T(8,128)(2,1)S(1)} %pad_maximum_fusion.1.refs_0_), channel_id=1, source_target_pairs={{0,8},{8,0},{16,24},{24,16},{1,9},{9,1},{17,25},{25,17},{2,10},{10... | collective-permute-start | bytes 786440 | tf_op jit(solution)/shard_map/ppermute | solution.py:23
  163.1 6.8 %collective-permute-start.24 = (bf16[64,1280]{1,0:T(8,128)(2,1)S(1)}, bf16[64,1280]{1,0:T(8,128)(2,1)S(1)}, u32[]{:S(2)}, u32[]{:S(2)}) collective-permute-start(bf16[64,1280]{1,0:T(8,128)(2,1)S(1)} %get-tuple-element.143), channel_id=1, source_target_pairs={{0,16},{8,24},{16,0},{24,8},{1,17},{9,25},{17,1},{25,9},{2,18},{10... | collective-permute-start | bytes 491528 | tf_op jit(solution)/shard_map/ppermute | solution.py:23
  170.2 8.7 %collective-permute-start.25 = (bf16[64,1280]{1,0:T(8,128)(2,1)S(1)}, bf16[64,1280]{1,0:T(8,128)(2,1)S(1)}, u32[]{:S(2)}, u32[]{:S(2)}) collective-permute-start(bf16[64,1280]{1,0:T(8,128)(2,1)S(1)} %fold.15), channel_id=1, source_target_pairs={{0,16},{8,24},{16,0},{24,8},{1,17},{9,25},{17,1},{25,9},{2,18},{10... | collective-permute-start | bytes 491528 | tf_op jit(solution)/shard_map/ppermute | solution.py:23
  179.0 7.1 %collective-permute-start.26 = (bf16[128,1280]{1,0:T(8,128)(2,1)S(1)}, bf16[128,1280]{1,0:T(8,128)(2,1)S(1)}, u32[]{:S(2)}, u32[]{:S(2)}) collective-permute-start(bf16[128,1280]{1,0:T(8,128)(2,1)S(1)} %pad_maximum_fusion.refs_2_), channel_id=1, source_target_pairs={{0,8},{8,0},{16,24},{24,16},{1,9},{9,1},{17,25},{25,17},{2,10},{10... | collective-permute-start | bytes 983048 | tf_op jit(solution)/shard_map/ppermute | solution.py:23

commit v5 on v4

--- a/solution.py
+++ b/solution.py
@@ -340,7 +340,7 @@
         out(slot, total)
 
 
-TILE = 128
+TILE = 256
 
 
 def normed_kernel(

time: 190 us -> 188 us (0.989)
  transfers between devices with their start and end apart: 27 -> 27, of which waited for: 16 -> 16; matrix products, arithmetic and copies ran while one was open for 0% -> 0% of each run, Pallas kernels for 26% -> 27%
where the time goes in v5:
time: 188 us; the launch traced here: 187 us
  Pallas kernels  88.1 us (47%)
  waiting for transfers between devices  51.1 us (27%)
  starting transfers between devices  32.5 us (17%)
  local copies, waits for them, and re-layouts  14.3 us (8%)
    ppermute x27, waiting for transfers between devices, send(): lax.ppermute(array, axis, [(i, i ^ mask) for i in range(lax.axis_size(axi...  51.1 us
    ppermute x27, starting transfers between devices, send(): lax.ppermute(array, axis, [(i, i ^ mask) for i in range(lax.axis_size(axi...  32.5 us
    pallas_call x4, Pallas kernels, weight_terms(): pl.pallas_call(functools.partial(term_kernel, picked, pieces), grid=(own....  14.7 us
    unnamed x73, local copies, waits for them, and re-layouts  14 us
    pallas_call x1, Pallas kernels, inner_back(): pl.pallas_call(inner_back_kernel, grid=(channels // GROUP,), in_specs=[bl...  12.5 us
    pallas_call x2, Pallas kernels, finish(): pl.pallas_call(functools.partial(finish_kernel, first, len(arrived), last...  12.5 us
    pallas_call x1, Pallas kernels, project(): pl.pallas_call(project_kernel, grid=(channels // PROJECTED,), in_specs=[w...  11 us
    pallas_call x2, Pallas kernels, inner(): pl.pallas_call(functools.partial(inner_kernel, branch), grid=(channels //...  10.9 us
  transfers between devices with their start and end apart: 27, of which 16 were waited for; matrix products, arithmetic and copies ran while one was open for 0% of the time, Pallas kernels for 27%

profile of v5, /device:TPU:0, one launch (start us, length us, event | category | flops | bytes accessed | tf_op | source)
XLA Modules:
  0.0 187.4 jit_solution(17008966549950154610)
XLA Ops:
  0.6 1.1 copy-done.23
  1.7 0.7 copy-done.31
  2.4 0.7 copy-done.33
  3.0 3.9 %small.1 = (bf16[512,2048]{1,0:T(8,128)(2,1)S(1)}, f32[2,256,384]{2,1,0:T(8,128)S(1)}, f32[2,64,256]{2,1,0:T(8,128)S(1)}, bf16[2,256,384]{2,1,0:T(8,128)(2,1)S(1...) custom-call(bf16[256,2048]{1,0:T(8,128)(2,1)} %bitcast.h_ref.own_ref, ...), custom_call_target="tpu_custom_call" | custom-call | tf_op jit(solution)/shard_map/small/pallas_call | solution.py:135
  6.9 11.0 %project.1 = (bf16[2,256,2048]{2,1,0:T(8,128)(2,1)S(1)}, f32[2,72,2048]{2,1,0:T(8,128)S(1)}) custom-call(bf16[512,2048]{1,0:T(8,128)(2,1)S(1)} %get-tuple-element.76.both_ref, bf16[2048,2048]{1,0:T(8,128)(2,1)} %w_ref.1, bf16[2,128,256]{2,1,0:T(8,128)(2,1)S(1)} %get-tuple-element.77.bt_ref, bf16[2,256,96]{2,1,0:T(8,128)(2,1)S(1)} %get-tuple-element.78.weight3_ref, ...), custom_call_target="tpu_custom_call" | custom-call | tf_op jit(solution)/shard_map/project/pallas_call | solution.py:173
  18.0 1.3 copy-done
  20.2 6.5 %inner.2.after.raw_fwd_ref = f32[256,2048]{1,0:T(8,128)S(1)} custom-call(bf16[2,256,2048]{2,1,0:T(8,128)(2,1)} %copy-done, f32[2,256,384]{2,1,0:T(8,128)S(1)} %get-tuple-element.81.nat_ref.nat_fwd_ref.nat_rc_ref.refs_12_, f32[2,64,256]{2,1,0:T(8,128)S(1)} %get-tuple-element.82.lines_ref, f32[2,72,2048]{2,1,0:T(8,128)S(1)} %get-tuple-element.83.after.refs_0_.own_ref.refs_4_), custom_call_target="tpu_custom_call" | custom-call | tf_op jit(solution)/shard_map/inner/pallas_call | solution.py:235
  26.7 0.9 merge.2
  28.4 3.9 %collective-permute-start.4 = (bf16[80,2048]{1,0:T(8,128)(2,1)S(1)}, bf16[80,2048]{1,0:T(8,128)(2,1)S(1)}, u32[]{:S(2)}, u32[]{:S(2)}) collective-permute-start(bf16[80,2048]{1,0:T(8,128)(2,1)S(1)} %get-tuple-element.86), channel_id=1, source_target_pairs={{0,6},{1,7},{2,4},{3,5},{4,2},{5,3},{6,0},{7,1},{8,14},{9,15},{10,... | collective-permute-start | bytes 983048 | tf_op jit(solution)/shard_map/ppermute | solution.py:23
  32.9 4.4 %turned.1.after.left_ref = bf16[1024,1024]{1,0:T(8,128)(2,1)S(1)} custom-call(s32[8]{0:T(128)S(1)} %pad_add_fusion.where_ref, bf16[256,2048]{1,0:T(8,128)(2,1)} %bitcast.h_ref.own_ref.own_mirror_ref, bf16[256,2048]{1,0:T(8,128)(2,1)} %bitcast.h_ref.own_ref.own_mirror_ref, bf16[256,2048]{1,0:T(8,128)(2,1)} %collective-permute-done.peer_ref.peer_mirror_ref, ...), custom_call_target="tpu_custom_call" | custom-call | tf_op jit(solution)/shard_map/turned/pallas_call | solution.py:674
  37.3 1.3 copy-done.3
  38.7 4.5 %inner.3.raw_rc_ref = f32[256,2048]{1,0:T(8,128)S(1)} custom-call(bf16[2,256,2048]{2,1,0:T(8,128)(2,1)S(1)} %copy-done.1, f32[2,256,384]{2,1,0:T(8,128)S(1)} %copy-done.7, f32[2,64,256]{2,1,0:T(8,128)S(1)} %get-tuple-element.82.lines_ref, bf16[1024,1024]{1,0:T(8,128)(2,1)} %copy-done.3), custom_call_target="tpu_custom_call" | custom-call | tf_op jit(solution)/shard_map/inner/pallas_call | solution.py:235
  43.1 1.4 copy-done.13
  44.5 2.9 %collective-permute-done.2.refs_0_ = bf16[80,2048]{1,0:T(8,128)(2,1)S(1)} collective-permute-done((bf16[80,2048]{1,0:T(8,128)(2,1)S(1)}, bf16[80,2048]{1,0:T(8,128)(2,1)S(1)}, u32[]{:S(2)}, u32[]{:S(2)}) %collective-permute-start.2) | collective-permute-done | bytes 327712 | tf_op jit(solution)/shard_map/ppermute | solution.py:23
  47.5 9.9 %normed.1 = (bf16[256,2048]{1,0:T(8,128)(2,1)}, bf16[2,256,2048]{2,1,0:T(8,128)(2,1)}, f32[2,256,32]{2,1,0:T(8,128)S(1)}, f32[2,64,2048]{2,1,0:T(8,128)S(1)}, f3...) custom-call(f32[256,2048]{1,0:T(8,128)} %copy-done.8, ...), custom_call_target="tpu_custom_call" | custom-call | tf_op jit(solution)/shard_map/normed/pallas_call | solution.py:425
  57.4 1.0 copy-done.17
  58.4 2.7 %collective-permute-done.5.refs_2_.refs_7_ = f32[2,64,2048]{2,1,0:T(8,128)S(1)} collective-permute-done((f32[2,64,2048]{2,1,0:T(8,128)S(1)}, f32[2,64,2048]{2,1,0:T(8,128)S(1)}, u32[]{:S(2)}, u32[]{:S(2)}) %collective-permute-start.5) | collective-permute-done | bytes 1048608 | tf_op jit(solution)/shard_map/ppermute | solution.py:23
  61.1 1.6 merge.3
  62.6 1.0 copy-done.11
  63.6 1.5 collective-permute-start.6
  65.1 1.4 collective-permute-start.8
  66.5 0.6 collective-permute-start.7
  67.2 1.6 copy-done.19
  68.8 12.5 %inner_back.1 = (f32[2,256,2048]{2,1,0:T(8,128)}, f32[2,256,64]{2,1,0:T(8,128)S(1)}, f32[2,256,64]{2,1,0:T(8,128)S(1)}) custom-call(bf16[2,256,2048]{2,1,0:T(8,128)(2,1)S(1)} %copy-done.2, bf16[2,256,2048]{2,1,0:T(8,128)(2,1)S(1)} %copy-done.19, f32[2,256,384]{2,1,0:T(8,128)S(1)} %copy-done.7, f32[2,64,256]{2,1,0:T(8,128)S(1)} %get-tuple-element.82.lines_ref, ...), custom_call_target="tpu_custom_call" | custom-call | tf_op jit(solution)/shard_map/inner_back/pallas_call | solution.py:525
  81.4 5.3 %finish.2 = (bf16[512,1024]{1,0:T(8,128)(2,1)S(1)}, f32[2,256,64]{2,1,0:T(8,128)S(1)}, f32[2,256,32]{2,1,0:T(8,128)S(1)}, f32[2,1,32]{2,1,0:T(1,128)S(1)}) custom-call(bf16[2,256,2048]{2,1,0:T(8,128)(2,1)} %copy-done, f32[2,256,2048]{2,1,0:T(8,128)} %get-tuple-element.93.refs_1_, bf16[2,256,384]{2,1,0:T(8,128)(2,1)S(1)} %copy-done.21, ...), custom_call_target="tpu_custom_call" | custom-call | tf_op jit(solution)/shard_map/finish/pallas_call | solution.py:630
  86.7 2.6 %collective-permute-done.9.peer_ref = bf16[512,1024]{1,0:T(8,128)(2,1)S(1)} collective-permute-done((bf16[512,1024]{1,0:T(8,128)(2,1)S(1)}, bf16[512,1024]{1,0:T(8,128)(2,1)S(1)}, u32[]{:S(2)}, u32[]{:S(2)}) %collective-permute-start.9) | collective-permute-done | bytes 1048608 | tf_op jit(solution)/shard_map/ppermute | solution.py:23
  89.4 2.3 %terms.4 = (bf16[512,512]{1,0:T(8,128)(2,1)S(1)}, bf16[512,512]{1,0:T(8,128)(2,1)S(1)}) custom-call(bf16[1024,1024]{1,0:T(8,128)(2,1)S(1)} %copy-done.4, bf16[512,1024]{1,0:T(8,128)(2,1)S(1)} %get-tuple-element.98.own_ref, bf16[512,1024]{1,0:T(8,128)(2,1)S(1)} %collective-permute-done.9.peer_ref, f32[2,1,32]{2,1,0:T(1,128)S(1)} %get-tuple-element.99.after.refs_20_), custom_call_target="tpu_custom_call" | custom-call | tf_op jit(solution)/shard_map/terms/pallas_call | solution.py:728
  91.7 1.5 collective-permute-start.11
  93.1 0.6 collective-permute-start.10
  93.7 3.9 %terms.5 = (f32[512,512]{1,0:T(8,128)S(1)}, f32[512,512]{1,0:T(8,128)S(1)}) custom-call(bf16[1024,1024]{1,0:T(8,128)(2,1)} %copy-done.3, bf16[512,1024]{1,0:T(8,128)(2,1)S(1)} %get-tuple-element.98.own_ref, bf16[512,1024]{1,0:T(8,128)(2,1)S(1)} %collective-permute-done.9.peer_ref, bf16[512,512]{1,0:T(8,128)(2,1)S(1)} %get-tuple-element.100.after), custom_call_target="tpu_custom_call" | custom-call | tf_op jit(solution)/shard_map/terms/pallas_call | solution.py:728
  97.6 1.0 copy-done.15
  98.6 7.2 %finish.3 = (bf16[512,1280]{1,0:T(8,128)(2,1)}, f32[2,256,64]{2,1,0:T(8,128)}, f32[2,256,32]{2,1,0:T(8,128)}, f32[2,1,32]{2,1,0:T(1,128)}) custom-call(bf16[2,256,2048]{2,1,0:T(8,128)(2,1)} %copy-done, f32[2,256,2048]{2,1,0:T(8,128)} %get-tuple-element.93.refs_1_, bf16[2,256,384]{2,1,0:T(8,128)(2,1)S(1)} %copy-done.21, f32[2,64,2048]{2,1,0:T(8,128)S(1)} %copy-done.18, ...), custom_call_target="tpu_custom_call" | custom-call | tf_op jit(solution)/shard_map/finish/pallas_call | solution.py:630
  105.9 0.9 collective-permute-done.10.refs_1_
  106.8 1.3 copy-done.9
  108.1 0.8 fold.8
  108.9 0.8 collective-permute-start.13
  109.7 1.4 collective-permute-start.14
  111.1 4.2 %terms.6 = (bf16[512,512]{1,0:T(8,128)(2,1)S(1)}, bf16[512,768]{1,0:T(8,128)(2,1)S(1)}) custom-call(bf16[1024,1024]{1,0:T(8,128)(2,1)} %copy-done.3, bf16[512,1280]{1,0:T(8,128)(2,1)S(1)} %copy-done.10, bf16[512,1280]{1,0:T(8,128)(2,1)S(1)} %collective-permute-done.12.peer_ref, f32[256,512]{1,0:T(8,128)S(1)} %get-tuple-element.113.after.refs_0_), custom_call_target="tpu_custom_call" | custom-call | tf_op jit(solution)/shard_map/terms/pallas_call | solution.py:728
  115.4 2.3 %collective-permute-done.13.refs_1_ = bf16[256,512]{1,0:T(8,128)(2,1)S(1)} collective-permute-done((bf16[256,512]{1,0:T(8,128)(2,1)S(1)}, bf16[256,512]{1,0:T(8,128)(2,1)S(1)}, u32[]{:S(2)}, u32[]{:S(2)}) %collective-permute-start.13) | collective-permute-done | bytes 262176 | tf_op jit(solution)/shard_map/ppermute | solution.py:23
  118.1 1.4 collective-permute-start.17
  119.4 0.6 collective-permute-start.16
  120.5 1.8 collective-permute-start.15
  122.4 4.3 %terms.7 = (f32[512,512]{1,0:T(8,128)S(1)}, f32[512,768]{1,0:T(8,128)S(1)}) custom-call(bf16[1024,1024]{1,0:T(8,128)(2,1)} %copy-done.3, bf16[512,1280]{1,0:T(8,128)(2,1)S(1)} %copy-done.10, bf16[512,1280]{1,0:T(8,128)(2,1)S(1)} %collective-permute-done.12.peer_ref, f32[128,1024]{1,0:T(8,128)S(1)} %get-tuple-element.121.after.refs_0_), custom_call_target="tpu_custom_call" | custom-call | tf_op jit(solution)/shard_map/terms/pallas_call | solution.py:728
  126.7 1.1 collective-permute-done.15.refs_1_
  127.7 4.7 %collective-permute-done.16.refs_1_ = bf16[512,512]{1,0:T(8,128)(2,1)S(1)} collective-permute-done((bf16[512,512]{1,0:T(8,128)(2,1)S(1)}, bf16[512,512]{1,0:T(8,128)(2,1)S(1)}, u32[]{:S(2)}, u32[]{:S(2)}) %collective-permute-start.16) | collective-permute-done | bytes 524320 | tf_op jit(solution)/shard_map/ppermute | solution.py:23
  132.4 4.5 %collective-permute-done.17.refs_3_ = bf16[512,768]{1,0:T(8,128)(2,1)S(1)} collective-permute-done((bf16[512,768]{1,0:T(8,128)(2,1)S(1)}, bf16[512,768]{1,0:T(8,128)(2,1)S(1)}, u32[]{:S(2)}, u32[]{:S(2)}) %collective-permute-start.17) | collective-permute-done | bytes 786464 | tf_op jit(solution)/shard_map/ppermute | solution.py:23
  137.2 1.0 fold.11
  138.2 1.5 collective-permute-start.20
  139.7 0.6 collective-permute-start.19
  140.3 2.7 %collective-permute-start.18 = (bf16[64,1024]{1,0:T(8,128)(2,1)S(1)}, bf16[64,1024]{1,0:T(8,128)(2,1)S(1)}, u32[]{:S(2)}, u32[]{:S(2)}) collective-permute-start(bf16[64,1024]{1,0:T(8,128)(2,1)S(1)} %get-tuple-element.132), channel_id=1, source_target_pairs={{0,16},{8,24},{16,0},{24,8},{1,17},{9,25},{17,1},{25,9},{2,18},{10... | collective-permute-start | bytes 393224 | tf_op jit(solution)/shard_map/ppermute | solution.py:23
  143.0 4.6 %collective-permute-done.18.refs_1_ = bf16[64,1024]{1,0:T(8,128)(2,1)S(1)} collective-permute-done((bf16[64,1024]{1,0:T(8,128)(2,1)S(1)}, bf16[64,1024]{1,0:T(8,128)(2,1)S(1)}, u32[]{:S(2)}, u32[]{:S(2)}) %collective-permute-start.18) | collective-permute-done | bytes 131104 | tf_op jit(solution)/shard_map/ppermute | solution.py:23
  148.0 0.6 fold.13
  148.6 1.6 collective-permute-start.22
  150.2 2.6 %collective-permute-start.21 = (bf16[64,1024]{1,0:T(8,128)(2,1)S(1)}, bf16[64,1024]{1,0:T(8,128)(2,1)S(1)}, u32[]{:S(2)}, u32[]{:S(2)}) collective-permute-start(bf16[64,1024]{1,0:T(8,128)(2,1)S(1)} %fold.12.after), channel_id=1, source_target_pairs={{0,16},{8,24},{16,0},{24,8},{1,17},{9,25},{17,1},{25,9},{2,18},{10... | collective-permute-start | bytes 393224 | tf_op jit(solution)/shard_map/ppermute | solution.py:23
  152.8 4.9 %collective-permute-done.21 = bf16[64,1024]{1,0:T(8,128)(2,1)S(1)} collective-permute-done((bf16[64,1024]{1,0:T(8,128)(2,1)S(1)}, bf16[64,1024]{1,0:T(8,128)(2,1)S(1)}, u32[]{:S(2)}, u32[]{:S(2)}) %collective-permute-start.21) | collective-permute-done | bytes 131104 | tf_op jit(solution)/shard_map/ppermute | solution.py:23
  157.7 1.0 collective-permute-done.22.refs_1_
  158.7 2.6 %collective-permute-start.23 = (bf16[128,1024]{1,0:T(8,128)(2,1)S(1)}, bf16[128,1024]{1,0:T(8,128)(2,1)S(1)}, u32[]{:S(2)}, u32[]{:S(2)}) collective-permute-start(bf16[128,1024]{1,0:T(8,128)(2,1)S(1)} %pad_maximum_fusion.1.refs_0_), channel_id=1, source_target_pairs={{0,8},{8,0},{16,24},{24,16},{1,9},{9,1},{17,25},{25,17},{2,10},{10... | collective-permute-start | bytes 786440 | tf_op jit(solution)/shard_map/ppermute | solution.py:23
  161.6 1.6 collective-permute-start.24
  163.3 5.2 %collective-permute-done.24.refs_1_ = bf16[64,1280]{1,0:T(8,128)(2,1)S(1)} collective-permute-done((bf16[64,1280]{1,0:T(8,128)(2,1)S(1)}, bf16[64,1280]{1,0:T(8,128)(2,1)S(1)}, u32[]{:S(2)}, u32[]{:S(2)}) %collective-permute-start.24) | collective-permute-done | bytes 163872 | tf_op jit(solution)/shard_map/ppermute | solution.py:23
  168.7 2.5 %collective-permute-start.25 = (bf16[64,1280]{1,0:T(8,128)(2,1)S(1)}, bf16[64,1280]{1,0:T(8,128)(2,1)S(1)}, u32[]{:S(2)}, u32[]{:S(2)}) collective-permute-start(bf16[64,1280]{1,0:T(8,128)(2,1)S(1)} %fold.15), channel_id=1, source_target_pairs={{0,16},{8,24},{16,0},{24,8},{1,17},{9,25},{17,1},{25,9},{2,18},{10... | collective-permute-start | bytes 491528 | tf_op jit(solution)/shard_map/ppermute | solution.py:23
  171.2 6.2 %collective-permute-done.25 = bf16[64,1280]{1,0:T(8,128)(2,1)S(1)} collective-permute-done((bf16[64,1280]{1,0:T(8,128)(2,1)S(1)}, bf16[64,1280]{1,0:T(8,128)(2,1)S(1)}, u32[]{:S(2)}, u32[]{:S(2)}) %collective-permute-start.25) | collective-permute-done | bytes 163872 | tf_op jit(solution)/shard_map/ppermute | solution.py:23
  177.7 6.9 %collective-permute-done.26.refs_3_ = bf16[128,1280]{1,0:T(8,128)(2,1)S(1)} collective-permute-done((bf16[128,1280]{1,0:T(8,128)(2,1)S(1)}, bf16[128,1280]{1,0:T(8,128)(2,1)S(1)}, u32[]{:S(2)}, u32[]{:S(2)}) %collective-permute-start.26) | collective-permute-done | bytes 327712 | tf_op jit(solution)/shard_map/ppermute | solution.py:23
  184.6 2.0 %placed.1 = (f32[256,2048]{1,0:T(8,128)}, f32[256,160]{1,0:T(8,128)S(1)}) custom-call(s32[8]{0:T(128)S(1)} %pad_add_fusion.where_ref, bf16[128,1024]{1,0:T(8,128)(2,1)S(1)} %pad_maximum_fusion.1.refs_0_, bf16[128,1024]{1,0:T(8,128)(2,1)S(1)} %collective-permute-done.23.refs_1_, bf16[128,1280]{1,0:T(8,128)(2,1)S(1)} %pad_maximum_fusion.refs_2_, ...), custom_call_target="tpu_custom_call" | custom-call | tf_op jit(solution)/shard_map/placed/pallas_call | solution.py:826
  186.6 0.8 copy.12
  (100 shorter events, 4.9 us)
Async XLA Ops:
  0.6 1.1 copy-start.23
  1.7 0.7 copy-start.31
  2.4 0.7 copy-start.33
  6.9 11.0 %copy-start.20 = (bf16[2,256,384]{2,1,0:T(8,128)(2,1)}, bf16[2,256,384]{2,1,0:T(8,128)(2,1)S(1)}, u32[]{:S(2)}) copy-start(bf16[2,256,384]{2,1,0:T(8,128)(2,1)S(1)} %get-tuple-element.94.refs_2_) | copy-start | bytes 1179652
  6.9 11.0 %copy-start.24 = (bf16[2,256,384]{2,1,0:T(8,128)(2,1)}, bf16[2,256,384]{2,1,0:T(8,128)(2,1)S(1)}, u32[]{:S(2)}) copy-start(bf16[2,256,384]{2,1,0:T(8,128)(2,1)S(1)} %get-tuple-element.85.cg3_ref) | copy-start | bytes 1179652
  6.9 13.3 %copy-start.6 = (f32[2,256,384]{2,1,0:T(8,128)}, f32[2,256,384]{2,1,0:T(8,128)S(1)}, u32[]{:S(2)}) copy-start(f32[2,256,384]{2,1,0:T(8,128)S(1)} %get-tuple-element.81.nat_ref.nat_fwd_ref.nat_rc_ref.refs_12_) | copy-start | bytes 2359300
  6.9 13.1 %copy-start.35 = (s32[2]{0:T(128)S(1)}, s32[2]{0:T(128)}, u32[]{:S(2)}) copy-start(s32[2]{0:T(128)} %constant.42.clone) | copy-start | bytes 28
  18.0 1.3 copy-start
  19.3 7.4 %copy-start.5 = (f32[2,72,2048]{2,1,0:T(8,128)}, f32[2,72,2048]{2,1,0:T(8,128)S(1)}, u32[]{:S(2)}) copy-start(f32[2,72,2048]{2,1,0:T(8,128)S(1)} %get-tuple-element.83.after.refs_0_.own_ref.refs_4_) | copy-start | bytes 3538948
  19.3 7.4 %collective-permute-start.1 = (f32[2,72,2048]{2,1,0:T(8,128)S(1)}, f32[2,72,2048]{2,1,0:T(8,128)S(1)}, u32[]{:S(2)}, u32[]{:S(2)}) collective-permute-start(f32[2,72,2048]{2,1,0:T(8,128)S(1)} %get-tuple-element.83.after.refs_0_.own_ref.refs_4_), channel_id=1, source_target_pairs={{0,1},{1,0},{2,3},{3,2},{4,5},{5,4},{6,7},{7,6},{8,9},{9,8},{10,11... | collective-permute-start | bytes 3538952 | tf_op jit(solution)/shard_map/ppermute | solution.py:23
  19.7 13.2 %collective-permute-start = (bf16[256,2048]{1,0:T(8,128)(2,1)}, bf16[256,2048]{1,0:T(8,128)(2,1)}, u32[]{:S(2)}, u32[]{:S(2)}) collective-permute-start(bf16[256,2048]{1,0:T(8,128)(2,1)} %bitcast.h_ref.own_ref.own_mirror_ref), channel_id=1, source_target_pairs={{0,1},{1,0},{2,3},{3,2},{4,5},{5,4},{6,7},{7,6},{8,9},{9,8},{10,11... | collective-permute-start | bytes 3145736 | tf_op jit(solution)/shard_map/ppermute | solution.py:23
  26.7 1.4 copy-start.8
  26.7 6.2 %copy-start.34 = (s32[4]{0:T(128)S(1)}, s32[4]{0:T(128)}, u32[]{:S(2)}) copy-start(s32[4]{0:T(128)} %constant.43.clone) | copy-start | bytes 52
  26.7 1.7 copy-start.14
  28.4 19.1 %collective-permute-start.4 = (bf16[80,2048]{1,0:T(8,128)(2,1)S(1)}, bf16[80,2048]{1,0:T(8,128)(2,1)S(1)}, u32[]{:S(2)}, u32[]{:S(2)}) collective-permute-start(bf16[80,2048]{1,0:T(8,128)(2,1)S(1)} %get-tuple-element.86), channel_id=1, source_target_pairs={{0,6},{1,7},{2,4},{3,5},{4,2},{5,3},{6,0},{7,1},{8,14},{9,15},{10,... | collective-permute-start | bytes 983048 | tf_op jit(solution)/shard_map/ppermute | solution.py:23
  32.3 15.2 %collective-permute-start.3 = (bf16[80,2048]{1,0:T(8,128)(2,1)S(1)}, bf16[80,2048]{1,0:T(8,128)(2,1)S(1)}, u32[]{:S(2)}, u32[]{:S(2)}) collective-permute-start(bf16[80,2048]{1,0:T(8,128)(2,1)S(1)} %get-tuple-element.86), channel_id=1, source_target_pairs={{0,4},{1,5},{2,6},{3,7},{4,0},{5,1},{6,2},{7,3},{8,12},{9,13},{10,... | collective-permute-start | bytes 983048 | tf_op jit(solution)/shard_map/ppermute | solution.py:23
  32.8 14.7 %collective-permute-start.2 = (bf16[80,2048]{1,0:T(8,128)(2,1)S(1)}, bf16[80,2048]{1,0:T(8,128)(2,1)S(1)}, u32[]{:S(2)}, u32[]{:S(2)}) collective-permute-start(bf16[80,2048]{1,0:T(8,128)(2,1)S(1)} %get-tuple-element.84.after), channel_id=1, source_target_pairs={{0,2},{1,3},{2,0},{3,1},{4,6},{5,7},{6,4},{7,5},{8,10},{9,11},{10,... | collective-permute-start | bytes 983048 | tf_op jit(solution)/shard_map/ppermute | solution.py:23
  32.9 5.7 %copy-start.1 = (bf16[2,256,2048]{2,1,0:T(8,128)(2,1)S(1)}, bf16[2,256,2048]{2,1,0:T(8,128)(2,1)}, u32[]{:S(2)}) copy-start(bf16[2,256,2048]{2,1,0:T(8,128)(2,1)} %copy-done) | copy-start | bytes 6291460
  32.9 5.7 %copy-start.7 = (f32[2,256,384]{2,1,0:T(8,128)S(1)}, f32[2,256,384]{2,1,0:T(8,128)}, u32[]{:S(2)}) copy-start(f32[2,256,384]{2,1,0:T(8,128)} %copy-done.6) | copy-start | bytes 2359300
  37.3 1.3 copy-start.3
  38.7 8.8 %copy-start.22 = (bf16[1,256,2048]{2,1,0:T(8,128)(2,1)S(1)}, bf16[1,256,2048]{2,1,0:T(8,128)(2,1)}, u32[]{:S(2)}) copy-start(bf16[1,256,2048]{2,1,0:T(8,128)(2,1)} %param.15) | copy-start | bytes 3145732
  38.7 8.8 %copy-start.25 = (bf16[2,256,384]{2,1,0:T(8,128)(2,1)S(1)}, bf16[2,256,384]{2,1,0:T(8,128)(2,1)}, u32[]{:S(2)}) copy-start(bf16[2,256,384]{2,1,0:T(8,128)(2,1)} %copy-done.24) | copy-start | bytes 1179652
  38.7 8.8 %copy-start.30 = (f32[2048]{0:T(1024)S(1)}, f32[2048]{0:T(1024)}, u32[]{:S(2)}) copy-start(f32[2048]{0:T(1024)} %param.14) | copy-start | bytes 24580
  43.1 1.4 copy-start.13
  57.4 1.0 copy-start.17
  58.4 4.2 %copy-start.26 = (f32[2,256,32]{2,1,0:T(8,128)}, f32[2,256,32]{2,1,0:T(8,128)S(1)}, u32[]{:S(2)}) copy-start(f32[2,256,32]{2,1,0:T(8,128)S(1)} %get-tuple-element.104.refs_16_) | copy-start | bytes 196612
  58.4 5.2 %copy-start.28 = (f32[2,256,64]{2,1,0:T(8,128)}, f32[2,256,64]{2,1,0:T(8,128)S(1)}, u32[]{:S(2)}) copy-start(f32[2,256,64]{2,1,0:T(8,128)S(1)} %get-tuple-element.103.refs_15_) | copy-start | bytes 393220
  58.4 8.8 %copy-start.2 = (bf16[2,256,2048]{2,1,0:T(8,128)(2,1)S(1)}, bf16[2,256,2048]{2,1,0:T(8,128)(2,1)}, u32[]{:S(2)}) copy-start(bf16[2,256,2048]{2,1,0:T(8,128)(2,1)} %copy-done) | copy-start | bytes 6291460
  58.4 2.7 %collective-permute-start.5 = (f32[2,64,2048]{2,1,0:T(8,128)S(1)}, f32[2,64,2048]{2,1,0:T(8,128)S(1)}, u32[]{:S(2)}, u32[]{:S(2)}) collective-permute-start(f32[2,64,2048]{2,1,0:T(8,128)S(1)} %get-tuple-element.90.after.refs_1_), channel_id=1, source_target_pairs={{0,1},{1,0},{2,3},{3,2},{4,5},{5,4},{6,7},{7,6},{8,9},{9,8},{10,11... | collective-permute-start | bytes 3145736 | tf_op jit(solution)/shard_map/ppermute | solution.py:23
  62.6 1.0 copy-start.11
  63.6 17.7 %collective-permute-start.6 = (bf16[64,2048]{1,0:T(8,128)(2,1)}, bf16[64,2048]{1,0:T(8,128)(2,1)S(1)}, u32[]{:S(2)}, u32[]{:S(2)}) collective-permute-start(bf16[64,2048]{1,0:T(8,128)(2,1)} %get-tuple-element.92.after), channel_id=1, source_target_pairs={{0,2},{1,3},{2,0},{3,1},{4,6},{5,7},{6,4},{7,5},{8,10},{9,11},{10,... | collective-permute-start | bytes 786440 | tf_op jit(solution)/shard_map/ppermute | solution.py:23
  65.1 16.2 %collective-permute-start.8 = (bf16[64,2048]{1,0:T(8,128)(2,1)}, bf16[64,2048]{1,0:T(8,128)(2,1)}, u32[]{:S(2)}, u32[]{:S(2)}) collective-permute-start(bf16[64,2048]{1,0:T(8,128)(2,1)} %get-tuple-element.96), channel_id=1, source_target_pairs={{0,6},{1,7},{2,4},{3,5},{4,2},{5,3},{6,0},{7,1},{8,14},{9,15},{10,... | collective-permute-start | bytes 786440 | tf_op jit(solution)/shard_map/ppermute | solution.py:23
  66.5 14.8 %collective-permute-start.7 = (bf16[64,2048]{1,0:T(8,128)(2,1)}, bf16[64,2048]{1,0:T(8,128)(2,1)}, u32[]{:S(2)}, u32[]{:S(2)}) collective-permute-start(bf16[64,2048]{1,0:T(8,128)(2,1)} %get-tuple-element.96), channel_id=1, source_target_pairs={{0,4},{1,5},{2,6},{3,7},{4,0},{5,1},{6,2},{7,3},{8,12},{9,13},{10,... | collective-permute-start | bytes 786440 | tf_op jit(solution)/shard_map/ppermute | solution.py:23
  67.2 1.6 copy-start.19
  68.8 12.6 %copy-start.12 = (f32[2,64,2048]{2,1,0:T(8,128)S(1)}, f32[2,64,2048]{2,1,0:T(8,128)}, u32[]{:S(2)}) copy-start(f32[2,64,2048]{2,1,0:T(8,128)} %copy-done.11) | copy-start | bytes 3145732
  68.8 12.6 %copy-start.18 = (f32[2,64,2048]{2,1,0:T(8,128)S(1)}, f32[2,64,2048]{2,1,0:T(8,128)}, u32[]{:S(2)}) copy-start(f32[2,64,2048]{2,1,0:T(8,128)} %copy-done.17) | copy-start | bytes 3145732
  68.8 12.6 %copy-start.21 = (bf16[2,256,384]{2,1,0:T(8,128)(2,1)S(1)}, bf16[2,256,384]{2,1,0:T(8,128)(2,1)}, u32[]{:S(2)}) copy-start(bf16[2,256,384]{2,1,0:T(8,128)(2,1)} %copy-done.20) | copy-start | bytes 1179652
  81.4 8.0 %copy-start.4 = (bf16[1024,1024]{1,0:T(8,128)(2,1)S(1)}, bf16[1024,1024]{1,0:T(8,128)(2,1)}, u32[]{:S(2)}) copy-start(bf16[1024,1024]{1,0:T(8,128)(2,1)} %copy-done.3) | copy-start | bytes 6291460
  86.6 2.7 %collective-permute-start.9 = (bf16[512,1024]{1,0:T(8,128)(2,1)S(1)}, bf16[512,1024]{1,0:T(8,128)(2,1)S(1)}, u32[]{:S(2)}, u32[]{:S(2)}) collective-permute-start(bf16[512,1024]{1,0:T(8,128)(2,1)S(1)} %get-tuple-element.98.own_ref), channel_id=1, source_target_pairs={{0,1},{1,0},{2,3},{3,2},{4,5},{5,4},{6,7},{7,6},{8,9},{9,8},{10,11... | collective-permute-start | bytes 3145736 | tf_op jit(solution)/shard_map/ppermute | solution.py:23
  91.7 14.2 %collective-permute-start.11 = (bf16[512,512]{1,0:T(8,128)(2,1)S(1)}, bf16[512,512]{1,0:T(8,128)(2,1)S(1)}, u32[]{:S(2)}, u32[]{:S(2)}) collective-permute-start(bf16[512,512]{1,0:T(8,128)(2,1)S(1)} %get-tuple-element.108), channel_id=1, source_target_pairs={{0,4},{1,5},{2,6},{3,7},{4,0},{5,1},{6,2},{7,3},{8,12},{9,13},{10,... | collective-permute-start | bytes 1572872 | tf_op jit(solution)/shard_map/ppermute | solution.py:23
  93.1 5.5 %copy-start.27 = (f32[2,256,32]{2,1,0:T(8,128)S(1)}, f32[2,256,32]{2,1,0:T(8,128)}, u32[]{:S(2)}) copy-start(f32[2,256,32]{2,1,0:T(8,128)} %copy-done.26) | copy-start | bytes 196612
  93.1 5.5 %copy-start.29 = (f32[2,256,64]{2,1,0:T(8,128)S(1)}, f32[2,256,64]{2,1,0:T(8,128)}, u32[]{:S(2)}) copy-start(f32[2,256,64]{2,1,0:T(8,128)} %copy-done.28) | copy-start | bytes 393220
  93.1 5.5 %copy-start.32 = (f32[32]{0:T(128)S(1)}, f32[32]{0:T(128)}, u32[]{:S(2)}) copy-start(f32[32]{0:T(128)} %param.12) | copy-start | bytes 388
  93.1 13.7 %collective-permute-start.10 = (bf16[512,512]{1,0:T(8,128)(2,1)S(1)}, bf16[512,512]{1,0:T(8,128)(2,1)S(1)}, u32[]{:S(2)}, u32[]{:S(2)}) collective-permute-start(bf16[512,512]{1,0:T(8,128)(2,1)S(1)} %get-tuple-element.100.after), channel_id=1, source_target_pairs={{0,2},{1,3},{2,0},{3,1},{4,6},{5,7},{6,4},{7,5},{8,10},{9,11},{10,... | collective-permute-start | bytes 1572872 | tf_op jit(solution)/shard_map/ppermute | solution.py:23
  97.6 1.0 copy-start.15
  98.6 8.2 %copy-start.16 = (f32[512,512]{1,0:T(8,128)S(1)}, f32[512,512]{1,0:T(8,128)}, u32[]{:S(2)}) copy-start(f32[512,512]{1,0:T(8,128)} %copy-done.15) | copy-start | bytes 3145732
  106.8 4.3 %collective-permute-start.12 = (bf16[512,1280]{1,0:T(8,128)(2,1)}, bf16[512,1280]{1,0:T(8,128)(2,1)S(1)}, u32[]{:S(2)}, u32[]{:S(2)}) collective-permute-start(bf16[512,1280]{1,0:T(8,128)(2,1)} %get-tuple-element.109.after.own_ref), channel_id=1, source_target_pairs={{0,1},{1,0},{2,3},{3,2},{4,5},{5,4},{6,7},{7,6},{8,9},{9,8},{10,11... | collective-permute-start | bytes 3932168 | tf_op jit(solution)/shard_map/ppermute | solution.py:23
  106.8 1.3 copy-start.9
  108.1 3.0 %copy-start.10 = (bf16[512,1280]{1,0:T(8,128)(2,1)S(1)}, bf16[512,1280]{1,0:T(8,128)(2,1)}, u32[]{:S(2)}) copy-start(bf16[512,1280]{1,0:T(8,128)(2,1)} %get-tuple-element.109.after.own_ref) | copy-start | bytes 3932164
  108.9 8.8 %collective-permute-start.13 = (bf16[256,512]{1,0:T(8,128)(2,1)S(1)}, bf16[256,512]{1,0:T(8,128)(2,1)S(1)}, u32[]{:S(2)}, u32[]{:S(2)}) collective-permute-start(bf16[256,512]{1,0:T(8,128)(2,1)S(1)} %get-tuple-element.116), channel_id=1, source_target_pairs={{0,4},{1,5},{2,6},{3,7},{4,0},{5,1},{6,2},{7,3},{8,12},{9,13},{10,... | collective-permute-start | bytes 786440 | tf_op jit(solution)/shard_map/ppermute | solution.py:23
  109.7 8.4 %collective-permute-start.14 = (bf16[256,512]{1,0:T(8,128)(2,1)S(1)}, bf16[256,512]{1,0:T(8,128)(2,1)S(1)}, u32[]{:S(2)}, u32[]{:S(2)}) collective-permute-start(bf16[256,512]{1,0:T(8,128)(2,1)S(1)} %get-tuple-element.117), channel_id=1, source_target_pairs={{0,2},{1,3},{2,0},{3,1},{4,6},{5,7},{6,4},{7,5},{8,10},{9,11},{10,... | collective-permute-start | bytes 786440 | tf_op jit(solution)/shard_map/ppermute | solution.py:23
  118.1 18.8 %collective-permute-start.17 = (bf16[512,768]{1,0:T(8,128)(2,1)S(1)}, bf16[512,768]{1,0:T(8,128)(2,1)S(1)}, u32[]{:S(2)}, u32[]{:S(2)}) collective-permute-start(bf16[512,768]{1,0:T(8,128)(2,1)S(1)} %get-tuple-element.125), channel_id=1, source_target_pairs={{0,4},{1,5},{2,6},{3,7},{4,0},{5,1},{6,2},{7,3},{8,12},{9,13},{10,... | collective-permute-start | bytes 2359304 | tf_op jit(solution)/shard_map/ppermute | solution.py:23
  119.4 13.0 %collective-permute-start.16 = (bf16[512,512]{1,0:T(8,128)(2,1)S(1)}, bf16[512,512]{1,0:T(8,128)(2,1)S(1)}, u32[]{:S(2)}, u32[]{:S(2)}) collective-permute-start(bf16[512,512]{1,0:T(8,128)(2,1)S(1)} %get-tuple-element.124.after), channel_id=1, source_target_pairs={{0,2},{1,3},{2,0},{3,1},{4,6},{5,7},{6,4},{7,5},{8,10},{9,11},{10,... | collective-permute-start | bytes 1572872 | tf_op jit(solution)/shard_map/ppermute | solution.py:23
  120.5 7.2 %collective-permute-start.15 = (bf16[128,1024]{1,0:T(8,128)(2,1)S(1)}, bf16[128,1024]{1,0:T(8,128)(2,1)S(1)}, u32[]{:S(2)}, u32[]{:S(2)}) collective-permute-start(bf16[128,1024]{1,0:T(8,128)(2,1)S(1)} %get-tuple-element.123), channel_id=1, source_target_pairs={{0,8},{8,0},{16,24},{24,16},{1,9},{9,1},{17,25},{25,17},{2,10},{10... | collective-permute-start | bytes 786440 | tf_op jit(solution)/shard_map/ppermute | solution.py:23
  138.2 9.6 %collective-permute-start.20 = (bf16[256,768]{1,0:T(8,128)(2,1)S(1)}, bf16[256,768]{1,0:T(8,128)(2,1)S(1)}, u32[]{:S(2)}, u32[]{:S(2)}) collective-permute-start(bf16[256,768]{1,0:T(8,128)(2,1)S(1)} %get-tuple-element.134), channel_id=1, source_target_pairs={{0,2},{1,3},{2,0},{3,1},{4,6},{5,7},{6,4},{7,5},{8,10},{9,11},{10,... | collective-permute-start | bytes 1179656 | tf_op jit(solution)/shard_map/ppermute | solution.py:23
  139.7 7.9 %collective-permute-start.19 = (bf16[256,512]{1,0:T(8,128)(2,1)S(1)}, bf16[256,512]{1,0:T(8,128)(2,1)S(1)}, u32[]{:S(2)}, u32[]{:S(2)}) collective-permute-start(bf16[256,512]{1,0:T(8,128)(2,1)S(1)} %get-tuple-element.133), channel_id=1, source_target_pairs={{0,4},{1,5},{2,6},{3,7},{4,0},{5,1},{6,2},{7,3},{8,12},{9,13},{10,... | collective-permute-start | bytes 786440 | tf_op jit(solution)/shard_map/ppermute | solution.py:23
  140.3 7.3 %collective-permute-start.18 = (bf16[64,1024]{1,0:T(8,128)(2,1)S(1)}, bf16[64,1024]{1,0:T(8,128)(2,1)S(1)}, u32[]{:S(2)}, u32[]{:S(2)}) collective-permute-start(bf16[64,1024]{1,0:T(8,128)(2,1)S(1)} %get-tuple-element.132), channel_id=1, source_target_pairs={{0,16},{8,24},{16,0},{24,8},{1,17},{9,25},{17,1},{25,9},{2,18},{10... | collective-permute-start | bytes 393224 | tf_op jit(solution)/shard_map/ppermute | solution.py:23
  148.6 10.1 %collective-permute-start.22 = (bf16[128,1280]{1,0:T(8,128)(2,1)S(1)}, bf16[128,1280]{1,0:T(8,128)(2,1)S(1)}, u32[]{:S(2)}, u32[]{:S(2)}) collective-permute-start(bf16[128,1280]{1,0:T(8,128)(2,1)S(1)} %get-tuple-element.139), channel_id=1, source_target_pairs={{0,8},{8,0},{16,24},{24,16},{1,9},{9,1},{17,25},{25,17},{2,10},{10... | collective-permute-start | bytes 983048 | tf_op jit(solution)/shard_map/ppermute | solution.py:23
  150.2 7.5 %collective-permute-start.21 = (bf16[64,1024]{1,0:T(8,128)(2,1)S(1)}, bf16[64,1024]{1,0:T(8,128)(2,1)S(1)}, u32[]{:S(2)}, u32[]{:S(2)}) collective-permute-start(bf16[64,1024]{1,0:T(8,128)(2,1)S(1)} %fold.12.after), channel_id=1, source_target_pairs={{0,16},{8,24},{16,0},{24,8},{1,17},{9,25},{17,1},{25,9},{2,18},{10... | collective-permute-start | bytes 393224 | tf_op jit(solution)/shard_map/ppermute | solution.py:23
  158.7 9.7 %collective-permute-start.23 = (bf16[128,1024]{1,0:T(8,128)(2,1)S(1)}, bf16[128,1024]{1,0:T(8,128)(2,1)S(1)}, u32[]{:S(2)}, u32[]{:S(2)}) collective-permute-start(bf16[128,1024]{1,0:T(8,128)(2,1)S(1)} %pad_maximum_fusion.1.refs_0_), channel_id=1, source_target_pairs={{0,8},{8,0},{16,24},{24,16},{1,9},{9,1},{17,25},{25,17},{2,10},{10... | collective-permute-start | bytes 786440 | tf_op jit(solution)/shard_map/ppermute | solution.py:23
  161.6 6.8 %collective-permute-start.24 = (bf16[64,1280]{1,0:T(8,128)(2,1)S(1)}, bf16[64,1280]{1,0:T(8,128)(2,1)S(1)}, u32[]{:S(2)}, u32[]{:S(2)}) collective-permute-start(bf16[64,1280]{1,0:T(8,128)(2,1)S(1)} %get-tuple-element.143), channel_id=1, source_target_pairs={{0,16},{8,24},{16,0},{24,8},{1,17},{9,25},{17,1},{25,9},{2,18},{10... | collective-permute-start | bytes 491528 | tf_op jit(solution)/shard_map/ppermute | solution.py:23
  168.7 8.7 %collective-permute-start.25 = (bf16[64,1280]{1,0:T(8,128)(2,1)S(1)}, bf16[64,1280]{1,0:T(8,128)(2,1)S(1)}, u32[]{:S(2)}, u32[]{:S(2)}) collective-permute-start(bf16[64,1280]{1,0:T(8,128)(2,1)S(1)} %fold.15), channel_id=1, source_target_pairs={{0,16},{8,24},{16,0},{24,8},{1,17},{9,25},{17,1},{25,9},{2,18},{10... | collective-permute-start | bytes 491528 | tf_op jit(solution)/shard_map/ppermute | solution.py:23
  177.5 7.1 %collective-permute-start.26 = (bf16[128,1280]{1,0:T(8,128)(2,1)S(1)}, bf16[128,1280]{1,0:T(8,128)(2,1)S(1)}, u32[]{:S(2)}, u32[]{:S(2)}) collective-permute-start(bf16[128,1280]{1,0:T(8,128)(2,1)S(1)} %pad_maximum_fusion.refs_2_), channel_id=1, source_target_pairs={{0,8},{8,0},{16,24},{24,16},{1,9},{9,1},{17,25},{25,17},{2,10},{10... | collective-permute-start | bytes 983048 | tf_op jit(solution)/shard_map/ppermute | solution.py:23
